TPU v7x, 768 devices: a whole 4x8x12 slice. The times are simulated.
768 devices in a mesh: grp: 64 (over y, x, core), mem: 12 (over z).
Axes of the slice: x: 4, y: 8, z: 12, core: 2. Of those that a mesh axis runs over, the one named last changes fastest.
Arguments:
- dyn_state: float32 [2, 58, 256, 384], P(None, None, 'grp', 'mem'), may hold values from -6 to 6
- wind_speed: float32 [58, 256, 384], P(None, 'grp', 'mem'), may hold values from -4 to 4
- mass_weight: float32 [256, 384], P('grp', 'mem'), may hold values from 0.5 to 2
- crm_state: float32 [24576, 58, 128], P(('grp', 'mem')), may hold values from -6 to 6
- batch_map: int32 [24576], P(('grp', 'mem')), may hold values from 0 to 383, as said below
- sub_steps: int32 [24576], P(('grp', 'mem')), may hold values from 1 to 2
- migrate_to: int32 [24576], P(('grp', 'mem')), may hold values from 0 to 24575, as said below
Outputs:
- dyn_next: float32 [2, 58, 256, 384], P(None, None, 'grp', 'mem')
- phys_tend: float32 [2, 58, 24576], P(None, None, ('grp', 'mem'))
- crm_next: float32 [24576, 58, 128], P(('grp', 'mem'))
Inputs may be any that keep to these rules, and one draw needn't show every extreme that they name: `batch_map`: within each aligned block of 384 slots (one group), the entries are a permutation of 0 to 383. `migrate_to`: A permutation of all slots. Every slot goes to a device with the same mem index. Exactly 32 of one device's slots leave its group, at most one of them to any one other device; the rest move within the device.
All inputs are finite; a program needn't handle non-finite values.
Results may differ from a plain program's by a relative error of at most 0.0003.
Values sent between devices are 32-bit elements; how exact they have to be, the bound alone decides.
No kernel may reach another device: no remote copies, remote signals or barrier semaphores. Data moves between devices by JAX's collectives and lax.ppermute only.
A program may use at most 64 MiB of HBM per device.

v0:
```python
import jax
import jax.numpy as jnp
import numpy as np
from jax import lax
from jax.sharding import PartitionSpec as P

NSUB = 2


def sent_together(arrays, axis, split_dim, concat_dim, along):
    columns = [a.reshape(*a.shape[:along], -1) for a in arrays]
    both = jnp.concatenate(columns, axis=along)
    filled, at, finished = (
        lax.all_to_all(both, axis, split_axis=split_dim, concat_axis=concat_dim, tiled=True),
        0,
        [],
    )
    for a, column in zip(arrays, columns):
        slab = filled[..., at : at + column.shape[along]]
        finished.append(slab.reshape(*slab.shape[:along], *a.shape[along:]))
        at += column.shape[along]
    return tuple(finished)


def extended(array, sides, width):
    for axis, dim in sides:
        peers, length = (lax.axis_size(axis), array.shape[dim])
        up = [(i, (i + 1) % peers) for i in range(peers)]
        down = [(j, i) for i, j in up]
        last = lax.slice_in_dim(array, length - width, length, axis=dim)
        first = lax.slice_in_dim(array, 0, width, axis=dim)
        before = lax.ppermute(last, axis, up)
        after = lax.ppermute(first, axis, down)
        array = jnp.concatenate([before, array, after], axis=dim)
    return array


def cut_along(array, dim, peers):
    dims = array.shape
    blocks = array.reshape(*dims[:dim], peers, dims[dim] // peers, *dims[dim + 1 :])
    return jnp.moveaxis(blocks, dim, 0)


def summed_on_arrival(array, axis, dim):
    blocks = cut_along(array, dim, lax.axis_size(axis))
    arrived = lax.all_to_all(blocks, axis, split_axis=0, concat_axis=0, tiled=True)
    return arrived.sum(axis=0)


def derivative_table():
    nodes = np.array([-1.0, -1.0 / np.sqrt(5.0), 1.0 / np.sqrt(5.0), 1.0])
    table = np.zeros((4, 4))
    for target_node in range(4):
        for source_node in range(4):
            if target_node == source_node:
                table[target_node, source_node] = sum(
                    (
                        1.0 / (nodes[source_node] - nodes[other_node])
                        for other_node in range(4)
                        if other_node != source_node
                    )
                )
            else:
                numerator = 1.0
                for other_node in range(4):
                    if other_node != source_node and other_node != target_node:
                        numerator = numerator * (nodes[target_node] - nodes[other_node])
                denominator = 1.0
                for other_node in range(4):
                    if other_node != source_node:
                        denominator = denominator * (nodes[source_node] - nodes[other_node])
                table[target_node, source_node] = numerator / denominator
    return table.astype(np.float32)


def element_derivative(field):
    shape_in = field.shape
    blocks = field.reshape(shape_in[:-1] + (shape_in[-1] // 4, 4))
    table = jnp.asarray(derivative_table())
    result = jnp.einsum("...ej,ij->...ei", blocks, table, precision=lax.Precision.HIGHEST)
    return result.reshape(shape_in)


def assemble_padded(values, axis):
    length = values.shape[axis] - 2
    shape_b = [1] * values.ndim
    shape_b[axis] = length
    position = jnp.arange(length, dtype=jnp.int32)
    opening = (position % 4 == 0).reshape(shape_b)
    closing = (position % 4 == 3).reshape(shape_b)
    center = lax.slice_in_dim(values, 1, length + 1, axis=axis)
    before = lax.slice_in_dim(values, 0, length, axis=axis)
    after = lax.slice_in_dim(values, 2, length + 2, axis=axis)
    return center + jnp.where(opening, before, 0.0) + jnp.where(closing, after, 0.0)


def second_levels(values):
    upper = jnp.concatenate([values[:, 1:], values[:, -1:]], 1)
    lower = jnp.concatenate([values[:, :1], values[:, :-1]], 1)
    return upper + lower - 2.0 * values


def crm_run(state, forcing, steps):
    width = state.shape[-1] // 2
    lanes = jnp.arange(2 * width, dtype=jnp.int32)
    heat_lane = (lanes < width)[None, None, :]
    first_lane = (lanes % width == 0)[None, None, :]
    last_lane = (lanes % width == width - 1)[None, None, :]
    forcing_lanes = jnp.where(heat_lane, forcing[0].T[:, :, None], forcing[1].T[:, :, None])
    condense_sign = jnp.where(heat_lane, 0.5, -1.0)
    current = state
    for substep in range(NSUB):
        other = jnp.roll(current, width, -1)
        gap = jnp.where(heat_lane, other - current, current - other)
        condense = 0.1 * jax.nn.softplus(gap)
        left = jnp.where(first_lane, jnp.roll(current, 1 - width, -1), jnp.roll(current, 1, -1))
        right = jnp.where(last_lane, jnp.roll(current, width - 1, -1), jnp.roll(current, -1, -1))
        columns_term = left + right - 2.0 * current
        updated = (
            current
            + 0.25 * forcing_lanes
            + 0.15 * columns_term
            + 0.1 * second_levels(current)
            + condense_sign * condense
        )
        active = (steps > substep)[:, None, None]
        current = jnp.where(active, updated, current)
    change = current - state
    halves = change.reshape(change.shape[0], change.shape[1], 2, width).mean(-1)
    tendency = halves.transpose(2, 1, 0)
    return (current, tendency)


def relocate(state, side, migrate_to):
    slots = migrate_to.shape[0]
    group_size = lax.axis_size("grp")
    member_size = lax.axis_size("mem")
    dest_group = migrate_to // (member_size * slots)
    dest_slot = migrate_to % slots
    own_group = lax.axis_index("grp")
    staying = dest_group == own_group
    kept_target = jnp.where(staying, dest_slot, slots)
    retained_state = jnp.zeros_like(state).at[kept_target].set(state, mode="drop")
    kept_side = jnp.zeros_like(side).at[kept_target].set(side, mode="drop")
    outgoing = jnp.where(staying, group_size, dest_group)
    sender = (
        jnp.zeros((group_size,), jnp.int32)
        .at[outgoing]
        .set(jnp.arange(slots, dtype=jnp.int32), mode="drop")
    )
    filled_rows = jnp.zeros((group_size,), jnp.float32).at[outgoing].set(1.0, mode="drop")
    marker = filled_rows * (dest_slot[sender].astype(jnp.float32) + 1.0)
    bucket_state = state[sender] * filled_rows[:, None, None]
    holding_bucket_side = jnp.concatenate([side[sender] * filled_rows[:, None], marker[:, None]], 1)
    arrived_state, arrived_side = sent_together((bucket_state, holding_bucket_side), "grp", 0, 0, 1)
    target = arrived_side[:, -1].astype(jnp.int32) - 1
    target = jnp.where(target < 0, slots, target)
    new_state = retained_state.at[target].set(arrived_state, mode="drop")
    new_side = kept_side.at[target].set(arrived_side[:, :-1], mode="drop")
    return (new_state, new_side)


def on_device(dyn_state, wind_speed, mass_weight, crm_state, batch_map, sub_steps, migrate_to):
    levels = dyn_state.shape[1]
    rows_local = dyn_state.shape[2]
    points_local = dyn_state.shape[3]
    slots = crm_state.shape[0]
    advection = -wind_speed[None] * element_derivative(dyn_state)
    stacked = jnp.concatenate(
        [
            (mass_weight[None, None] * advection).reshape(2 * levels, rows_local, points_local),
            mass_weight[None],
        ],
        0,
    )
    padded = extended(stacked, (("grp", 1), ("mem", 2)), 1)
    swept = assemble_padded(assemble_padded(padded, 2), 1)
    numerator = swept[: 2 * levels].reshape(2, levels, rows_local, points_local)
    assembled = numerator / swept[2 * levels]
    dyn_next = dyn_state + 0.2 * assembled
    forcing = (
        assembled.reshape(2, levels, rows_local // 2, 2, points_local // 2, 2)
        .mean((3, 5))
        .reshape(2, levels, slots)
    )
    partition_piece = lax.all_gather(forcing, "mem", axis=2, tiled=True)
    length = partition_piece.shape[2]
    column_picker = (batch_map[None, :] == jnp.arange(length, dtype=jnp.int32)[:, None]).astype(
        jnp.float32
    )
    forcing_position = jnp.einsum(
        "zoy,yd->zod", partition_piece, column_picker, precision=lax.Precision.HIGHEST
    )
    stepped, tendency_slot = crm_run(crm_state, forcing_position, sub_steps)
    crm_next, unused_side = relocate(stepped, jnp.zeros((slots, 0), jnp.float32), migrate_to)
    flat_tendency = tendency_slot.reshape(2 * levels, slots)
    column_picker = (
        batch_map[None, :] == jnp.arange(slots * lax.axis_size("mem"), dtype=jnp.int32)[:, None]
    ).astype(jnp.float32)
    gathered_rows = summed_on_arrival(
        jnp.einsum("cs,ks->ck", column_picker, flat_tendency, precision=lax.Precision.HIGHEST),
        "mem",
        0,
    )
    phys_tend = gathered_rows.reshape(slots, 2, levels).transpose(1, 2, 0)
    return (dyn_next, phys_tend, crm_next)


def solution(mesh):
    placed = (
        P(None, None, "grp", "mem"),
        P(None, "grp", "mem"),
        P("grp", "mem"),
        P(("grp", "mem"), None, None),
        P(("grp", "mem")),
        P(("grp", "mem")),
        P(("grp", "mem")),
    )
    return jax.shard_map(
        on_device,
        mesh=mesh,
        in_specs=placed,
        out_specs=(
            P(None, None, "grp", "mem"),
            P(None, None, ("grp", "mem")),
            P(("grp", "mem"), None, None),
        ),
        check_vma=False,
    )
```

profile of v0, /device:TPU:1, one launch (start us, length us, event | category | flops | bytes accessed | tf_op | source)
XLA Modules:
  0.0 174.6 jit_solution(10951603563965929502)
XLA Ops:
  0.6 1.4 convolution_bitcast_fusion
  2.2 0.8 neg.11
  3.3 0.8 copy.131
  4.9 4.5 %collective-permute-start = (f32[117,1,32]{0,2,1:T(8,128)S(1)}, f32[117,1,32]{0,2,1:T(8,128)S(1)}, u32[]{:S(2)}, u32[]{:S(2)}) collective-permute-start(f32[117,1,32]{0,2,1:T(8,128)S(1)} %get-tuple-element.52), channel_id=1, source_target_pairs={{0,12},{12,24},{24,36},{36,48},{48,60},{60,72},{72,84},{84,96},{96... | collective-permute-start | bytes 44936 | tf_op jit(solution)/shard_map/ppermute | solution.py:32
  9.4 9.8 %collective-permute-start.1 = (f32[117,1,32]{0,2,1:T(8,128)S(1)}, f32[117,1,32]{0,2,1:T(8,128)S(1)}, u32[]{:S(2)}, u32[]{:S(2)}) collective-permute-start(f32[117,1,32]{0,2,1:T(8,128)S(1)} %get-tuple-element.53), channel_id=1, source_target_pairs={{12,0},{24,12},{36,24},{48,36},{60,48},{72,60},{84,72},{96,84},{10... | collective-permute-start | bytes 44936 | tf_op jit(solution)/shard_map/ppermute | solution.py:33
  19.6 1.6 fusion.53
  21.2 1.6 fusion.54
  22.9 1.6 fusion.55
  24.5 1.6 fusion.56
  26.1 1.5 fusion.52
  30.0 1.9 %collective-permute-start.2 = (f32[117,6,1]{0,2,1:T(1,128)S(1)}, f32[117,6,1]{0,2,1:T(1,128)S(1)}, u32[]{:S(2)}, u32[]{:S(2)}) collective-permute-start(f32[117,6,1]{0,2,1:T(1,128)S(1)} %get-tuple-element.54), channel_id=1, source_target_pairs={{0,1},{1,2},{2,3},{3,4},{4,5},{5,6},{6,7},{7,8},{8,9},{9,10},{10,1... | collective-permute-start | bytes 8432 | tf_op jit(solution)/shard_map/ppermute | solution.py:32
  31.9 6.4 %collective-permute-start.3 = (f32[117,6,1]{0,2,1:T(1,128)S(1)}, f32[117,6,1]{0,2,1:T(1,128)S(1)}, u32[]{:S(2)}, u32[]{:S(2)}) collective-permute-start(f32[117,6,1]{0,2,1:T(1,128)S(1)} %get-tuple-element.55), channel_id=1, source_target_pairs={{1,0},{2,1},{3,2},{4,3},{5,4},{6,5},{7,6},{8,7},{9,8},{10,9},{11,1... | collective-permute-start | bytes 8432 | tf_op jit(solution)/shard_map/ppermute | solution.py:33
  39.9 19.9 %all_gather.3 = f32[2,58,384]{1,2,0:T(8,128)S(1)} all-gather(f32[2,58,32]{1,2,0:T(8,128)S(1)} %bitcast.56), channel_id=1, replica_groups=mesh['grp'=64,'mem'=12] {'mem'}, dimensions={2}, use_global_device_ids=true | all-gather | bytes 193024 | tf_op jit(solution)/shard_map/all_gather | solution.py:186
  60.3 4.8 %fusion.2 = f32[32,58,128]{2,0,1:T(8,128)S(1)} fusion(f32[32,58,128]{2,0,1:T(8,128)S(1)} %copy-done, f32[32,58,63]{2,0,1:T(8,128)} %get-tuple-element.49, f32[32,58,65]{2,0,1:T(8,128)} %get-tuple-element.51, f32[32,58,127]{2,0,1:T(8,128)} %get-tuple-element.45, f32[32,58,1]{2,0,1:T(8,128)} %get-tuple-element.47, f32[32,58,65]{2,0,1:T(8,128)} %get-tuple-element.50, ...), kind=kLoop, calls=%fused_computation.14 | loop fusion | flops 7839744 | bytes 8568224 | tf_op jit(solution)/shard_map/jit(_where)/select_n | solution.py:127
  67.1 2.6 %fusion.41 = (f32[32,58,128]{2,0,1:T(8,128)S(1)}, f32[32,58,128]{2,0,1:T(8,128)S(1)}) fusion(f32[32,58,128]{2,0,1:T(8,128)S(1)} %copy-done, f32[32,58,128]{2,0,1:T(8,128)S(1)} %fusion.2, f32[128]{0:T(128)S(1)} %select_multiply_fusion.1, f32[32,58,64]{2,0,1:T(8,128)S(1)} %get-tuple-element.37, f32[32,58,64]{2,0,1:T(8,128)S(1)} %get-tuple-element.36, ...), kind=kLoop, calls=%fused_computation.111 | loop fusion | flops 8077312 | bytes 10468768 | tf_op jit(solution)/shard_map/sub | solution.py:128
  70.3 2.0 %gather_fusion = f32[64,58,128]{2,1,0:T(8,128)} fusion(f32[32,58,128]{2,1,0:T(8,128)S(1)} %copy.138, s32[1024]{0:T(1024)S(1)} %pad_clamp_fusion), kind=kCustom, calls=%fused_computation | custom fusion | bytes 3801344 | tf_op jit(solution)/shard_map/gather | solution.py:153
  72.3 4.0 %bitcast_multiply_fusion = f32[64,7424]{1,0:T(8,128)} fusion(f32[8,8,58,128]{3,2,1,0:T(8,128)} %bitcast.49, f32[64]{0:T(128)S(1)} %scatter_custom_fusion.2), kind=kLoop, calls=%fused_computation.10 | loop fusion | flops 475136 | bytes 3801344 | tf_op jit(solution)/shard_map/mul | solution.py:153
  76.3 2.3 %reshape.128 = f32[32,58,2,64]{3,2,0,1:T(2,128)} reshape(f32[32,58,128]{2,0,1:T(8,128)S(1)} %get-tuple-element.22) | data formatting | bytes 1900544 | tf_op jit(solution)/shard_map/reshape | solution.py:129
  78.7 3.6 %reduce_sum.28 = f32[32,58,2]{2,0,1:T(8,128)S(1)} reduce(f32[32,58,2,64]{3,2,0,1:T(2,128)} %reshape.128, f32[]{:T(128)} %constant.102.clone.1), dimensions={3}, to_apply=%region_1.2 | reduce | flops 233856 | bytes 965124 | tf_op jit(solution)/shard_map/reduce_sum | solution.py:129
  83.1 1.0 fusion.20
  84.1 3.8 %all-to-all-start = ((f32[12,32,116]{2,1,0:T(8,128)}), f32[12,32,116]{2,1,0:T(8,128)S(1)}, u32[]{:S(2)}, u32[]{:S(2)}) async-start(f32[12,32,116]{2,1,0:T(8,128)} %fusion.20), calls=%async_computation | async-start | bytes 393216 | tf_op jit(solution)/shard_map/all_to_all | solution.py:46
  87.9 1.6 maximum_bitcast_fusion
  89.5 3.2 %copy.141 = f32[64,1,7425]{2,1,0:T(1,128)} copy(f32[64,1,7425]{2,0,1:T(8,128)S(1)} %maximum_bitcast_fusion) | data formatting | bytes 3801600 | tf_op jit(solution)/shard_map/all_to_all | solution.py:14
  92.8 6.0 %all-to-all-done = f32[12,32,116]{2,1,0:T(8,128)S(1)} async-done(((f32[12,32,116]{2,1,0:T(8,128)}), f32[12,32,116]{2,1,0:T(8,128)S(1)}, u32[]{:S(2)}, u32[]{:S(2)}) %all-to-all-start) | async-done | bytes 178208 | tf_op jit(solution)/shard_map/all_to_all | solution.py:46
  98.8 20.6 %all-to-all-start.1 = ((f32[64,1,7425]{2,1,0:T(1,128)}), f32[64,1,7425]{2,1,0:T(1,128)}, u32[]{:S(2)}, u32[]{:S(2)}) async-start(f32[64,1,7425]{2,1,0:T(1,128)} %copy.141), calls=%async_computation.1 | async-start | bytes 3866624 | tf_op jit(solution)/shard_map/all_to_all | solution.py:14
  120.6 1.6 scatter_fusion
  123.0 42.7 %all-to-all-done.1 = f32[64,1,7425]{2,1,0:T(1,128)} async-done(((f32[64,1,7425]{2,1,0:T(1,128)}), f32[64,1,7425]{2,1,0:T(1,128)}, u32[]{:S(2)}, u32[]{:S(2)}) %all-to-all-start.1) | async-done | bytes 1900832 | tf_op jit(solution)/shard_map/all_to_all | solution.py:14
  165.7 1.7 copy.155
  167.3 1.4 slice.212
  168.8 1.6 reshape.176
  170.5 2.7 %scatter_fusion.1 = f32[32,58,128]{2,1,0:T(8,128)S(1)} fusion(f32[32,58,128]{2,1,0:T(8,128)S(1)} %scatter_fusion, s32[64]{0:T(128)S(1)} %fusion.33, f32[64,58,128]{2,1,0:T(8,128)S(1)} %reshape.176), kind=kCustom, calls=%fused_computation.5 | custom fusion | bytes 5701888 | tf_op jit(solution)/shard_map/scatter | solution.py:158
  173.1 1.5 copy.144
  (72 shorter events, 11.2 us)
Async XLA Ops:
  0.6 18.7 %copy-start = (f32[32,58,128]{2,0,1:T(8,128)S(1)}, f32[32,58,128]{2,0,1:T(8,128)}, u32[]{:S(2)}) copy-start(f32[32,58,128]{2,0,1:T(8,128)} %param.11) | copy-start | bytes 2850820
  4.9 25.0 %collective-permute-start = (f32[117,1,32]{0,2,1:T(8,128)S(1)}, f32[117,1,32]{0,2,1:T(8,128)S(1)}, u32[]{:S(2)}, u32[]{:S(2)}) collective-permute-start(f32[117,1,32]{0,2,1:T(8,128)S(1)} %get-tuple-element.52), channel_id=1, source_target_pairs={{0,12},{12,24},{24,36},{36,48},{48,60},{60,72},{72,84},{84,96},{96... | collective-permute-start | bytes 44936 | tf_op jit(solution)/shard_map/ppermute | solution.py:32
  9.4 20.5 %collective-permute-start.1 = (f32[117,1,32]{0,2,1:T(8,128)S(1)}, f32[117,1,32]{0,2,1:T(8,128)S(1)}, u32[]{:S(2)}, u32[]{:S(2)}) collective-permute-start(f32[117,1,32]{0,2,1:T(8,128)S(1)} %get-tuple-element.53), channel_id=1, source_target_pairs={{12,0},{24,12},{36,24},{48,36},{60,48},{72,60},{84,72},{96,84},{10... | collective-permute-start | bytes 44936 | tf_op jit(solution)/shard_map/ppermute | solution.py:33
  26.1 1.5 copy-start.4
  26.1 1.6 copy-start.3
  27.6 32.2 %copy-start.2 = (s32[32]{0:T(128)S(1)}, s32[32]{0:T(128)}, u32[]{:S(2)}) copy-start(s32[32]{0:T(128)} %param.12) | copy-start | bytes 388
  30.0 8.4 %collective-permute-start.2 = (f32[117,6,1]{0,2,1:T(1,128)S(1)}, f32[117,6,1]{0,2,1:T(1,128)S(1)}, u32[]{:S(2)}, u32[]{:S(2)}) collective-permute-start(f32[117,6,1]{0,2,1:T(1,128)S(1)} %get-tuple-element.54), channel_id=1, source_target_pairs={{0,1},{1,2},{2,3},{3,4},{4,5},{5,6},{6,7},{7,8},{8,9},{9,10},{10,1... | collective-permute-start | bytes 8432 | tf_op jit(solution)/shard_map/ppermute | solution.py:32
  31.9 7.1 %collective-permute-start.3 = (f32[117,6,1]{0,2,1:T(1,128)S(1)}, f32[117,6,1]{0,2,1:T(1,128)S(1)}, u32[]{:S(2)}, u32[]{:S(2)}) collective-permute-start(f32[117,6,1]{0,2,1:T(1,128)S(1)} %get-tuple-element.55), channel_id=1, source_target_pairs={{1,0},{2,1},{3,2},{4,3},{5,4},{6,5},{7,6},{8,7},{9,8},{10,9},{11,1... | collective-permute-start | bytes 8432 | tf_op jit(solution)/shard_map/ppermute | solution.py:33
  84.1 14.7 %all-to-all-start = ((f32[12,32,116]{2,1,0:T(8,128)}), f32[12,32,116]{2,1,0:T(8,128)S(1)}, u32[]{:S(2)}, u32[]{:S(2)}) async-start(f32[12,32,116]{2,1,0:T(8,128)} %fusion.20), calls=%async_computation | async-start | bytes 393216 | tf_op jit(solution)/shard_map/all_to_all | solution.py:46
  92.8 26.8 %copy-start.1 = (f32[2,58,4,32]{1,3,2,0:T(8,128)S(1)}, f32[2,58,4,32]{1,3,2,0:T(8,128)}, u32[]{:S(2)}) copy-start(f32[2,58,4,32]{1,3,2,0:T(8,128)} %param.8) | copy-start | bytes 178180
  98.8 66.9 %all-to-all-start.1 = ((f32[64,1,7425]{2,1,0:T(1,128)}), f32[64,1,7425]{2,1,0:T(1,128)}, u32[]{:S(2)}, u32[]{:S(2)}) async-start(f32[64,1,7425]{2,1,0:T(1,128)} %copy.141), calls=%async_computation.1 | async-start | bytes 3866624 | tf_op jit(solution)/shard_map/all_to_all | solution.py:14
where the time goes:
time: 176 us; the launch traced here: 175 us
  waiting for transfers between devices  49.3 us (28%)
  starting transfers between devices  47 us (27%)
  local copies, waits for them, and re-layouts  35.2 us (20%)
  blocking collectives  19.9 us (11%)
  other arithmetic  19.5 us (11%)
  matrix products  2.61 us (1%)
    all_to_all x1, waiting for transfers between devices, sent_together(): lax.all_to_all(both, axis, split_axis=split_dim, concat_axis=concat_dim,...  42.7 us
    all_to_all x1, starting transfers between devices, sent_together(): lax.all_to_all(both, axis, split_axis=split_dim, concat_axis=concat_dim,...  20.6 us
    all_gather x1, blocking collectives, on_device(): partition_piece = lax.all_gather(forcing, 'mem', axis=2, tiled=True)  19.9 us
    ppermute x2, starting transfers between devices, extended(): after = lax.ppermute(first, axis, down)  16.2 us
    ppermute x2, starting transfers between devices, extended(): before = lax.ppermute(last, axis, up)  6.42 us
    all_to_all x1, waiting for transfers between devices, summed_on_arrival(): lax.all_to_all(blocks, axis, split_axis=0, concat_axis=0, tiled=True)  6.05 us
    select_n x1, other arithmetic, crm_run(): current = jnp.where(active, updated, current)  4.84 us
    unnamed x14, local copies, waits for them, and re-layouts  4.45 us
  transfers between devices with their start and end apart: 6, of which 3 were waited for; matrix products, arithmetic and copies ran while one was open for 11% of the time, Pallas kernels for 0%

commit v1 on v0

v1 whole, which is shorter than its diff:
```python
import jax
import jax.numpy as jnp
import numpy as np
from jax import lax
from jax.experimental import pallas as pl
from jax.experimental.pallas import tpu as pltpu
from jax.sharding import PartitionSpec as P

NSUB = 2
LEV = 58
HALF = 64
SLOTS = 32
N_GRP = 64
N_MEM = 12
ROWS = 4
POINTS = 32
COLS = SLOTS * N_MEM
HIGH = lax.Precision.HIGHEST
VMEM = pl.BlockSpec(memory_space=pltpu.VMEM)
SMEM = pl.BlockSpec(memory_space=pltpu.SMEM)
F32 = jnp.float32


def derivative_table():
    nodes = np.array([-1.0, -1.0 / np.sqrt(5.0), 1.0 / np.sqrt(5.0), 1.0])
    table = np.zeros((4, 4))
    for i in range(4):
        for j in range(4):
            if i == j:
                table[i, j] = sum(1.0 / (nodes[j] - nodes[k]) for k in range(4) if k != j)
            else:
                top = np.prod([nodes[i] - nodes[k] for k in range(4) if k not in (i, j)])
                low = np.prod([nodes[j] - nodes[k] for k in range(4) if k != j])
                table[i, j] = top / low
    return table.astype(np.float32)


def iota(shape, dim):
    return lax.broadcasted_iota(jnp.int32, shape, dim)


def dot(a, b):
    return jnp.dot(a, b, precision=HIGH, preferred_element_type=F32)


def dot_t(a, b):
    return lax.dot_general(a, b, (((0,), (0,)), ((), ())), precision=HIGH, preferred_element_type=F32)


def to_column(row):
    n = row.shape[1]
    return jnp.sum(jnp.where(iota((n, n), 0) == iota((n, n), 1), row, 0.0), axis=1, keepdims=True)


def both_kinds(heat, moist):
    gap = jnp.zeros((heat.shape[0], HALF - LEV), F32)
    return jnp.concatenate([heat, gap, moist, gap], axis=1)


def bucket_kernel(migrate, state, out):
    for s in range(SLOTS):
        group = lax.div(migrate[s], COLS)
        out[pl.ds(group * LEV, LEV), :] = state[pl.ds(s, LEV, stride=SLOTS), :]


def weigh_kernel(dyn, wind, mass, table, out):
    field = both_kinds(dyn[0].reshape(ROWS * POINTS, LEV), dyn[1].reshape(ROWS * POINTS, LEV))
    blow = wind[...].reshape(ROWS * POINTS, LEV)
    slope = dot(table[...], field)
    column = jnp.concatenate([to_column(mass[y : y + 1, :]) for y in range(ROWS)], axis=0)
    weighed = column * (-both_kinds(blow, blow) * slope)
    lane = iota((ROWS * POINTS, 2 * HALF), 1)
    out[...] = jnp.where(lane == LEV, column, weighed).reshape(ROWS, POINTS, 2 * HALF)


def assemble_kernel(own, before, after, batch, inner, payload):
    rows = [own[0] + before[0], own[1], own[2], own[3] + after[0]]
    point = iota((POINTS, 2 * HALF), 0)
    means, edges = [], []
    for y, row in enumerate(rows):
        opening = (point % 4 == 0) & (point > 0)
        closing = (point % 4 == 3) & (point < POINTS - 1)
        full = (
            row
            + jnp.where(opening, pltpu.roll(row, 1, 0), 0.0)
            + jnp.where(closing, pltpu.roll(row, POINTS - 1, 0), 0.0)
        )
        ratio = full / full[:, LEV : LEV + 1]
        inner[y] = ratio
        means.append(jnp.where((point == 0) | (point == POINTS - 1), 0.0, ratio))
        edges.append(row)
    col, pt = iota((SLOTS, ROWS * POINTS), 0), iota((SLOTS, ROWS * POINTS), 1)
    inside = (col // 16 == pt // (2 * POINTS)) & (col % 16 == (pt % POINTS) // 2)
    average = jnp.where(inside, 0.25, 0.0).astype(F32)
    forcing = dot(average, jnp.concatenate(means, axis=0))
    left = [row[0:1] for row in edges]
    right = [row[POINTS - 1 : POINTS] for row in edges]
    lane = iota((SLOTS, 2 * HALF), 1)
    forcing = jnp.where(lane == LEV, to_column(batch[...].astype(F32)), forcing)
    payload[...] = jnp.concatenate([forcing] + left + right, axis=0)


def forcing_kernel(gathered, batch, migrate, steps, force, edge):
    rows = []
    for d in range(N_MEM):
        right = gathered[d, SLOTS + ROWS : SLOTS + 2 * ROWS, :]
        left = gathered[(d + 1) % N_MEM, SLOTS : SLOTS + ROWS, :]
        both = right + left
        rows.append(both / both[:, LEV : LEV + 1])
    joined = jnp.concatenate(rows, axis=0)
    edge[...] = joined
    columns = gathered[:, :SLOTS, :].reshape(COLS, 2 * HALF)
    slot = batch[...]
    pick = jnp.where(iota((COLS, SLOTS), 0) == slot, 1.0, 0.0).astype(F32)
    e = iota((N_MEM * ROWS, SLOTS), 0)
    dev, half = e // ROWS, (e % ROWS) // 2
    ahead = jnp.where(dev == N_MEM - 1, 0, dev + 1)
    last = slot == dev * SLOTS + half * 16 + 15
    first = slot == ahead * SLOTS + half * 16
    pick_edge = jnp.where(last, 0.25, 0.0) + jnp.where(first, 0.25, 0.0)
    forced = dot_t(pick, columns) + dot_t(pick_edge, joined)
    place = to_column(migrate[...].astype(F32))
    count = to_column(steps[...].astype(F32))
    lane = iota((SLOTS, 2 * HALF), 1)
    force[...] = jnp.where(lane == LEV, place, jnp.where(lane == LEV + 1, count, forced))


def substep(source, level, quarter, active):
    shape = (SLOTS, 2 * HALF)
    lane = iota(shape, 1)
    at = lambda l: source[pl.ds(pl.multiple_of(l * SLOTS, SLOTS), SLOTS), :]
    current = at(level)
    upper = at(jnp.minimum(level + 1, LEV - 1))
    lower = at(jnp.maximum(level - 1, 0))
    heat = lane < HALF
    other = pltpu.roll(current, HALF, 1)
    gap = jnp.where(heat, other - current, current - other)
    soft = jnp.maximum(gap, 0.0) + jnp.log(1.0 + jnp.exp(-jnp.abs(gap)))
    column = lane & (HALF - 1)
    left = pltpu.roll(jnp.where(column == HALF - 1, other, current), 1, 1)
    right = pltpu.roll(jnp.where(column == 0, other, current), 2 * HALF - 1, 1)
    force = jnp.take_along_axis(quarter, (lane & HALF) + level, axis=1, mode="promise_in_bounds")
    updated = (
        current
        + force
        + 0.15 * (left + right - 2.0 * current)
        + 0.1 * (upper + lower - 2.0 * current)
        + jnp.where(heat, 0.05, -0.1) * soft
    )
    return jnp.where(active, updated, current)


def tendency_kernel(state, force, send, middle):
    shape = (SLOTS, 2 * HALF)
    count = force[:, LEV + 1 : LEV + 2]
    quarter = 0.25 * force[...]

    def first(level, carry):
        at = pl.ds(pl.multiple_of(level * SLOTS, SLOTS), SLOTS)
        middle[at, :] = substep(state, level, quarter, count > 0.5)
        return carry

    lax.fori_loop(0, LEV, first, 0, unroll=2)
    lane = iota(shape, 1)
    heat = lane < HALF

    def second(level, total):
        at = pl.ds(pl.multiple_of(level * SLOTS, SLOTS), SLOTS)
        change = substep(middle, level, quarter, count > 1.5) - state[at, :]
        h = jnp.sum(jnp.where(heat, change, 0.0), axis=1, keepdims=True)
        q = jnp.sum(jnp.where(heat, 0.0, change), axis=1, keepdims=True)
        mean = jnp.where(heat, h, q) * (1.0 / HALF)
        return jnp.where((lane & (HALF - 1)) == level, mean, total)

    send[...] = lax.fori_loop(0, LEV, second, jnp.zeros(shape, F32), unroll=2)


def select_kernel(every, force, origin):
    me = lax.axis_index("grp") * COLS + lax.axis_index("mem") * SLOTS
    place = every[:, LEV : LEV + 1] - me.astype(F32)
    slot = iota((N_GRP * SLOTS, SLOTS), 1).astype(F32)
    pick = jnp.where(place == slot, 1.0, 0.0).astype(F32)
    force[...] = dot_t(pick, every[...])
    group = (iota((N_GRP * SLOTS, SLOTS), 0) // SLOTS).astype(F32)
    origin[...] = jnp.sum(pick * group, axis=0, keepdims=True).astype(jnp.int32)


def arrive_kernel(source, main, force, out, held, middle):
    for j in range(SLOTS):
        held[pl.ds(j, LEV, stride=SLOTS), :] = main[pl.ds(source[0, j] * LEV, LEV), :]
    count = force[:, LEV + 1 : LEV + 2]
    quarter = 0.25 * force[...]

    def first(level, carry):
        at = pl.ds(pl.multiple_of(level * SLOTS, SLOTS), SLOTS)
        middle[at, :] = substep(held, level, quarter, count > 0.5)
        return carry

    lax.fori_loop(0, LEV, first, 0, unroll=2)

    def second(level, carry):
        at = pl.ds(pl.multiple_of(level * SLOTS, SLOTS), SLOTS)
        out[at, :] = substep(middle, level, quarter, count > 1.5)
        return carry

    lax.fori_loop(0, LEV, second, 0, unroll=2)


def next_kernel(dyn, inner, edge, out):
    me = lax.axis_index("mem")
    behind = lax.rem(me + N_MEM - 1, N_MEM)
    for y in range(ROWS):
        point = iota((POINTS, 2 * HALF), 0)
        left = edge[pl.ds(behind * ROWS + y, 1), :]
        right = edge[pl.ds(me * ROWS + y, 1), :]
        ratio = jnp.where(point == 0, left, jnp.where(point == POINTS - 1, right, inner[y]))
        out[0, y] = dyn[0, y] + 0.2 * ratio[:, :LEV]
        out[1, y] = dyn[1, y] + 0.2 * ratio[:, HALF : HALF + LEV]


def column_kernel(tendency, gathered, out):
    serves = gathered[:, :SLOTS, :].reshape(COLS, 2 * HALF)[:, LEV : LEV + 1]
    column = (iota((COLS, SLOTS), 1) + lax.axis_index("mem") * SLOTS).astype(F32)
    pick = jnp.where(serves == column, 1.0, 0.0).astype(F32)
    mine = dot_t(pick, tendency[...])
    out[0] = mine[:, :LEV]
    out[1] = mine[:, HALF : HALF + LEV]


def call(kernel, shapes, specs, scratch=()):
    many = isinstance(shapes, list)
    out = [jax.ShapeDtypeStruct(s, F32) for s in shapes] if many else jax.ShapeDtypeStruct(shapes, F32)
    return pl.pallas_call(
        kernel,
        out_shape=out,
        in_specs=specs,
        out_specs=[VMEM] * len(shapes) if many else VMEM,
        scratch_shapes=[pltpu.VMEM(s, F32) for s in scratch],
        compiler_params=pltpu.CompilerParams(vmem_limit_bytes=24 * 2**20),
    )


def on_device(dyn_state, wind_speed, mass_weight, crm_state, batch_map, sub_steps, migrate_to):
    lanes = 2 * HALF
    dyn = dyn_state.transpose(0, 2, 3, 1)
    wind = wind_speed.transpose(1, 2, 0)
    state = crm_state.transpose(1, 0, 2).reshape(LEV * SLOTS, lanes)
    batch, steps, moves = (a.reshape(1, SLOTS) for a in (batch_map, sub_steps, migrate_to))
    table = jnp.asarray(np.kron(np.eye(ROWS * POINTS // 4), derivative_table()).astype(np.float32))

    buckets = call(bucket_kernel, (N_GRP * LEV, lanes), [SMEM, VMEM])(migrate_to, state)
    main = lax.all_to_all(buckets.reshape(N_GRP, LEV // 2, 2, lanes), "grp", 0, 0, tiled=True)

    weighed = call(weigh_kernel, (ROWS, POINTS, lanes), [VMEM] * 4)(dyn, wind, mass_weight, table)
    up = [(i, (i + 1) % N_GRP) for i in range(N_GRP)]
    down = [(j, i) for i, j in up]
    before = lax.ppermute(weighed[ROWS - 1 :], "grp", up)
    after = lax.ppermute(weighed[:1], "grp", down)
    inner, payload = call(
        assemble_kernel, [(ROWS, POINTS, lanes), (SLOTS + 2 * ROWS, lanes)], [VMEM] * 4
    )(weighed, before, after, batch)
    gathered = lax.all_gather(payload, "mem", axis=0)
    force, edge = call(
        forcing_kernel, [(SLOTS, lanes), (N_MEM * ROWS, lanes)], [VMEM] * 4
    )(gathered, batch, moves, steps)
    every = lax.all_gather(force, "grp", axis=0, tiled=True)
    cells = LEV * SLOTS
    tendency = call(tendency_kernel, (SLOTS, lanes), [VMEM] * 2, [(cells, lanes)])(state, force)
    tendencies = lax.all_gather(tendency, "mem", axis=0, tiled=True)
    dyn_next = call(next_kernel, (2, ROWS, POINTS, LEV), [VMEM] * 3)(dyn, inner, edge)
    phys = call(column_kernel, (2, SLOTS, LEV), [VMEM] * 2)(tendencies, gathered)

    brought, origin = pl.pallas_call(
        select_kernel,
        out_shape=[jax.ShapeDtypeStruct((SLOTS, lanes), F32), jax.ShapeDtypeStruct((1, SLOTS), jnp.int32)],
        in_specs=[VMEM],
        out_specs=[VMEM] * 2,
        compiler_params=pltpu.CompilerParams(vmem_limit_bytes=24 * 2**20),
    )(every)
    new = call(arrive_kernel, (cells, lanes), [SMEM, VMEM, VMEM], [(cells, lanes)] * 2)(
        origin, main.reshape(N_GRP * LEV, lanes), brought
    )
    crm_next = new.reshape(LEV, SLOTS, lanes).transpose(1, 0, 2)
    return (dyn_next.transpose(0, 3, 1, 2), phys.transpose(0, 2, 1), crm_next)


def solution(mesh):
    placed = (
        P(None, None, "grp", "mem"),
        P(None, "grp", "mem"),
        P("grp", "mem"),
        P(("grp", "mem"), None, None),
        P(("grp", "mem")),
        P(("grp", "mem")),
        P(("grp", "mem")),
    )
    return jax.shard_map(
        on_device,
        mesh=mesh,
        in_specs=placed,
        out_specs=(
            P(None, None, "grp", "mem"),
            P(None, None, ("grp", "mem")),
            P(("grp", "mem"), None, None),
        ),
        check_vma=False,
    )
```

time: 176 us -> 203 us (1.15)
  waiting for transfers between devices: 49.3 us -> 90.6 us
  local copies, waits for them, and re-layouts: 35.2 us -> 4.38 us
  Pallas kernels: 0 us -> 30.5 us
  starting transfers between devices: 47 us -> 20.4 us
  blocking collectives: 19.9 us -> 42.6 us
  other arithmetic: 19.5 us -> 0 us
  between operations: 1.1 us -> 14.2 us
  matrix products: 2.61 us -> 0 us
    all_gather x0 -> x1, waiting for transfers between devices: none -> 86.2 us  [on_device(): every = lax.all_gather(force, 'grp', axis=0, tiled=True)]
    all_to_all x2 -> x1, waiting for transfers between devices: 48.7 us -> 0.01 us  [on_device(): lax.all_to_all(buckets.reshape(N_GRP, LEV // 2, 2, lanes), 'grp', 0, 0, t...]
    pallas_call x0 -> x9, Pallas kernels: none -> 30.5 us  [the longest x1 12.8 us: on_device(): call(tendency_kernel, (SLOTS, lanes), [VMEM] * 2, [(cells, lanes)])]
    all_gather x1 -> x2, blocking collectives: 19.9 us -> 42.6 us  [the longest x1 26.6 us: on_device(): gathered = lax.all_gather(payload, 'mem', axis=0)]
    ppermute x4 -> x2, starting transfers between devices: 22.6 us -> 5.56 us  [the longest x1 3.09 us: on_device(): before = lax.ppermute(weighed[ROWS - 1:], 'grp', up)]
    slice x17 -> x1, local copies, waits for them, and re-layouts: 11.8 us -> 0.01 us  [on_device(): after = lax.ppermute(weighed[:1], 'grp', down)]
    all_to_all x2 -> x1, starting transfers between devices: 24.4 us -> 14.8 us  [on_device(): lax.all_to_all(buckets.reshape(N_GRP, LEV // 2, 2, lanes), 'grp', 0, 0, t...]
    scatter x4 -> x0, local copies, waits for them, and re-layouts: 5.64 us -> none  [the longest x1 2.67 us: relocate(): new_state = retained_state.at[target].set(arrived_state, mode='drop')]
  transfers between devices with their start and end apart: 6 -> 4, of which waited for: 3 -> 3; matrix products, arithmetic and copies ran while one was open for 11% -> 0% of each run, Pallas kernels for 0% -> 8%
where the time goes in v1:
time: 203 us
  waiting for transfers between devices  90.6 us (45%)
  blocking collectives  42.6 us (21%)
  Pallas kernels  30.5 us (15%)
  starting transfers between devices  20.4 us (10%)
  between operations  14.2 us (7%)
  local copies, waits for them, and re-layouts  4.38 us (2%)
    all_gather x1, waiting for transfers between devices, on_device(): every = lax.all_gather(force, 'grp', axis=0, tiled=True)  86.2 us
    all_gather x1, blocking collectives, on_device(): gathered = lax.all_gather(payload, 'mem', axis=0)  26.6 us
    all_gather x1, blocking collectives, on_device(): tendencies = lax.all_gather(tendency, 'mem', axis=0, tiled=True)  16 us
    all_to_all x1, starting transfers between devices, on_device(): lax.all_to_all(buckets.reshape(N_GRP, LEV // 2, 2, lanes), 'grp', 0, 0, t...  14.8 us
    pallas_call x1, Pallas kernels, on_device(): call(tendency_kernel, (SLOTS, lanes), [VMEM] * 2, [(cells, lanes)])  12.8 us
    pallas_call x1, Pallas kernels, on_device(): call(arrive_kernel, (cells, lanes), [SMEM, VMEM, VMEM], [(cells, lanes)]...  12.1 us
    unnamed x24, local copies, waits for them, and re-layouts  4.37 us
  transfers between devices with their start and end apart: 4, of which 3 were waited for; matrix products, arithmetic and copies ran while one was open for 0% of the time, Pallas kernels for 8%

profile of v1, /device:TPU:1, one launch (start us, length us, event | category | flops | bytes accessed | tf_op | source)
XLA Modules:
  0.0 202.7 jit_solution(8435034866709138649)
XLA Ops:
  7.2 0.0 copy-start.1
  7.2 1.2 copy-done.1
  8.4 0.7 copy-done.9
  9.0 1.1 shard_map.110
  10.1 1.3 copy-done
  11.4 0.0 copy-start.8
  11.4 0.0 copy-start.10
  11.4 0.0 copy-start.11
  11.4 0.0 copy-start.2
  11.5 14.8 %all-to-all-start = ((f32[64,29,2,128]{3,2,1,0:T(2,128)}), f32[64,29,2,128]{3,2,1,0:T(2,128)S(1)}, u32[]{:S(2)}, u32[]{:S(2)}) async-start(f32[64,29,2,128]{3,2,1,0:T(2,128)} %bitcast.17), calls=%async_computation | async-start | bytes 3801088 | tf_op jit(solution)/shard_map/all_to_all | solution.py:252
  26.2 0.0 all-gather.3.cloned.1.call-start
  26.3 0.0 copy-done.4
  26.3 0.0 copy-done.5
  26.3 0.0 copy-done.6
  26.3 0.3 shard_map.103.own
  26.7 2.5 %collective-permute-start.1 = (f32[1,32,128]{2,1,0:T(8,128)S(1)}, f32[1,32,128]{2,1,0:T(8,128)S(1)}, u32[]{:S(2)}, u32[]{:S(2)}) collective-permute-start(f32[1,32,128]{2,1,0:T(8,128)S(1)} %get-tuple-element.15), channel_id=1, source_target_pairs={{12,0},{24,12},{36,24},{48,36},{60,48},{72,60},{84,72},{96,84},{10... | collective-permute-start | bytes 49160 | tf_op jit(solution)/shard_map/ppermute | solution.py:258
  29.1 3.1 %collective-permute-start = (f32[1,32,128]{2,1,0:T(8,128)S(1)}, f32[1,32,128]{2,1,0:T(8,128)S(1)}, u32[]{:S(2)}, u32[]{:S(2)}) collective-permute-start(f32[1,32,128]{2,1,0:T(8,128)S(1)} %get-tuple-element.16), channel_id=1, source_target_pairs={{0,12},{12,24},{24,36},{36,48},{48,60},{60,72},{72,84},{84,96},{96... | collective-permute-start | bytes 49160 | tf_op jit(solution)/shard_map/ppermute | solution.py:257
  32.2 0.8 collective-permute-done.1.after
  33.1 3.6 %collective-permute-done.before = f32[1,32,128]{2,1,0:T(8,128)S(1)} collective-permute-done((f32[1,32,128]{2,1,0:T(8,128)S(1)}, f32[1,32,128]{2,1,0:T(8,128)S(1)}, u32[]{:S(2)}, u32[]{:S(2)}) %collective-permute-start) | collective-permute-done | bytes 16416 | tf_op jit(solution)/shard_map/ppermute | solution.py:257
  36.7 0.2 shard_map.104
  36.9 26.6 %all-gather = f32[480,128]{1,0:T(8,128)S(1)} all-gather(f32[40,128]{1,0:T(8,128)S(1)} %get-tuple-element.10), channel_id=2, replica_groups=mesh['grp'=64,'mem'=12] {'mem'}, dimensions={0}, use_global_device_ids=true | all-gather | bytes 266240 | tf_op jit(solution)/shard_map/all_gather | solution.py:262
  63.5 1.0 shard_map.105
  64.4 0.0 all-gather.3.cloned.1.call-update
  64.5 12.8 %shard_map.107 = f32[32,128]{1,0:T(8,128)S(1)} custom-call(f32[1856,128]{1,0:T(8,128)S(1)} %bitcast.19, f32[32,128]{1,0:T(8,128)} %get-tuple-element.12.force), custom_call_target="tpu_custom_call" | custom-call | tf_op jit(solution)/shard_map/pallas_call | solution.py:268
  77.3 16.0 %all_gather.14.tendency = f32[384,128]{1,0:T(8,128)S(1)} all-gather(f32[32,128]{1,0:T(8,128)S(1)} %shard_map.107), channel_id=1, replica_groups=mesh['grp'=64,'mem'=12] {'mem'}, dimensions={0}, use_global_device_ids=true | all-gather | bytes 212992 | tf_op jit(solution)/shard_map/all_gather | solution.py:269
  93.4 1.0 shard_map.108
  94.4 0.8 shard_map.106
  95.2 86.2 %all-gather.3.cloned.1.call-done.every = f32[2048,128]{1,0:T(8,128)} async-done(((f32[32,128]{1,0:T(8,128)}), f32[2048,128]{1,0:T(8,128)}) %all-gather.3.cloned.1.call-update) | async-done | bytes 1048592 | tf_op jit(solution)/shard_map/all_gather | solution.py:266
  181.4 1.2 copy-done.3
  182.6 1.1 shard_map.109
  183.7 0.0 all-to-all-done
  183.7 12.1 %shard_map.111 = f32[1856,128]{1,0:T(8,128)} custom-call(s32[1,32]{1,0:T(1,128)S(1)} %get-tuple-element.13.source, f32[3712,128]{1,0:T(8,128)S(1)} %bitcast.16, f32[32,128]{1,0:T(8,128)S(1)} %get-tuple-element.14.force), custom_call_target="tpu_custom_call" | custom-call | tf_op jit(solution)/shard_map/pallas_call | solution.py:280
  (13 shorter events, 0.0 us)
Async XLA Ops:
  7.2 1.2 copy-start.1
  8.4 0.7 copy-start.9
  10.1 1.3 copy-start
  11.4 14.9 %copy-start.4 = (f32[2,58,4,32]{1,3,2,0:T(8,128)S(1)}, f32[2,58,4,32]{1,3,2,0:T(8,128)}, u32[]{:S(2)}) copy-start(f32[2,58,4,32]{1,3,2,0:T(8,128)} %param.8) | copy-start | bytes 178180
  11.4 14.9 %copy-start.5 = (f32[58,4,32]{0,2,1:T(8,128)S(1)}, f32[58,4,32]{0,2,1:T(8,128)}, u32[]{:S(2)}) copy-start(f32[58,4,32]{0,2,1:T(8,128)} %param.9) | copy-start | bytes 89092
  11.4 14.9 %copy-start.6 = (f32[128,128]{1,0:T(8,128)S(1)}, f32[128,128]{1,0:T(8,128)}, u32[]{:S(2)}) copy-start(f32[128,128]{1,0:T(8,128)} %constant.2.clone.table) | copy-start | bytes 196612
  11.4 14.9 %copy-start.7 = (f32[4,32]{1,0:T(4,128)S(1)}, f32[4,32]{1,0:T(4,128)}, u32[]{:S(2)}) copy-start(f32[4,32]{1,0:T(4,128)} %mass.1) | copy-start | bytes 1540
  11.4 25.3 %copy-start.8 = (s32[32]{0:T(128)S(1)}, s32[32]{0:T(128)}, u32[]{:S(2)}) copy-start(s32[32]{0:T(128)} %param.12) | copy-start | bytes 388
  11.4 52.1 %copy-start.10 = (s32[32]{0:T(128)S(1)}, s32[32]{0:T(128)}, u32[]{:S(2)}) copy-start(s32[32]{0:T(128)} %migrate.1) | copy-start | bytes 388
  11.4 52.0 %copy-start.11 = (s32[32]{0:T(128)S(1)}, s32[32]{0:T(128)}, u32[]{:S(2)}) copy-start(s32[32]{0:T(128)} %param.13) | copy-start | bytes 388
  11.4 53.0 %copy-start.2 = (f32[32,58,128]{2,0,1:T(8,128)S(1)}, f32[32,58,128]{2,0,1:T(8,128)}, u32[]{:S(2)}) copy-start(f32[32,58,128]{2,0,1:T(8,128)} %param.11) | copy-start | bytes 2850820
  11.5 172.2 %all-to-all-start = ((f32[64,29,2,128]{3,2,1,0:T(2,128)}), f32[64,29,2,128]{3,2,1,0:T(2,128)S(1)}, u32[]{:S(2)}, u32[]{:S(2)}) async-start(f32[64,29,2,128]{3,2,1,0:T(2,128)} %bitcast.17), calls=%async_computation | async-start | bytes 3801088 | tf_op jit(solution)/shard_map/all_to_all | solution.py:252
  26.2 155.1 %all-gather.3.cloned.1.call-start = ((), (), s32[]{:S(2)}) async-start(), calls=%async_computation.1 | async-start | bytes 1064960 | tf_op jit(solution)/shard_map/all_gather | solution.py:266
  26.7 6.4 %collective-permute-start.1 = (f32[1,32,128]{2,1,0:T(8,128)S(1)}, f32[1,32,128]{2,1,0:T(8,128)S(1)}, u32[]{:S(2)}, u32[]{:S(2)}) collective-permute-start(f32[1,32,128]{2,1,0:T(8,128)S(1)} %get-tuple-element.15), channel_id=1, source_target_pairs={{12,0},{24,12},{36,24},{48,36},{60,48},{72,60},{84,72},{96,84},{10... | collective-permute-start | bytes 49160 | tf_op jit(solution)/shard_map/ppermute | solution.py:258
  29.1 7.5 %collective-permute-start = (f32[1,32,128]{2,1,0:T(8,128)S(1)}, f32[1,32,128]{2,1,0:T(8,128)S(1)}, u32[]{:S(2)}, u32[]{:S(2)}) collective-permute-start(f32[1,32,128]{2,1,0:T(8,128)S(1)} %get-tuple-element.16), channel_id=1, source_target_pairs={{0,12},{12,24},{24,36},{36,48},{48,60},{60,72},{72,84},{84,96},{96... | collective-permute-start | bytes 49160 | tf_op jit(solution)/shard_map/ppermute | solution.py:257
  181.3 1.2 copy-start.3
Sparse Core Ops, SparseCore 0:
  64.6 116.7 all-gather.2

commit v2 on v1

--- a/solution.py
+++ b/solution.py
@@ -100,7 +100,7 @@
     payload[...] = jnp.concatenate([forcing] + left + right, axis=0)
 
 
-def forcing_kernel(gathered, batch, migrate, steps, force, edge):
+def forcing_kernel(gathered, batch, migrate, steps, force, edge, send):
     rows = []
     for d in range(N_MEM):
         right = gathered[d, SLOTS + ROWS : SLOTS + 2 * ROWS, :]
@@ -119,91 +119,118 @@
     first = slot == ahead * SLOTS + half * 16
     pick_edge = jnp.where(last, 0.25, 0.0) + jnp.where(first, 0.25, 0.0)
     forced = dot_t(pick, columns) + dot_t(pick_edge, joined)
-    place = to_column(migrate[...].astype(F32))
+    new = migrate[...]
+    place = to_column((new & (SLOTS - 1)).astype(F32)) + 1.0
     count = to_column(steps[...].astype(F32))
     lane = iota((SLOTS, 2 * HALF), 1)
-    force[...] = jnp.where(lane == LEV, place, jnp.where(lane == LEV + 1, count, forced))
-
-
-def substep(source, level, quarter, active):
-    shape = (SLOTS, 2 * HALF)
-    lane = iota(shape, 1)
-    at = lambda l: source[pl.ds(pl.multiple_of(l * SLOTS, SLOTS), SLOTS), :]
-    current = at(level)
-    upper = at(jnp.minimum(level + 1, LEV - 1))
-    lower = at(jnp.maximum(level - 1, 0))
-    heat = lane < HALF
-    other = pltpu.roll(current, HALF, 1)
-    gap = jnp.where(heat, other - current, current - other)
+    forced = jnp.where(lane == LEV, place, jnp.where(lane == LEV + 1, count, forced))
+    force[...] = forced
+    group = jnp.floor((new.astype(F32) + 0.5) * (1.0 / COLS)).astype(jnp.int32)
+    goes = jnp.where(iota((N_GRP, SLOTS), 0) == group, 1.0, 0.0).astype(F32)
+    send[...] = dot(goes, forced)
+
+
+def neighbours_table():
+    lanes = 2 * HALF
+    table = np.zeros((lanes, 2 * lanes))
+    for base in (0, HALF):
+        for c in range(HALF):
+            table[base + (c + 1) % HALF, base + c] += 1.0
+            table[base + (c - 1) % HALF, base + c] += 1.0
+            table[c, lanes + base + c] -= 1.0
+            table[HALF + c, lanes + base + c] += 1.0
+    return np.concatenate([table, table], axis=0).astype(jnp.bfloat16)
+
+
+def means_table():
+    same = np.kron(np.eye(2), np.ones((HALF, HALF))) / HALF
+    return np.concatenate([same, same], axis=0).astype(jnp.bfloat16)
+
+
+def two_parts(value):
+    lead = value.astype(jnp.bfloat16)
+    trail = (value - lead.astype(F32)).astype(jnp.bfloat16)
+    return jnp.concatenate([lead, trail], axis=1)
+
+
+CHUNKS = [(0, 8), (8, 8), (16, 8), (24, 8), (32, 8), (40, 8), (48, 8), (56, 2)]
+
+
+def substep(source, first, count, forced, active, table):
+    rows = count * SLOTS
+    at = lambda l, n: source[l * SLOTS : (l + n) * SLOTS, :]
+    current = at(first, count)
+    if first + count < LEV:
+        upper = at(first + 1, count)
+    else:
+        upper = jnp.concatenate([at(first + 1, count - 1), at(LEV - 1, 1)], axis=0)
+    if first > 0:
+        lower = at(first - 1, count)
+    else:
+        lower = jnp.concatenate([at(0, 1), at(0, count - 1)], axis=0)
+    mixed = jnp.dot(two_parts(current), table, preferred_element_type=F32)
+    side, gap = mixed[:, : 2 * HALF], mixed[:, 2 * HALF :]
     soft = jnp.maximum(gap, 0.0) + jnp.log(1.0 + jnp.exp(-jnp.abs(gap)))
-    column = lane & (HALF - 1)
-    left = pltpu.roll(jnp.where(column == HALF - 1, other, current), 1, 1)
-    right = pltpu.roll(jnp.where(column == 0, other, current), 2 * HALF - 1, 1)
-    force = jnp.take_along_axis(quarter, (lane & HALF) + level, axis=1, mode="promise_in_bounds")
-    updated = (
-        current
-        + force
-        + 0.15 * (left + right - 2.0 * current)
-        + 0.1 * (upper + lower - 2.0 * current)
-        + jnp.where(heat, 0.05, -0.1) * soft
-    )
-    return jnp.where(active, updated, current)
-
-
-def tendency_kernel(state, force, send, middle):
-    shape = (SLOTS, 2 * HALF)
-    count = force[:, LEV + 1 : LEV + 2]
+    sign = jnp.where(iota((rows, 2 * HALF), 1) < HALF, 0.05, -0.1)
+    updated = 0.5 * current + forced + 0.15 * side + 0.1 * (upper + lower) + sign * soft
+    on = jnp.broadcast_to(active, (SLOTS, 2 * HALF))
+    return jnp.where(jnp.concatenate([on] * count, axis=0), updated, current)
+
+
+def spread(quarter, first, count):
+    lane = iota((SLOTS, 2 * HALF), 1)
+    return jnp.concatenate(
+        [
+            jnp.take_along_axis(quarter, (lane & HALF) + level, axis=1, mode="promise_in_bounds")
+            for level in range(first, first + count)
+        ],
+        axis=0,
+    )
+
+
+def run_cloud(state, force, table, middle, keep):
+    steps = force[:, LEV + 1 : LEV + 2]
     quarter = 0.25 * force[...]
-
-    def first(level, carry):
-        at = pl.ds(pl.multiple_of(level * SLOTS, SLOTS), SLOTS)
-        middle[at, :] = substep(state, level, quarter, count > 0.5)
-        return carry
-
-    lax.fori_loop(0, LEV, first, 0, unroll=2)
-    lane = iota(shape, 1)
-    heat = lane < HALF
-
-    def second(level, total):
-        at = pl.ds(pl.multiple_of(level * SLOTS, SLOTS), SLOTS)
-        change = substep(middle, level, quarter, count > 1.5) - state[at, :]
-        h = jnp.sum(jnp.where(heat, change, 0.0), axis=1, keepdims=True)
-        q = jnp.sum(jnp.where(heat, 0.0, change), axis=1, keepdims=True)
-        mean = jnp.where(heat, h, q) * (1.0 / HALF)
-        return jnp.where((lane & (HALF - 1)) == level, mean, total)
-
-    send[...] = lax.fori_loop(0, LEV, second, jnp.zeros(shape, F32), unroll=2)
-
-
-def select_kernel(every, force, origin):
-    me = lax.axis_index("grp") * COLS + lax.axis_index("mem") * SLOTS
-    place = every[:, LEV : LEV + 1] - me.astype(F32)
-    slot = iota((N_GRP * SLOTS, SLOTS), 1).astype(F32)
-    pick = jnp.where(place == slot, 1.0, 0.0).astype(F32)
-    force[...] = dot_t(pick, every[...])
-    group = (iota((N_GRP * SLOTS, SLOTS), 0) // SLOTS).astype(F32)
+    for first, count in CHUNKS:
+        forced = spread(quarter, first, count)
+        rows = pl.ds(first * SLOTS, count * SLOTS)
+        middle[rows, :] = substep(state, first, count, forced, steps > 0.5, table[...])
+    for first, count in CHUNKS:
+        forced = spread(quarter, first, count)
+        keep(first, count, substep(middle, first, count, forced, steps > 1.5, table[...]))
+
+
+def tendency_kernel(state, force, table, means, send, middle):
+    column = iota((SLOTS, 2 * HALF), 1) & (HALF - 1)
+    send[...] = jnp.zeros((SLOTS, 2 * HALF), F32)
+
+    def keep(first, count, stepped):
+        change = stepped - state[first * SLOTS : (first + count) * SLOTS, :]
+        mean = jnp.dot(two_parts(change), means[...], preferred_element_type=F32)
+        total = send[...]
+        for i in range(count):
+            total = jnp.where(column == first + i, mean[i * SLOTS : (i + 1) * SLOTS, :], total)
+        send[...] = total
+
+    run_cloud(state, force, table, middle, keep)
+
+
+def select_kernel(rest, force, origin):
+    slot = (iota((N_GRP, SLOTS), 1) + 1).astype(F32)
+    pick = jnp.where(rest[:, LEV : LEV + 1] == slot, 1.0, 0.0).astype(F32)
+    force[...] = dot_t(pick, rest[...])
+    group = iota((N_GRP, SLOTS), 0).astype(F32)
     origin[...] = jnp.sum(pick * group, axis=0, keepdims=True).astype(jnp.int32)
 
 
-def arrive_kernel(source, main, force, out, held, middle):
+def arrive_kernel(source, main, force, table, out, held, middle):
     for j in range(SLOTS):
         held[pl.ds(j, LEV, stride=SLOTS), :] = main[pl.ds(source[0, j] * LEV, LEV), :]
-    count = force[:, LEV + 1 : LEV + 2]
-    quarter = 0.25 * force[...]
-
-    def first(level, carry):
-        at = pl.ds(pl.multiple_of(level * SLOTS, SLOTS), SLOTS)
-        middle[at, :] = substep(held, level, quarter, count > 0.5)
-        return carry
-
-    lax.fori_loop(0, LEV, first, 0, unroll=2)
-
-    def second(level, carry):
-        at = pl.ds(pl.multiple_of(level * SLOTS, SLOTS), SLOTS)
-        out[at, :] = substep(middle, level, quarter, count > 1.5)
-        return carry
-
-    lax.fori_loop(0, LEV, second, 0, unroll=2)
+
+    def keep(first, count, stepped):
+        out[first * SLOTS : (first + count) * SLOTS, :] = stepped
+
+    run_cloud(held, force, table, middle, keep)
 
 
 def next_kernel(dyn, inner, edge, out):
@@ -248,25 +275,28 @@
     batch, steps, moves = (a.reshape(1, SLOTS) for a in (batch_map, sub_steps, migrate_to))
     table = jnp.asarray(np.kron(np.eye(ROWS * POINTS // 4), derivative_table()).astype(np.float32))
 
-    buckets = call(bucket_kernel, (N_GRP * LEV, lanes), [SMEM, VMEM])(migrate_to, state)
-    main = lax.all_to_all(buckets.reshape(N_GRP, LEV // 2, 2, lanes), "grp", 0, 0, tiled=True)
-
     weighed = call(weigh_kernel, (ROWS, POINTS, lanes), [VMEM] * 4)(dyn, wind, mass_weight, table)
+    weighed, state_later = lax.optimization_barrier((weighed, state))
+    buckets = call(bucket_kernel, (N_GRP * LEV, lanes), [SMEM, VMEM])(migrate_to, state_later)
     up = [(i, (i + 1) % N_GRP) for i in range(N_GRP)]
     down = [(j, i) for i, j in up]
     before = lax.ppermute(weighed[ROWS - 1 :], "grp", up)
     after = lax.ppermute(weighed[:1], "grp", down)
+    buckets, before, after = lax.optimization_barrier((buckets, before, after))
+    main = lax.all_to_all(buckets.reshape(N_GRP, LEV // 2, 2, lanes), "grp", 0, 0, tiled=True)
     inner, payload = call(
         assemble_kernel, [(ROWS, POINTS, lanes), (SLOTS + 2 * ROWS, lanes)], [VMEM] * 4
     )(weighed, before, after, batch)
     gathered = lax.all_gather(payload, "mem", axis=0)
-    force, edge = call(
-        forcing_kernel, [(SLOTS, lanes), (N_MEM * ROWS, lanes)], [VMEM] * 4
+    force, edge, send = call(
+        forcing_kernel, [(SLOTS, lanes), (N_MEM * ROWS, lanes), (N_GRP, lanes)], [VMEM] * 4
     )(gathered, batch, moves, steps)
-    every = lax.all_gather(force, "grp", axis=0, tiled=True)
     cells = LEV * SLOTS
-    tendency = call(tendency_kernel, (SLOTS, lanes), [VMEM] * 2, [(cells, lanes)])(state, force)
+    mix, means = jnp.asarray(neighbours_table()), jnp.asarray(means_table())
+    tendency = call(tendency_kernel, (SLOTS, lanes), [VMEM] * 4, [(cells, lanes)])(state, force, mix, means)
     tendencies = lax.all_gather(tendency, "mem", axis=0, tiled=True)
+    send, main, tendencies = lax.optimization_barrier((send, main, tendencies))
+    rest = lax.all_to_all(send.reshape(N_GRP, 1, lanes), "grp", 0, 0, tiled=True)
     dyn_next = call(next_kernel, (2, ROWS, POINTS, LEV), [VMEM] * 3)(dyn, inner, edge)
     phys = call(column_kernel, (2, SLOTS, LEV), [VMEM] * 2)(tendencies, gathered)
 
@@ -276,9 +306,9 @@
         in_specs=[VMEM],
         out_specs=[VMEM] * 2,
         compiler_params=pltpu.CompilerParams(vmem_limit_bytes=24 * 2**20),
-    )(every)
-    new = call(arrive_kernel, (cells, lanes), [SMEM, VMEM, VMEM], [(cells, lanes)] * 2)(
-        origin, main.reshape(N_GRP * LEV, lanes), brought
+    )(rest.reshape(N_GRP, lanes))
+    new = call(arrive_kernel, (cells, lanes), [SMEM, VMEM, VMEM, VMEM], [(cells, lanes)] * 2)(
+        origin, main.reshape(N_GRP * LEV, lanes), brought, mix
     )
     crm_next = new.reshape(LEV, SLOTS, lanes).transpose(1, 0, 2)
     return (dyn_next.transpose(0, 3, 1, 2), phys.transpose(0, 2, 1), crm_next)

time: 203 us -> 109 us (0.54)
  waiting for transfers between devices: 90.6 us -> 7.5 us
  Pallas kernels: 30.5 us -> 10.4 us
  starting transfers between devices: 20.4 us -> 39 us
  between operations: 14.2 us -> 0.8 us
  local copies, waits for them, and re-layouts: 4.38 us -> 6.41 us
    all_gather x1 -> x0, waiting for transfers between devices: 86.2 us -> none  [on_device(): every = lax.all_gather(force, 'grp', axis=0, tiled=True)]
    pallas_call x4, Pallas kernels: 27 us -> 7.8 us  [the longest x1 3.69 us: on_device(): call(arrive_kernel, (cells, lanes), [SMEM, VMEM, VMEM, VMEM], [(cells, la...]
    all_to_all x0 -> x1, starting transfers between devices: none -> 17.6 us  [on_device(): lax.all_to_all(send.reshape(N_GRP, 1, lanes), 'grp', 0, 0, tiled=True)]
    ppermute x1, starting transfers between devices: 2.48 us -> 12.4 us  [on_device(): after = lax.ppermute(weighed[:1], 'grp', down)]
    all_to_all x1, starting transfers between devices: 14.8 us -> 7.04 us  [on_device(): lax.all_to_all(buckets.reshape(N_GRP, LEV // 2, 2, lanes), 'grp', 0, 0, t...]
    all_to_all x0 -> x1, waiting for transfers between devices: none -> 7.49 us  [on_device(): lax.all_to_all(send.reshape(N_GRP, 1, lanes), 'grp', 0, 0, tiled=True)]
    ppermute x1, waiting for transfers between devices: 3.58 us -> 0.01 us  [on_device(): before = lax.ppermute(weighed[ROWS - 1:], 'grp', up)]
    unnamed x24 -> x28, local copies, waits for them, and re-layouts: 4.37 us -> 6.41 us
  transfers between devices with their start and end apart: 4 -> 4, of which waited for: 3 -> 1; matrix products, arithmetic and copies ran while one was open for 0% -> 0% of each run, Pallas kernels for 8% -> 6%
where the time goes in v2:
time: 109 us; the launch traced here: 108 us
  blocking collectives  44.1 us (40%)
  starting transfers between devices  39 us (36%)
  Pallas kernels  10.4 us (10%)
  waiting for transfers between devices  7.5 us (7%)
  local copies, waits for them, and re-layouts  6.41 us (6%)
    all_gather x1, blocking collectives, on_device(): gathered = lax.all_gather(payload, 'mem', axis=0)  27.1 us
    all_to_all x1, starting transfers between devices, on_device(): lax.all_to_all(send.reshape(N_GRP, 1, lanes), 'grp', 0, 0, tiled=True)  17.6 us
    all_gather x1, blocking collectives, on_device(): tendencies = lax.all_gather(tendency, 'mem', axis=0, tiled=True)  17.1 us
    ppermute x1, starting transfers between devices, on_device(): after = lax.ppermute(weighed[:1], 'grp', down)  12.4 us
    all_to_all x1, waiting for transfers between devices, on_device(): lax.all_to_all(send.reshape(N_GRP, 1, lanes), 'grp', 0, 0, tiled=True)  7.49 us
    all_to_all x1, starting transfers between devices, on_device(): lax.all_to_all(buckets.reshape(N_GRP, LEV // 2, 2, lanes), 'grp', 0, 0, t...  7.04 us
    unnamed x28, local copies, waits for them, and re-layouts  6.41 us
    pallas_call x1, Pallas kernels, on_device(): call(arrive_kernel, (cells, lanes), [SMEM, VMEM, VMEM, VMEM], [(cells, la...  3.69 us
  transfers between devices with their start and end apart: 4, of which 1 were waited for; matrix products, arithmetic and copies ran while one was open for 0% of the time, Pallas kernels for 6%

profile of v2, /device:TPU:1, one launch (start us, length us, event | category | flops | bytes accessed | tf_op | source)
XLA Modules:
  0.0 108.3 jit_solution(5475739512237104941)
XLA Ops:
  0.6 0.0 copy-start.4
  0.6 0.9 copy-done.4
  1.5 0.8 copy-done.6
  2.4 0.8 copy-done.8
  3.2 0.7 copy-done.9
  3.9 0.3 shard_map.121.own
  4.2 12.4 %collective-permute-start.1 = (f32[1,32,128]{2,1,0:T(8,128)S(1)}, f32[1,32,128]{2,1,0:T(8,128)S(1)}, u32[]{:S(2)}, u32[]{:S(2)}) collective-permute-start(f32[1,32,128]{2,1,0:T(8,128)S(1)} %get-tuple-element.33), channel_id=1, source_target_pairs={{12,0},{24,12},{36,24},{48,36},{60,48},{72,60},{84,72},{96,84},{10... | collective-permute-start | bytes 49160 | tf_op jit(solution)/shard_map/ppermute | solution.py:284
  16.6 1.9 %collective-permute-start = (f32[1,32,128]{2,1,0:T(8,128)S(1)}, f32[1,32,128]{2,1,0:T(8,128)S(1)}, u32[]{:S(2)}, u32[]{:S(2)}) collective-permute-start(f32[1,32,128]{2,1,0:T(8,128)S(1)} %get-tuple-element.34), channel_id=1, source_target_pairs={{0,12},{12,24},{24,36},{36,48},{48,60},{60,72},{72,84},{84,96},{96... | collective-permute-start | bytes 49160 | tf_op jit(solution)/shard_map/ppermute | solution.py:283
  18.6 0.0 copy-start.1
  18.6 1.2 %copy-done.1 = f32[32,58,128]{2,0,1:T(8,128)S(1)} copy-done((f32[32,58,128]{2,0,1:T(8,128)S(1)}, f32[32,58,128]{2,0,1:T(8,128)}, u32[]{:S(2)}) %copy-start.1) | copy-done | bytes 950296
  19.8 0.7 copy-done.11
  20.4 1.1 %shard_map.122 = f32[3712,128]{1,0:T(8,128)S(1)} custom-call(s32[32]{0:T(128)S(1)} %copy-done.11, f32[1856,128]{1,0:T(8,128)S(1)} %bitcast.22), custom_call_target="tpu_custom_call" | custom-call | tf_op jit(solution)/shard_map/pallas_call | solution.py:280
  21.5 1.3 %copy-done = f32[3712,128]{1,0:T(8,128)} copy-done((f32[3712,128]{1,0:T(8,128)}, f32[3712,128]{1,0:T(8,128)S(1)}, u32[]{:S(2)}) %copy-start) | copy-done | bytes 1900568
  22.8 0.0 collective-permute-done.1.after
  22.8 0.0 copy-start.12
  22.8 0.0 copy-start.13
  22.8 0.0 copy-start.2
  22.9 0.0 copy-start.3
  22.9 0.0 copy-start.7
  22.9 7.0 %all-to-all-start = ((f32[64,29,2,128]{3,2,1,0:T(2,128)}), f32[64,29,2,128]{3,2,1,0:T(2,128)S(1)}, u32[]{:S(2)}, u32[]{:S(2)}) async-start(f32[64,29,2,128]{3,2,1,0:T(2,128)} %bitcast.21), calls=%async_computation | async-start | bytes 3801088 | tf_op jit(solution)/shard_map/all_to_all | solution.py:286
  29.9 0.0 copy-start.5
  30.0 0.2 shard_map.123
  30.2 27.1 %all-gather = f32[480,128]{1,0:T(8,128)S(1)} all-gather(f32[40,128]{1,0:T(8,128)S(1)} %get-tuple-element.23), channel_id=2, replica_groups=mesh['grp'=64,'mem'=12] {'mem'}, dimensions={0}, use_global_device_ids=true | all-gather | bytes 266240 | tf_op jit(solution)/shard_map/all_gather | solution.py:290
  57.3 1.1 %shard_map.124 = (f32[32,128]{1,0:T(8,128)S(1)}, f32[48,128]{1,0:T(8,128)S(1)}, f32[64,128]{1,0:T(8,128)}) custom-call(f32[12,40,128]{2,1,0:T(8,128)S(1)} %bitcast.24, s32[1,32]{1,0:T(1,128)S(1)} %bitcast.31, s32[1,32]{1,0:T(1,128)S(1)} %bitcast.32, s32[1,32]{1,0:T(1,128)S(1)} %bitcast.33), custom_call_target="tpu_custom_call" | custom-call | tf_op jit(solution)/shard_map/pallas_call | solution.py:291
  58.4 1.9 %shard_map.126 = f32[32,128]{1,0:T(8,128)S(1)} custom-call(f32[1856,128]{1,0:T(8,128)S(1)} %bitcast.23, f32[32,128]{1,0:T(8,128)S(1)} %get-tuple-element.27.force, bf16[256,256]{1,0:T(8,128)(2,1)S(1)} %copy-done.3, bf16[256,128]{1,0:T(8,128)(2,1)S(1)} %copy-done.7), custom_call_target="tpu_custom_call" | custom-call | tf_op jit(solution)/shard_map/pallas_call | solution.py:296
  60.3 17.1 %all_gather.11.tendency = f32[384,128]{1,0:T(8,128)S(1)} all-gather(f32[32,128]{1,0:T(8,128)S(1)} %shard_map.126), channel_id=1, replica_groups=mesh['grp'=64,'mem'=12] {'mem'}, dimensions={0}, use_global_device_ids=true | all-gather | bytes 212992 | tf_op jit(solution)/shard_map/all_gather | solution.py:297
  77.4 17.6 %all-to-all-start.1 = ((f32[64,1,128]{2,1,0:T(1,128)}), f32[64,1,128]{2,1,0:T(1,128)S(1)}, u32[]{:S(2)}, u32[]{:S(2)}) async-start(f32[64,1,128]{2,1,0:T(1,128)} %bitcast.13), calls=%async_computation.1 | async-start | bytes 65536 | tf_op jit(solution)/shard_map/all_to_all | solution.py:299
  95.0 0.8 shard_map.125
  95.8 1.0 shard_map.127
  96.8 7.5 %all-to-all-done.1 = f32[64,1,128]{2,1,0:T(1,128)S(1)} async-done(((f32[64,1,128]{2,1,0:T(1,128)}), f32[64,1,128]{2,1,0:T(1,128)S(1)}, u32[]{:S(2)}, u32[]{:S(2)}) %all-to-all-start.1) | async-done | bytes 32800 | tf_op jit(solution)/shard_map/all_to_all | solution.py:299
  104.3 0.3 shard_map.128
  104.6 3.7 %shard_map.129 = f32[1856,128]{1,0:T(8,128)} custom-call(s32[1,32]{1,0:T(1,128)S(1)} %get-tuple-element.30.source, f32[3712,128]{1,0:T(8,128)S(1)} %bitcast.20, f32[32,128]{1,0:T(8,128)S(1)} %get-tuple-element.32.force, bf16[256,256]{1,0:T(8,128)(2,1)S(1)} %copy-done.3), custom_call_target="tpu_custom_call" | custom-call | tf_op jit(solution)/shard_map/pallas_call | solution.py:310
  (16 shorter events, 0.0 us)
Async XLA Ops:
  0.6 0.9 copy-start.4
  1.5 0.8 copy-start.6
  2.4 0.8 copy-start.8
  3.2 0.7 copy-start.9
  4.2 18.6 %collective-permute-start.1 = (f32[1,32,128]{2,1,0:T(8,128)S(1)}, f32[1,32,128]{2,1,0:T(8,128)S(1)}, u32[]{:S(2)}, u32[]{:S(2)}) collective-permute-start(f32[1,32,128]{2,1,0:T(8,128)S(1)} %get-tuple-element.33), channel_id=1, source_target_pairs={{12,0},{24,12},{36,24},{48,36},{60,48},{72,60},{84,72},{96,84},{10... | collective-permute-start | bytes 49160 | tf_op jit(solution)/shard_map/ppermute | solution.py:284
  16.6 6.2 %collective-permute-start = (f32[1,32,128]{2,1,0:T(8,128)S(1)}, f32[1,32,128]{2,1,0:T(8,128)S(1)}, u32[]{:S(2)}, u32[]{:S(2)}) collective-permute-start(f32[1,32,128]{2,1,0:T(8,128)S(1)} %get-tuple-element.34), channel_id=1, source_target_pairs={{0,12},{12,24},{24,36},{36,48},{48,60},{60,72},{72,84},{84,96},{96... | collective-permute-start | bytes 49160 | tf_op jit(solution)/shard_map/ppermute | solution.py:283
  18.6 1.2 %copy-start.1 = (f32[32,58,128]{2,0,1:T(8,128)S(1)}, f32[32,58,128]{2,0,1:T(8,128)}, u32[]{:S(2)}) copy-start(f32[32,58,128]{2,0,1:T(8,128)} %param.13) | copy-start | bytes 2850820
  19.8 0.7 copy-start.11
  21.5 1.3 %copy-start = (f32[3712,128]{1,0:T(8,128)}, f32[3712,128]{1,0:T(8,128)S(1)}, u32[]{:S(2)}) copy-start(f32[3712,128]{1,0:T(8,128)S(1)} %shard_map.122) | copy-start | bytes 5701636
  22.8 7.1 %copy-start.10 = (s32[32]{0:T(128)S(1)}, s32[32]{0:T(128)}, u32[]{:S(2)}) copy-start(s32[32]{0:T(128)} %param.14) | copy-start | bytes 388
  22.8 34.4 %copy-start.12 = (s32[32]{0:T(128)S(1)}, s32[32]{0:T(128)}, u32[]{:S(2)}) copy-start(s32[32]{0:T(128)} %migrate.1) | copy-start | bytes 388
  22.8 34.4 %copy-start.13 = (s32[32]{0:T(128)S(1)}, s32[32]{0:T(128)}, u32[]{:S(2)}) copy-start(s32[32]{0:T(128)} %param.15) | copy-start | bytes 388
  22.8 35.6 %copy-start.2 = (f32[32,58,128]{2,0,1:T(8,128)S(1)}, f32[32,58,128]{2,0,1:T(8,128)}, u32[]{:S(2)}) copy-start(f32[32,58,128]{2,0,1:T(8,128)} %param.13) | copy-start | bytes 2850820
  22.9 35.6 %copy-start.3 = (bf16[256,256]{1,0:T(8,128)(2,1)S(1)}, bf16[256,256]{1,0:T(8,128)(2,1)}, u32[]{:S(2)}) copy-start(bf16[256,256]{1,0:T(8,128)(2,1)} %constant.7.clone.table) | copy-start | bytes 393220
  22.9 35.6 %copy-start.7 = (bf16[256,128]{1,0:T(8,128)(2,1)S(1)}, bf16[256,128]{1,0:T(8,128)(2,1)}, u32[]{:S(2)}) copy-start(bf16[256,128]{1,0:T(8,128)(2,1)} %constant.8.clone.means) | copy-start | bytes 196612
  22.9 54.5 %all-to-all-start = ((f32[64,29,2,128]{3,2,1,0:T(2,128)}), f32[64,29,2,128]{3,2,1,0:T(2,128)S(1)}, u32[]{:S(2)}, u32[]{:S(2)}) async-start(f32[64,29,2,128]{3,2,1,0:T(2,128)} %bitcast.21), calls=%async_computation | async-start | bytes 3801088 | tf_op jit(solution)/shard_map/all_to_all | solution.py:286
  29.9 65.1 %copy-start.5 = (f32[2,58,4,32]{1,3,2,0:T(8,128)S(1)}, f32[2,58,4,32]{1,3,2,0:T(8,128)}, u32[]{:S(2)}) copy-start(f32[2,58,4,32]{1,3,2,0:T(8,128)} %param.10) | copy-start | bytes 178180
  77.4 26.9 %all-to-all-start.1 = ((f32[64,1,128]{2,1,0:T(1,128)}), f32[64,1,128]{2,1,0:T(1,128)S(1)}, u32[]{:S(2)}, u32[]{:S(2)}) async-start(f32[64,1,128]{2,1,0:T(1,128)} %bitcast.13), calls=%async_computation.1 | async-start | bytes 65536 | tf_op jit(solution)/shard_map/all_to_all | solution.py:299

commit v3 on v2

--- a/solution.py
+++ b/solution.py
@@ -18,6 +18,7 @@
 HIGH = lax.Precision.HIGHEST
 VMEM = pl.BlockSpec(memory_space=pltpu.VMEM)
 SMEM = pl.BlockSpec(memory_space=pltpu.SMEM)
+HBM = pl.BlockSpec(memory_space=pltpu.HBM)
 F32 = jnp.float32
 
 
@@ -57,23 +58,41 @@
     return jnp.concatenate([heat, gap, moist, gap], axis=1)
 
 
-def bucket_kernel(migrate, state, out):
+def bucket_kernel(migrate, state, out, done):
+    copies = []
     for s in range(SLOTS):
         group = lax.div(migrate[s], COLS)
-        out[pl.ds(group * LEV, LEV), :] = state[pl.ds(s, LEV, stride=SLOTS), :]
-
-
-def weigh_kernel(dyn, wind, mass, table, out):
+        copies.append(
+            pltpu.make_async_copy(state.at[:, s], out.at[group, pl.ds(0, LEV)], done.at[s])
+        )
+        copies[-1].start()
+    for copy in copies:
+        copy.wait()
+
+
+def weigh_kernel(dyn_at, wind_at, mass_at, table_at, batch_at, out, top, end, dyn, wind, mass, table, batch, done):
+    pairs = [(dyn_at, dyn), (wind_at, wind), (mass_at, mass), (table_at, table), (batch_at, batch)]
+    copies = [pltpu.make_async_copy(a, b, done.at[i]) for i, (a, b) in enumerate(pairs)]
+    for copy in copies:
+        copy.start()
+    for copy in copies:
+        copy.wait()
     field = both_kinds(dyn[0].reshape(ROWS * POINTS, LEV), dyn[1].reshape(ROWS * POINTS, LEV))
     blow = wind[...].reshape(ROWS * POINTS, LEV)
     slope = dot(table[...], field)
     column = jnp.concatenate([to_column(mass[y : y + 1, :]) for y in range(ROWS)], axis=0)
     weighed = column * (-both_kinds(blow, blow) * slope)
     lane = iota((ROWS * POINTS, 2 * HALF), 1)
-    out[...] = jnp.where(lane == LEV, column, weighed).reshape(ROWS, POINTS, 2 * HALF)
-
-
-def assemble_kernel(own, before, after, batch, inner, payload):
+    serves = jnp.concatenate([to_column(batch[...].astype(F32))] * ROWS, axis=0)
+    spare = jnp.where(lane == LEV, column, serves)
+    weighed = jnp.where((lane == LEV) | (lane == LEV + 1), spare, weighed)
+    weighed = weighed.reshape(ROWS, POINTS, 2 * HALF)
+    out[...] = weighed
+    top[0] = weighed[0]
+    end[0] = weighed[ROWS - 1]
+
+
+def assemble_kernel(own, before, after, inner, payload):
     rows = [own[0] + before[0], own[1], own[2], own[3] + after[0]]
     point = iota((POINTS, 2 * HALF), 0)
     means, edges = [], []
@@ -96,11 +115,13 @@
     left = [row[0:1] for row in edges]
     right = [row[POINTS - 1 : POINTS] for row in edges]
     lane = iota((SLOTS, 2 * HALF), 1)
-    forcing = jnp.where(lane == LEV, to_column(batch[...].astype(F32)), forcing)
-    payload[...] = jnp.concatenate([forcing] + left + right, axis=0)
-
-
-def forcing_kernel(gathered, batch, migrate, steps, force, edge, send):
+    forcing = jnp.where(lane == LEV, own[0][:, LEV + 1 : LEV + 2], forcing)
+    whole = jnp.concatenate([forcing] + left + right, axis=0)
+    for d in range(N_MEM):
+        payload[d] = whole
+
+
+def forcing_kernel(gathered, batch, migrate, steps, buckets, force, edge, filled, row, done):
     rows = []
     for d in range(N_MEM):
         right = gathered[d, SLOTS + ROWS : SLOTS + 2 * ROWS, :]
@@ -127,7 +148,10 @@
     force[...] = forced
     group = jnp.floor((new.astype(F32) + 0.5) * (1.0 / COLS)).astype(jnp.int32)
     goes = jnp.where(iota((N_GRP, SLOTS), 0) == group, 1.0, 0.0).astype(F32)
-    send[...] = dot(goes, forced)
+    row[...] = dot(goes, forced).reshape(N_GRP, 1, 2 * HALF)
+    copy = pltpu.make_async_copy(row, filled.at[:, LEV], done)
+    copy.start()
+    copy.wait()
 
 
 def neighbours_table():
@@ -153,6 +177,7 @@
     return jnp.concatenate([lead, trail], axis=1)
 
 
+SENT = LEV + 1
 CHUNKS = [(0, 8), (8, 8), (16, 8), (24, 8), (32, 8), (40, 8), (48, 8), (56, 2)]
 
 
@@ -215,17 +240,18 @@
     run_cloud(state, force, table, middle, keep)
 
 
-def select_kernel(rest, force, origin):
+def arrive_kernel(main, table, out, held, middle, force, row, origin, done):
+    last = main[pl.ds(LEV, N_GRP, stride=SENT), :]
     slot = (iota((N_GRP, SLOTS), 1) + 1).astype(F32)
-    pick = jnp.where(rest[:, LEV : LEV + 1] == slot, 1.0, 0.0).astype(F32)
-    force[...] = dot_t(pick, rest[...])
+    pick = jnp.where(last[:, LEV : LEV + 1] == slot, 1.0, 0.0).astype(F32)
     group = iota((N_GRP, SLOTS), 0).astype(F32)
-    origin[...] = jnp.sum(pick * group, axis=0, keepdims=True).astype(jnp.int32)
-
-
-def arrive_kernel(source, main, force, table, out, held, middle):
+    row[...] = jnp.sum(pick * group, axis=0, keepdims=True).astype(jnp.int32)
+    copy = pltpu.make_async_copy(row, origin, done)
+    copy.start()
+    force[...] = dot_t(pick, last)
+    copy.wait()
     for j in range(SLOTS):
-        held[pl.ds(j, LEV, stride=SLOTS), :] = main[pl.ds(source[0, j] * LEV, LEV), :]
+        held[pl.ds(j, LEV, stride=SLOTS), :] = main[pl.ds(origin[0, j] * SENT, LEV), :]
 
     def keep(first, count, stepped):
         out[first * SLOTS : (first + count) * SLOTS, :] = stepped
@@ -254,16 +280,17 @@
     out[1] = mine[:, HALF : HALF + LEV]
 
 
-def call(kernel, shapes, specs, scratch=()):
+def call(kernel, shapes, specs, scratch=(), out_specs=None, aliases=None, limit=24):
     many = isinstance(shapes, list)
     out = [jax.ShapeDtypeStruct(s, F32) for s in shapes] if many else jax.ShapeDtypeStruct(shapes, F32)
     return pl.pallas_call(
         kernel,
         out_shape=out,
         in_specs=specs,
-        out_specs=[VMEM] * len(shapes) if many else VMEM,
-        scratch_shapes=[pltpu.VMEM(s, F32) for s in scratch],
-        compiler_params=pltpu.CompilerParams(vmem_limit_bytes=24 * 2**20),
+        out_specs=out_specs or ([VMEM] * len(shapes) if many else VMEM),
+        scratch_shapes=[pltpu.VMEM(s, F32) if isinstance(s, tuple) else s for s in scratch],
+        input_output_aliases=aliases or {},
+        compiler_params=pltpu.CompilerParams(vmem_limit_bytes=limit * 2**20),
     )
 
 
@@ -275,41 +302,50 @@
     batch, steps, moves = (a.reshape(1, SLOTS) for a in (batch_map, sub_steps, migrate_to))
     table = jnp.asarray(np.kron(np.eye(ROWS * POINTS // 4), derivative_table()).astype(np.float32))
 
-    weighed = call(weigh_kernel, (ROWS, POINTS, lanes), [VMEM] * 4)(dyn, wind, mass_weight, table)
+    cells = LEV * SLOTS
+    dma = pltpu.SemaphoreType.DMA
+    ints = pltpu.VMEM((1, SLOTS), jnp.int32)
+    weighed, top, end = call(
+        weigh_kernel,
+        [(ROWS, POINTS, lanes), (1, POINTS, lanes), (1, POINTS, lanes)],
+        [HBM] * 5,
+        [(2, ROWS, POINTS, LEV), (ROWS, POINTS, LEV), (ROWS, POINTS), table.shape, ints, dma((5,))],
+        limit=60,
+    )(dyn, wind, mass_weight, table, batch)
     weighed, state_later = lax.optimization_barrier((weighed, state))
-    buckets = call(bucket_kernel, (N_GRP * LEV, lanes), [SMEM, VMEM])(migrate_to, state_later)
+    buckets = call(bucket_kernel, (N_GRP, SENT, 1, lanes), [SMEM, HBM], [dma((SLOTS,))], HBM, limit=60)(
+        migrate_to, state_later.reshape(LEV, SLOTS, 1, lanes)
+    )
     up = [(i, (i + 1) % N_GRP) for i in range(N_GRP)]
     down = [(j, i) for i, j in up]
-    before = lax.ppermute(weighed[ROWS - 1 :], "grp", up)
-    after = lax.ppermute(weighed[:1], "grp", down)
-    buckets, before, after = lax.optimization_barrier((buckets, before, after))
-    main = lax.all_to_all(buckets.reshape(N_GRP, LEV // 2, 2, lanes), "grp", 0, 0, tiled=True)
+    before = lax.ppermute(end, "grp", up)
+    after = lax.ppermute(top, "grp", down)
     inner, payload = call(
-        assemble_kernel, [(ROWS, POINTS, lanes), (SLOTS + 2 * ROWS, lanes)], [VMEM] * 4
-    )(weighed, before, after, batch)
-    gathered = lax.all_gather(payload, "mem", axis=0)
-    force, edge, send = call(
-        forcing_kernel, [(SLOTS, lanes), (N_MEM * ROWS, lanes), (N_GRP, lanes)], [VMEM] * 4
-    )(gathered, batch, moves, steps)
-    cells = LEV * SLOTS
+        assemble_kernel, [(ROWS, POINTS, lanes), (N_MEM, SLOTS + 2 * ROWS, lanes)], [VMEM] * 3
+    )(weighed, before, after)
+    gathered = lax.all_to_all(payload, "mem", 0, 0, tiled=True)
+    force, edge, filled = call(
+        forcing_kernel,
+        [(SLOTS, lanes), (N_MEM * ROWS, lanes), (N_GRP, SENT, 1, lanes)],
+        [VMEM] * 4 + [HBM],
+        [(N_GRP, 1, lanes), dma],
+        [VMEM, VMEM, HBM],
+        {4: 2},
+        limit=61,
+    )(gathered, batch, moves, steps, buckets)
+    main = lax.all_to_all(filled, "grp", 0, 0, tiled=True)
     mix, means = jnp.asarray(neighbours_table()), jnp.asarray(means_table())
     tendency = call(tendency_kernel, (SLOTS, lanes), [VMEM] * 4, [(cells, lanes)])(state, force, mix, means)
     tendencies = lax.all_gather(tendency, "mem", axis=0, tiled=True)
-    send, main, tendencies = lax.optimization_barrier((send, main, tendencies))
-    rest = lax.all_to_all(send.reshape(N_GRP, 1, lanes), "grp", 0, 0, tiled=True)
     dyn_next = call(next_kernel, (2, ROWS, POINTS, LEV), [VMEM] * 3)(dyn, inner, edge)
     phys = call(column_kernel, (2, SLOTS, LEV), [VMEM] * 2)(tendencies, gathered)
-
-    brought, origin = pl.pallas_call(
-        select_kernel,
-        out_shape=[jax.ShapeDtypeStruct((SLOTS, lanes), F32), jax.ShapeDtypeStruct((1, SLOTS), jnp.int32)],
-        in_specs=[VMEM],
-        out_specs=[VMEM] * 2,
-        compiler_params=pltpu.CompilerParams(vmem_limit_bytes=24 * 2**20),
-    )(rest.reshape(N_GRP, lanes))
-    new = call(arrive_kernel, (cells, lanes), [SMEM, VMEM, VMEM, VMEM], [(cells, lanes)] * 2)(
-        origin, main.reshape(N_GRP * LEV, lanes), brought, mix
-    )
+    new = call(
+        arrive_kernel,
+        (cells, lanes),
+        [VMEM] * 2,
+        [(cells, lanes)] * 2
+        + [(SLOTS, lanes), ints, pltpu.SMEM((1, SLOTS), jnp.int32), dma],
+    )(main.reshape(N_GRP * SENT, lanes), mix)
     crm_next = new.reshape(LEV, SLOTS, lanes).transpose(1, 0, 2)
     return (dyn_next.transpose(0, 3, 1, 2), phys.transpose(0, 2, 1), crm_next)
 

time: 109 us -> 127 us (1.17)
  Pallas kernels: 10.4 us -> 43.9 us
  blocking collectives: 44.1 us -> 20.4 us
  waiting for transfers between devices: 7.5 us -> 22.5 us
  local copies, waits for them, and re-layouts: 6.41 us -> 2.28 us
  starting transfers between devices: 39 us -> 36 us
    pallas_call x6 -> x5, Pallas kernels: 6.76 us -> 40.2 us  [the longest x1 30.9 us: on_device(): call(bucket_kernel, (N_GRP, SENT, 1, lanes), [SMEM, HBM], [dma((SLOTS,))]...]
    all_gather x1 -> x0, blocking collectives: 27.1 us -> none  [on_device(): gathered = lax.all_gather(payload, 'mem', axis=0)]
    all_to_all x2, waiting for transfers between devices: 7.49 us -> 21.5 us  [the longest x1 21.5 us: on_device(): main = lax.all_to_all(filled, 'grp', 0, 0, tiled=True)]
    unnamed x28 -> x18, local copies, waits for them, and re-layouts: 6.41 us -> 2.28 us
    all_gather x1, blocking collectives: 17.1 us -> 20.4 us  [on_device(): tendencies = lax.all_gather(tendency, 'mem', axis=0, tiled=True)]
    all_to_all x2, starting transfers between devices: 24.7 us -> 21.7 us  [the longest x1 12.4 us: on_device(): main = lax.all_to_all(filled, 'grp', 0, 0, tiled=True)]
  transfers between devices with their start and end apart: 4 -> 4, of which waited for: 1 -> 2; matrix products, arithmetic and copies ran while one was open for 0% -> 0% of each run, Pallas kernels for 6% -> 27%
where the time goes in v3:
time: 127 us; the launch traced here: 126 us
  Pallas kernels  43.9 us (35%)
  starting transfers between devices  36 us (28%)
  waiting for transfers between devices  22.5 us (18%)
  blocking collectives  20.4 us (16%)
  local copies, waits for them, and re-layouts  2.28 us (2%)
    pallas_call x1, Pallas kernels, on_device(): call(bucket_kernel, (N_GRP, SENT, 1, lanes), [SMEM, HBM], [dma((SLOTS,))]...  30.9 us
    all_to_all x1, waiting for transfers between devices, on_device(): main = lax.all_to_all(filled, 'grp', 0, 0, tiled=True)  21.5 us
    all_gather x1, blocking collectives, on_device(): tendencies = lax.all_gather(tendency, 'mem', axis=0, tiled=True)  20.4 us
    all_to_all x1, starting transfers between devices, on_device(): main = lax.all_to_all(filled, 'grp', 0, 0, tiled=True)  12.4 us
    ppermute x1, starting transfers between devices, on_device(): after = lax.ppermute(top, 'grp', down)  9.84 us
    all_to_all x1, starting transfers between devices, on_device(): gathered = lax.all_to_all(payload, 'mem', 0, 0, tiled=True)  9.27 us
    ppermute x1, starting transfers between devices, on_device(): before = lax.ppermute(end, 'grp', up)  4.51 us
    pallas_call x1, Pallas kernels, on_device(): call(arrive_kernel, (cells, lanes), [VMEM] * 2, [(cells, lanes)] * 2 + [(...  3.76 us
  transfers between devices with their start and end apart: 4, of which 2 were waited for; matrix products, arithmetic and copies ran while one was open for 0% of the time, Pallas kernels for 27%

profile of v3, /device:TPU:1, one launch (start us, length us, event | category | flops | bytes accessed | tf_op | source)
XLA Modules:
  0.0 125.9 jit_solution(4716137446043205329)
XLA Ops:
  0.6 1.9 %shard_map.121 = (f32[4,32,128]{2,1,0:T(8,128)}, f32[1,32,128]{2,1,0:T(8,128)}, f32[1,32,128]{2,1,0:T(8,128)}) custom-call(f32[2,4,32,58]{3,2,1,0:T(8,128)} %bitcast.20, f32[4,32,58]{2,1,0:T(8,128)} %bitcast.24, f32[4,32]{1,0:T(4,128)} %mass_at.1, f32[128,128]{1,0:T(8,128)} %constant.6.clone.table_at, s32[1,32]{1,0:T(1,128)} %bitcast.26), custom_call_target="tpu_custom_call" | custom-call | tf_op jit(solution)/shard_map/pallas_call | solution.py:308
  2.5 4.5 %collective-permute-start = (f32[1,32,128]{2,1,0:T(8,128)}, f32[1,32,128]{2,1,0:T(8,128)S(1)}, u32[]{:S(2)}, u32[]{:S(2)}) collective-permute-start(f32[1,32,128]{2,1,0:T(8,128)} %get-tuple-element.15), channel_id=1, source_target_pairs={{0,12},{12,24},{24,36},{36,48},{48,60},{60,72},{72,84},{84,96},{96... | collective-permute-start | bytes 49160 | tf_op jit(solution)/shard_map/ppermute | solution.py:321
  7.1 9.8 %collective-permute-start.1 = (f32[1,32,128]{2,1,0:T(8,128)}, f32[1,32,128]{2,1,0:T(8,128)S(1)}, u32[]{:S(2)}, u32[]{:S(2)}) collective-permute-start(f32[1,32,128]{2,1,0:T(8,128)} %get-tuple-element.16), channel_id=1, source_target_pairs={{12,0},{24,12},{36,24},{48,36},{60,48},{72,60},{84,72},{96,84},{10... | collective-permute-start | bytes 49160 | tf_op jit(solution)/shard_map/ppermute | solution.py:322
  16.9 0.0 collective-permute-done.before
  16.9 1.0 collective-permute-done.1.after
  17.9 0.8 copy-done.6
  18.8 1.0 shard_map.122
  19.7 9.3 %all-to-all-start = ((f32[12,40,128]{2,1,0:T(8,128)}), f32[12,40,128]{2,1,0:T(8,128)S(1)}, u32[]{:S(2)}, u32[]{:S(2)}) async-start(f32[12,40,128]{2,1,0:T(8,128)} %get-tuple-element.18), calls=%async_computation | async-start | bytes 491520 | tf_op jit(solution)/shard_map/all_to_all | solution.py:326
  29.0 30.9 %shard_map.123.buckets = f32[64,59,1,128]{3,2,1,0:T(1,128)} custom-call(s32[32]{0:T(128)} %migrate.1, f32[58,32,1,128]{3,2,1,0:T(1,128)} %bitcast.18), custom_call_target="tpu_custom_call" | custom-call | tf_op jit(solution)/shard_map/pallas_call | solution.py:316
  59.9 0.0 all-to-all-done.gathered
  59.9 0.0 copy-start.1
  59.9 0.7 copy-done.1
  60.6 2.7 %shard_map.124 = (f32[32,128]{1,0:T(8,128)}, f32[48,128]{1,0:T(8,128)}, f32[64,59,1,128]{3,2,1,0:T(1,128)}) custom-call(f32[12,40,128]{2,1,0:T(8,128)} %copy-done.1, s32[1,32]{1,0:T(1,128)} %bitcast.27, s32[1,32]{1,0:T(1,128)} %bitcast.28, s32[1,32]{1,0:T(1,128)} %bitcast.29, f32[64,59,1,128]{3,2,1,0:T(1,128)} %shard_map.123.buckets), custom_call_target="tpu_custom_call", output_to_operand_aliasing={{2}: (4, {})} | custom-call | tf_op jit(solution)/shard_map/pallas_call | solution.py:327
  63.3 0.0 copy-start.4
  63.3 0.0 copy-start.7
  63.4 0.0 copy-start
  63.4 0.0 copy-start.3
  63.4 0.0 copy-start.5
  63.4 0.0 copy-start.2
  63.4 12.4 %all-to-all-start.1 = ((f32[64,59,1,128]{3,2,1,0:T(1,128)}), f32[64,59,1,128]{3,2,1,0:T(1,128)S(1)}, u32[]{:S(2)}, u32[]{:S(2)}) async-start(f32[64,59,1,128]{3,2,1,0:T(1,128)} %get-tuple-element.22), calls=%async_computation.1 | async-start | bytes 3866624 | tf_op jit(solution)/shard_map/all_to_all | solution.py:336
  75.8 0.0 copy-done.4
  75.8 0.0 copy-done.7
  75.8 0.8 shard_map.125
  76.6 0.0 copy-done
  76.6 0.0 copy-done.3
  76.6 0.7 copy-done.8
  77.3 1.9 %shard_map.126 = f32[32,128]{1,0:T(8,128)S(1)} custom-call(f32[1856,128]{1,0:T(8,128)S(1)} %bitcast.19, f32[32,128]{1,0:T(8,128)S(1)} %copy-done.8, bf16[256,256]{1,0:T(8,128)(2,1)S(1)} %copy-done.3, bf16[256,128]{1,0:T(8,128)(2,1)S(1)} %copy-done.5), custom_call_target="tpu_custom_call" | custom-call | tf_op jit(solution)/shard_map/pallas_call | solution.py:338
  79.2 20.4 %all_gather.3.tendency = f32[384,128]{1,0:T(8,128)S(1)} all-gather(f32[32,128]{1,0:T(8,128)S(1)} %shard_map.126), channel_id=1, replica_groups=mesh['grp'=64,'mem'=12] {'mem'}, dimensions={0}, use_global_device_ids=true | all-gather | bytes 212992 | tf_op jit(solution)/shard_map/all_gather | solution.py:339
  99.6 0.0 copy-done.2
  99.6 1.0 shard_map.127
  100.6 21.5 %all-to-all-done.1 = f32[64,59,1,128]{3,2,1,0:T(1,128)S(1)} async-done(((f32[64,59,1,128]{3,2,1,0:T(1,128)}), f32[64,59,1,128]{3,2,1,0:T(1,128)S(1)}, u32[]{:S(2)}, u32[]{:S(2)}) %all-to-all-start.1) | async-done | bytes 1933344 | tf_op jit(solution)/shard_map/all_to_all | solution.py:336
  122.1 3.8 %shard_map.128 = f32[1856,128]{1,0:T(8,128)} custom-call(f32[3776,128]{1,0:T(8,128)S(1)} %bitcast.17, bf16[256,256]{1,0:T(8,128)(2,1)S(1)} %copy-done.3), custom_call_target="tpu_custom_call" | custom-call | tf_op jit(solution)/shard_map/pallas_call | solution.py:342
  (3 shorter events, 0.0 us)
Async XLA Ops:
  2.5 14.4 %collective-permute-start = (f32[1,32,128]{2,1,0:T(8,128)}, f32[1,32,128]{2,1,0:T(8,128)S(1)}, u32[]{:S(2)}, u32[]{:S(2)}) collective-permute-start(f32[1,32,128]{2,1,0:T(8,128)} %get-tuple-element.15), channel_id=1, source_target_pairs={{0,12},{12,24},{24,36},{36,48},{48,60},{60,72},{72,84},{84,96},{96... | collective-permute-start | bytes 49160 | tf_op jit(solution)/shard_map/ppermute | solution.py:321
  7.1 10.9 %collective-permute-start.1 = (f32[1,32,128]{2,1,0:T(8,128)}, f32[1,32,128]{2,1,0:T(8,128)S(1)}, u32[]{:S(2)}, u32[]{:S(2)}) collective-permute-start(f32[1,32,128]{2,1,0:T(8,128)} %get-tuple-element.16), channel_id=1, source_target_pairs={{12,0},{24,12},{36,24},{48,36},{60,48},{72,60},{84,72},{96,84},{10... | collective-permute-start | bytes 49160 | tf_op jit(solution)/shard_map/ppermute | solution.py:322
  17.9 0.8 copy-start.6
  19.7 40.1 %all-to-all-start = ((f32[12,40,128]{2,1,0:T(8,128)}), f32[12,40,128]{2,1,0:T(8,128)S(1)}, u32[]{:S(2)}, u32[]{:S(2)}) async-start(f32[12,40,128]{2,1,0:T(8,128)} %get-tuple-element.18), calls=%async_computation | async-start | bytes 491520 | tf_op jit(solution)/shard_map/all_to_all | solution.py:326
  59.9 0.7 copy-start.1
  63.3 12.5 %copy-start.4 = (f32[2,58,4,32]{1,3,2,0:T(8,128)S(1)}, f32[2,58,4,32]{1,3,2,0:T(8,128)}, u32[]{:S(2)}) copy-start(f32[2,58,4,32]{1,3,2,0:T(8,128)} %param.10) | copy-start | bytes 178180
  63.3 12.5 %copy-start.7 = (f32[48,128]{1,0:T(8,128)S(1)}, f32[48,128]{1,0:T(8,128)}, u32[]{:S(2)}) copy-start(f32[48,128]{1,0:T(8,128)} %get-tuple-element.20.edge) | copy-start | bytes 73732
  63.4 13.3 %copy-start = (f32[32,58,128]{2,0,1:T(8,128)S(1)}, f32[32,58,128]{2,0,1:T(8,128)}, u32[]{:S(2)}) copy-start(f32[32,58,128]{2,0,1:T(8,128)} %param.13) | copy-start | bytes 2850820
  63.4 13.2 %copy-start.3 = (bf16[256,256]{1,0:T(8,128)(2,1)S(1)}, bf16[256,256]{1,0:T(8,128)(2,1)}, u32[]{:S(2)}) copy-start(bf16[256,256]{1,0:T(8,128)(2,1)} %constant.7.clone.table) | copy-start | bytes 393220
  63.4 13.2 %copy-start.5 = (bf16[256,128]{1,0:T(8,128)(2,1)S(1)}, bf16[256,128]{1,0:T(8,128)(2,1)}, u32[]{:S(2)}) copy-start(bf16[256,128]{1,0:T(8,128)(2,1)} %constant.8.clone.means) | copy-start | bytes 196612
  63.4 36.2 %copy-start.2 = (f32[12,40,128]{2,1,0:T(8,128)S(1)}, f32[12,40,128]{2,1,0:T(8,128)}, u32[]{:S(2)}) copy-start(f32[12,40,128]{2,1,0:T(8,128)} %copy-done.1) | copy-start | bytes 737284
  63.4 58.7 %all-to-all-start.1 = ((f32[64,59,1,128]{3,2,1,0:T(1,128)}), f32[64,59,1,128]{3,2,1,0:T(1,128)S(1)}, u32[]{:S(2)}, u32[]{:S(2)}) async-start(f32[64,59,1,128]{3,2,1,0:T(1,128)} %get-tuple-element.22), calls=%async_computation.1 | async-start | bytes 3866624 | tf_op jit(solution)/shard_map/all_to_all | solution.py:336
  76.6 0.7 copy-start.8

commit v4 on v3

--- a/solution.py
+++ b/solution.py
@@ -58,16 +58,10 @@
     return jnp.concatenate([heat, gap, moist, gap], axis=1)
 
 
-def bucket_kernel(migrate, state, out, done):
-    copies = []
+def bucket_kernel(migrate, state, out):
     for s in range(SLOTS):
         group = lax.div(migrate[s], COLS)
-        copies.append(
-            pltpu.make_async_copy(state.at[:, s], out.at[group, pl.ds(0, LEV)], done.at[s])
-        )
-        copies[-1].start()
-    for copy in copies:
-        copy.wait()
+        out[pl.ds(group * SENT, LEV), :] = state[pl.ds(s, LEV, stride=SLOTS), :]
 
 
 def weigh_kernel(dyn_at, wind_at, mass_at, table_at, batch_at, out, top, end, dyn, wind, mass, table, batch, done):
@@ -313,9 +307,7 @@
         limit=60,
     )(dyn, wind, mass_weight, table, batch)
     weighed, state_later = lax.optimization_barrier((weighed, state))
-    buckets = call(bucket_kernel, (N_GRP, SENT, 1, lanes), [SMEM, HBM], [dma((SLOTS,))], HBM, limit=60)(
-        migrate_to, state_later.reshape(LEV, SLOTS, 1, lanes)
-    )
+    buckets = call(bucket_kernel, (N_GRP * SENT, lanes), [SMEM, VMEM])(migrate_to, state_later)
     up = [(i, (i + 1) % N_GRP) for i in range(N_GRP)]
     down = [(j, i) for i, j in up]
     before = lax.ppermute(end, "grp", up)
@@ -332,7 +324,7 @@
         [VMEM, VMEM, HBM],
         {4: 2},
         limit=61,
-    )(gathered, batch, moves, steps, buckets)
+    )(gathered, batch, moves, steps, buckets.reshape(N_GRP, SENT, 1, lanes))
     main = lax.all_to_all(filled, "grp", 0, 0, tiled=True)
     mix, means = jnp.asarray(neighbours_table()), jnp.asarray(means_table())
     tendency = call(tendency_kernel, (SLOTS, lanes), [VMEM] * 4, [(cells, lanes)])(state, force, mix, means)

time: 127 us -> 109 us (0.86)
  Pallas kernels: 43.9 us -> 14.2 us
  waiting for transfers between devices: 22.5 us -> 31.1 us
  local copies, waits for them, and re-layouts: 2.28 us -> 5.4 us
  starting transfers between devices: 36 us -> 37.3 us
    pallas_call x1, Pallas kernels: 30.9 us -> 1.1 us  [on_device(): call(bucket_kernel, (N_GRP * SENT, lanes), [SMEM, VMEM])]
    all_to_all x1, waiting for transfers between devices: 0.01 us -> 7.43 us  [on_device(): gathered = lax.all_to_all(payload, 'mem', 0, 0, tiled=True)]
    unnamed x18 -> x24, local copies, waits for them, and re-layouts: 2.28 us -> 5.4 us
    all_to_all x1, starting transfers between devices: 12.4 us -> 13.7 us  [on_device(): main = lax.all_to_all(filled, 'grp', 0, 0, tiled=True)]
  transfers between devices with their start and end apart: 4 -> 4, of which waited for: 2 -> 3; matrix products, arithmetic and copies ran while one was open for 0% -> 0% of each run, Pallas kernels for 27% -> 4%
where the time goes in v4:
time: 109 us; the launch traced here: 108 us
  starting transfers between devices  37.3 us (34%)
  waiting for transfers between devices  31.1 us (29%)
  blocking collectives  19.2 us (18%)
  Pallas kernels  14.2 us (13%)
  local copies, waits for them, and re-layouts  5.4 us (5%)
    all_to_all x1, waiting for transfers between devices, on_device(): main = lax.all_to_all(filled, 'grp', 0, 0, tiled=True)  22.7 us
    all_gather x1, blocking collectives, on_device(): tendencies = lax.all_gather(tendency, 'mem', axis=0, tiled=True)  19.2 us
    all_to_all x1, starting transfers between devices, on_device(): main = lax.all_to_all(filled, 'grp', 0, 0, tiled=True)  13.7 us
    ppermute x1, starting transfers between devices, on_device(): after = lax.ppermute(top, 'grp', down)  9.84 us
    all_to_all x1, starting transfers between devices, on_device(): gathered = lax.all_to_all(payload, 'mem', 0, 0, tiled=True)  9.27 us
    all_to_all x1, waiting for transfers between devices, on_device(): gathered = lax.all_to_all(payload, 'mem', 0, 0, tiled=True)  7.43 us
    unnamed x24, local copies, waits for them, and re-layouts  5.4 us
    ppermute x1, starting transfers between devices, on_device(): before = lax.ppermute(end, 'grp', up)  4.51 us
  transfers between devices with their start and end apart: 4, of which 3 were waited for; matrix products, arithmetic and copies ran while one was open for 0% of the time, Pallas kernels for 4%

profile of v4, /device:TPU:1, one launch (start us, length us, event | category | flops | bytes accessed | tf_op | source)
XLA Modules:
  0.0 108.0 jit_solution(8726286799131645122)
XLA Ops:
  0.6 1.9 %shard_map.121 = (f32[4,32,128]{2,1,0:T(8,128)}, f32[1,32,128]{2,1,0:T(8,128)}, f32[1,32,128]{2,1,0:T(8,128)}) custom-call(f32[2,4,32,58]{3,2,1,0:T(8,128)} %bitcast.19, f32[4,32,58]{2,1,0:T(8,128)} %bitcast.24, f32[4,32]{1,0:T(4,128)} %mass_at.1, f32[128,128]{1,0:T(8,128)} %constant.6.clone.table_at, s32[1,32]{1,0:T(1,128)} %bitcast.26), custom_call_target="tpu_custom_call" | custom-call | tf_op jit(solution)/shard_map/pallas_call | solution.py:302
  2.5 4.5 %collective-permute-start = (f32[1,32,128]{2,1,0:T(8,128)}, f32[1,32,128]{2,1,0:T(8,128)S(1)}, u32[]{:S(2)}, u32[]{:S(2)}) collective-permute-start(f32[1,32,128]{2,1,0:T(8,128)} %get-tuple-element.15), channel_id=1, source_target_pairs={{0,12},{12,24},{24,36},{36,48},{48,60},{60,72},{72,84},{84,96},{96... | collective-permute-start | bytes 49160 | tf_op jit(solution)/shard_map/ppermute | solution.py:313
  7.1 9.8 %collective-permute-start.1 = (f32[1,32,128]{2,1,0:T(8,128)}, f32[1,32,128]{2,1,0:T(8,128)S(1)}, u32[]{:S(2)}, u32[]{:S(2)}) collective-permute-start(f32[1,32,128]{2,1,0:T(8,128)} %get-tuple-element.16), channel_id=1, source_target_pairs={{12,0},{24,12},{36,24},{48,36},{60,48},{72,60},{84,72},{96,84},{10... | collective-permute-start | bytes 49160 | tf_op jit(solution)/shard_map/ppermute | solution.py:314
  16.9 0.0 collective-permute-done.before
  16.9 1.0 collective-permute-done.1.after
  17.9 0.8 copy-done.8
  18.8 1.0 shard_map.122
  19.7 9.3 %all-to-all-start = ((f32[12,40,128]{2,1,0:T(8,128)}), f32[12,40,128]{2,1,0:T(8,128)S(1)}, u32[]{:S(2)}, u32[]{:S(2)}) async-start(f32[12,40,128]{2,1,0:T(8,128)} %get-tuple-element.18), calls=%async_computation | async-start | bytes 491520 | tf_op jit(solution)/shard_map/all_to_all | solution.py:318
  29.0 0.0 copy-start.1
  29.0 1.2 %copy-done.1 = f32[32,58,128]{2,0,1:T(8,128)S(1)} copy-done((f32[32,58,128]{2,0,1:T(8,128)S(1)}, f32[32,58,128]{2,0,1:T(8,128)}, u32[]{:S(2)}) %copy-start.1) | copy-done | bytes 950296
  30.2 0.7 copy-done.11
  30.9 1.1 %shard_map.123 = f32[3776,128]{1,0:T(8,128)S(1)} custom-call(s32[32]{0:T(128)S(1)} %copy-done.11, f32[1856,128]{1,0:T(8,128)S(1)} %bitcast.17), custom_call_target="tpu_custom_call" | custom-call | tf_op jit(solution)/shard_map/pallas_call | solution.py:310
  32.0 0.0 copy-start
  32.0 1.3 %copy-done = f32[3776,128]{1,0:T(8,128)} copy-done((f32[3776,128]{1,0:T(8,128)}, f32[3776,128]{1,0:T(8,128)S(1)}, u32[]{:S(2)}) %copy-start) | copy-done | bytes 1933336
  33.3 7.4 %all-to-all-done.gathered = f32[12,40,128]{2,1,0:T(8,128)S(1)} async-done(((f32[12,40,128]{2,1,0:T(8,128)}), f32[12,40,128]{2,1,0:T(8,128)S(1)}, u32[]{:S(2)}, u32[]{:S(2)}) %all-to-all-start) | async-done | bytes 245792 | tf_op jit(solution)/shard_map/all_to_all | solution.py:318
  40.7 0.7 copy-done.3
  41.4 2.8 %shard_map.124 = (f32[32,128]{1,0:T(8,128)}, f32[48,128]{1,0:T(8,128)}, f32[64,59,1,128]{3,2,1,0:T(1,128)}) custom-call(f32[12,40,128]{2,1,0:T(8,128)} %copy-done.3, s32[1,32]{1,0:T(1,128)} %bitcast.27, s32[1,32]{1,0:T(1,128)} %bitcast.21, s32[1,32]{1,0:T(1,128)} %bitcast.28, f32[64,59,1,128]{3,2,1,0:T(1,128)} %bitcast.15), custom_call_target="tpu_custom_call", output_to_operand_aliasing={{2}: (4, {})} | custom-call | tf_op jit(solution)/shard_map/pallas_call | solution.py:319
  44.2 0.0 copy-start.6
  44.2 0.0 copy-start.9
  44.2 0.0 copy-start.2
  44.2 0.0 copy-start.5
  44.2 0.0 copy-start.7
  44.2 0.0 copy-start.4
  44.2 13.7 %all-to-all-start.1 = ((f32[64,59,1,128]{3,2,1,0:T(1,128)}), f32[64,59,1,128]{3,2,1,0:T(1,128)S(1)}, u32[]{:S(2)}, u32[]{:S(2)}) async-start(f32[64,59,1,128]{3,2,1,0:T(1,128)} %get-tuple-element.22), calls=%async_computation.1 | async-start | bytes 3866624 | tf_op jit(solution)/shard_map/all_to_all | solution.py:328
  58.0 0.8 shard_map.125
  58.7 0.0 copy-done.2
  58.7 0.7 copy-done.10
  59.4 1.9 %shard_map.126 = f32[32,128]{1,0:T(8,128)S(1)} custom-call(f32[1856,128]{1,0:T(8,128)S(1)} %bitcast.18, f32[32,128]{1,0:T(8,128)S(1)} %copy-done.10, bf16[256,256]{1,0:T(8,128)(2,1)S(1)} %copy-done.5, bf16[256,128]{1,0:T(8,128)(2,1)S(1)} %copy-done.7), custom_call_target="tpu_custom_call" | custom-call | tf_op jit(solution)/shard_map/pallas_call | solution.py:330
  61.3 19.2 %all_gather.3.tendency = f32[384,128]{1,0:T(8,128)S(1)} all-gather(f32[32,128]{1,0:T(8,128)S(1)} %shard_map.126), channel_id=1, replica_groups=mesh['grp'=64,'mem'=12] {'mem'}, dimensions={0}, use_global_device_ids=true | all-gather | bytes 212992 | tf_op jit(solution)/shard_map/all_gather | solution.py:331
  80.5 1.0 shard_map.127
  81.5 22.7 %all-to-all-done.1 = f32[64,59,1,128]{3,2,1,0:T(1,128)S(1)} async-done(((f32[64,59,1,128]{3,2,1,0:T(1,128)}), f32[64,59,1,128]{3,2,1,0:T(1,128)S(1)}, u32[]{:S(2)}, u32[]{:S(2)}) %all-to-all-start.1) | async-done | bytes 1933344 | tf_op jit(solution)/shard_map/all_to_all | solution.py:328
  104.2 3.8 %shard_map.128 = f32[1856,128]{1,0:T(8,128)} custom-call(f32[3776,128]{1,0:T(8,128)S(1)} %bitcast.16, bf16[256,256]{1,0:T(8,128)(2,1)S(1)} %copy-done.5), custom_call_target="tpu_custom_call" | custom-call | tf_op jit(solution)/shard_map/pallas_call | solution.py:334
  (9 shorter events, 0.0 us)
Async XLA Ops:
  2.5 14.4 %collective-permute-start = (f32[1,32,128]{2,1,0:T(8,128)}, f32[1,32,128]{2,1,0:T(8,128)S(1)}, u32[]{:S(2)}, u32[]{:S(2)}) collective-permute-start(f32[1,32,128]{2,1,0:T(8,128)} %get-tuple-element.15), channel_id=1, source_target_pairs={{0,12},{12,24},{24,36},{36,48},{48,60},{60,72},{72,84},{84,96},{96... | collective-permute-start | bytes 49160 | tf_op jit(solution)/shard_map/ppermute | solution.py:313
  7.1 10.9 %collective-permute-start.1 = (f32[1,32,128]{2,1,0:T(8,128)}, f32[1,32,128]{2,1,0:T(8,128)S(1)}, u32[]{:S(2)}, u32[]{:S(2)}) collective-permute-start(f32[1,32,128]{2,1,0:T(8,128)} %get-tuple-element.16), channel_id=1, source_target_pairs={{12,0},{24,12},{36,24},{48,36},{60,48},{72,60},{84,72},{96,84},{10... | collective-permute-start | bytes 49160 | tf_op jit(solution)/shard_map/ppermute | solution.py:314
  17.9 0.8 copy-start.8
  19.7 21.0 %all-to-all-start = ((f32[12,40,128]{2,1,0:T(8,128)}), f32[12,40,128]{2,1,0:T(8,128)S(1)}, u32[]{:S(2)}, u32[]{:S(2)}) async-start(f32[12,40,128]{2,1,0:T(8,128)} %get-tuple-element.18), calls=%async_computation | async-start | bytes 491520 | tf_op jit(solution)/shard_map/all_to_all | solution.py:318
  29.0 1.2 %copy-start.1 = (f32[32,58,128]{2,0,1:T(8,128)S(1)}, f32[32,58,128]{2,0,1:T(8,128)}, u32[]{:S(2)}) copy-start(f32[32,58,128]{2,0,1:T(8,128)} %param.13) | copy-start | bytes 2850820
  30.2 0.7 copy-start.11
  32.0 1.3 %copy-start = (f32[3776,128]{1,0:T(8,128)}, f32[3776,128]{1,0:T(8,128)S(1)}, u32[]{:S(2)}) copy-start(f32[3776,128]{1,0:T(8,128)S(1)} %shard_map.123) | copy-start | bytes 5799940
  40.7 0.7 copy-start.3
  44.2 13.8 %copy-start.6 = (f32[2,58,4,32]{1,3,2,0:T(8,128)S(1)}, f32[2,58,4,32]{1,3,2,0:T(8,128)}, u32[]{:S(2)}) copy-start(f32[2,58,4,32]{1,3,2,0:T(8,128)} %param.10) | copy-start | bytes 178180
  44.2 13.8 %copy-start.9 = (f32[48,128]{1,0:T(8,128)S(1)}, f32[48,128]{1,0:T(8,128)}, u32[]{:S(2)}) copy-start(f32[48,128]{1,0:T(8,128)} %get-tuple-element.20.edge) | copy-start | bytes 73732
  44.2 14.5 %copy-start.2 = (f32[32,58,128]{2,0,1:T(8,128)S(1)}, f32[32,58,128]{2,0,1:T(8,128)}, u32[]{:S(2)}) copy-start(f32[32,58,128]{2,0,1:T(8,128)} %param.13) | copy-start | bytes 2850820
  44.2 14.5 %copy-start.5 = (bf16[256,256]{1,0:T(8,128)(2,1)S(1)}, bf16[256,256]{1,0:T(8,128)(2,1)}, u32[]{:S(2)}) copy-start(bf16[256,256]{1,0:T(8,128)(2,1)} %constant.7.clone.table) | copy-start | bytes 393220
  44.2 14.5 %copy-start.7 = (bf16[256,128]{1,0:T(8,128)(2,1)S(1)}, bf16[256,128]{1,0:T(8,128)(2,1)}, u32[]{:S(2)}) copy-start(bf16[256,128]{1,0:T(8,128)(2,1)} %constant.8.clone.means) | copy-start | bytes 196612
  44.2 36.3 %copy-start.4 = (f32[12,40,128]{2,1,0:T(8,128)S(1)}, f32[12,40,128]{2,1,0:T(8,128)}, u32[]{:S(2)}) copy-start(f32[12,40,128]{2,1,0:T(8,128)} %copy-done.3) | copy-start | bytes 737284
  44.2 60.0 %all-to-all-start.1 = ((f32[64,59,1,128]{3,2,1,0:T(1,128)}), f32[64,59,1,128]{3,2,1,0:T(1,128)S(1)}, u32[]{:S(2)}, u32[]{:S(2)}) async-start(f32[64,59,1,128]{3,2,1,0:T(1,128)} %get-tuple-element.22), calls=%async_computation.1 | async-start | bytes 3866624 | tf_op jit(solution)/shard_map/all_to_all | solution.py:328
  58.7 0.7 copy-start.10

commit v5 on v4

--- a/solution.py
+++ b/solution.py
@@ -58,10 +58,11 @@
     return jnp.concatenate([heat, gap, moist, gap], axis=1)
 
 
-def bucket_kernel(migrate, state, out):
+def bucket_kernel(migrate, state, early, late):
     for s in range(SLOTS):
         group = lax.div(migrate[s], COLS)
-        out[pl.ds(group * SENT, LEV), :] = state[pl.ds(s, LEV, stride=SLOTS), :]
+        early[pl.ds(group * EARLY, EARLY), :] = state[pl.ds(s, EARLY, stride=SLOTS), :]
+        late[pl.ds(group * SENT, LATE), :] = state[pl.ds(EARLY * SLOTS + s, LATE, stride=SLOTS), :]
 
 
 def weigh_kernel(dyn_at, wind_at, mass_at, table_at, batch_at, out, top, end, dyn, wind, mass, table, batch, done):
@@ -110,12 +111,10 @@
     right = [row[POINTS - 1 : POINTS] for row in edges]
     lane = iota((SLOTS, 2 * HALF), 1)
     forcing = jnp.where(lane == LEV, own[0][:, LEV + 1 : LEV + 2], forcing)
-    whole = jnp.concatenate([forcing] + left + right, axis=0)
-    for d in range(N_MEM):
-        payload[d] = whole
-
-
-def forcing_kernel(gathered, batch, migrate, steps, buckets, force, edge, filled, row, done):
+    payload[...] = jnp.concatenate([forcing] + left + right, axis=0)
+
+
+def forcing_kernel(gathered, batch, migrate, steps, late, force, edge, filled):
     rows = []
     for d in range(N_MEM):
         right = gathered[d, SLOTS + ROWS : SLOTS + 2 * ROWS, :]
@@ -142,10 +141,8 @@
     force[...] = forced
     group = jnp.floor((new.astype(F32) + 0.5) * (1.0 / COLS)).astype(jnp.int32)
     goes = jnp.where(iota((N_GRP, SLOTS), 0) == group, 1.0, 0.0).astype(F32)
-    row[...] = dot(goes, forced).reshape(N_GRP, 1, 2 * HALF)
-    copy = pltpu.make_async_copy(row, filled.at[:, LEV], done)
-    copy.start()
-    copy.wait()
+    filled[...] = late[...]
+    filled[pl.ds(LATE, N_GRP, stride=SENT), :] = dot(goes, forced)
 
 
 def neighbours_table():
@@ -171,7 +168,9 @@
     return jnp.concatenate([lead, trail], axis=1)
 
 
-SENT = LEV + 1
+EARLY = 30
+LATE = LEV - EARLY
+SENT = LATE + 1
 CHUNKS = [(0, 8), (8, 8), (16, 8), (24, 8), (32, 8), (40, 8), (48, 8), (56, 2)]
 
 
@@ -234,8 +233,8 @@
     run_cloud(state, force, table, middle, keep)
 
 
-def arrive_kernel(main, table, out, held, middle, force, row, origin, done):
-    last = main[pl.ds(LEV, N_GRP, stride=SENT), :]
+def arrive_kernel(early, late, table, out, held, middle, force, row, origin, done):
+    last = late[pl.ds(LATE, N_GRP, stride=SENT), :]
     slot = (iota((N_GRP, SLOTS), 1) + 1).astype(F32)
     pick = jnp.where(last[:, LEV : LEV + 1] == slot, 1.0, 0.0).astype(F32)
     group = iota((N_GRP, SLOTS), 0).astype(F32)
@@ -245,7 +244,9 @@
     force[...] = dot_t(pick, last)
     copy.wait()
     for j in range(SLOTS):
-        held[pl.ds(j, LEV, stride=SLOTS), :] = main[pl.ds(origin[0, j] * SENT, LEV), :]
+        g = origin[0, j]
+        held[pl.ds(j, EARLY, stride=SLOTS), :] = early[pl.ds(g * EARLY, EARLY), :]
+        held[pl.ds(EARLY * SLOTS + j, LATE, stride=SLOTS), :] = late[pl.ds(g * SENT, LATE), :]
 
     def keep(first, count, stepped):
         out[first * SLOTS : (first + count) * SLOTS, :] = stepped
@@ -307,25 +308,26 @@
         limit=60,
     )(dyn, wind, mass_weight, table, batch)
     weighed, state_later = lax.optimization_barrier((weighed, state))
-    buckets = call(bucket_kernel, (N_GRP * SENT, lanes), [SMEM, VMEM])(migrate_to, state_later)
+    early, late = call(bucket_kernel, [(N_GRP * EARLY, lanes), (N_GRP * SENT, lanes)], [SMEM, VMEM])(
+        migrate_to, state_later
+    )
     up = [(i, (i + 1) % N_GRP) for i in range(N_GRP)]
     down = [(j, i) for i, j in up]
     before = lax.ppermute(end, "grp", up)
     after = lax.ppermute(top, "grp", down)
+    early, before, after = lax.optimization_barrier((early, before, after))
+    first = lax.all_to_all(early.reshape(N_GRP, EARLY, 1, lanes), "grp", 0, 0, tiled=True)
     inner, payload = call(
-        assemble_kernel, [(ROWS, POINTS, lanes), (N_MEM, SLOTS + 2 * ROWS, lanes)], [VMEM] * 3
+        assemble_kernel, [(ROWS, POINTS, lanes), (SLOTS + 2 * ROWS, lanes)], [VMEM] * 3
     )(weighed, before, after)
-    gathered = lax.all_to_all(payload, "mem", 0, 0, tiled=True)
+    gathered = lax.all_gather(payload, "mem", axis=0)
     force, edge, filled = call(
         forcing_kernel,
-        [(SLOTS, lanes), (N_MEM * ROWS, lanes), (N_GRP, SENT, 1, lanes)],
-        [VMEM] * 4 + [HBM],
-        [(N_GRP, 1, lanes), dma],
-        [VMEM, VMEM, HBM],
-        {4: 2},
-        limit=61,
-    )(gathered, batch, moves, steps, buckets.reshape(N_GRP, SENT, 1, lanes))
-    main = lax.all_to_all(filled, "grp", 0, 0, tiled=True)
+        [(SLOTS, lanes), (N_MEM * ROWS, lanes), (N_GRP * SENT, lanes)],
+        [VMEM] * 5,
+    )(gathered, batch, moves, steps, late)
+    filled, first = lax.optimization_barrier((filled, first))
+    second = lax.all_to_all(filled.reshape(N_GRP, SENT, 1, lanes), "grp", 0, 0, tiled=True)
     mix, means = jnp.asarray(neighbours_table()), jnp.asarray(means_table())
     tendency = call(tendency_kernel, (SLOTS, lanes), [VMEM] * 4, [(cells, lanes)])(state, force, mix, means)
     tendencies = lax.all_gather(tendency, "mem", axis=0, tiled=True)
@@ -334,10 +336,10 @@
     new = call(
         arrive_kernel,
         (cells, lanes),
-        [VMEM] * 2,
+        [VMEM] * 3,
         [(cells, lanes)] * 2
         + [(SLOTS, lanes), ints, pltpu.SMEM((1, SLOTS), jnp.int32), dma],
-    )(main.reshape(N_GRP * SENT, lanes), mix)
+    )(first.reshape(N_GRP * EARLY, lanes), second.reshape(N_GRP * SENT, lanes), mix)
     crm_next = new.reshape(LEV, SLOTS, lanes).transpose(1, 0, 2)
     return (dyn_next.transpose(0, 3, 1, 2), phys.transpose(0, 2, 1), crm_next)
 

time: 109 us -> 101 us (0.927)
  waiting for transfers between devices: 31.1 us -> 5.24 us
  blocking collectives: 19.2 us -> 41.3 us
  Pallas kernels: 14.2 us -> 12.1 us
  local copies, waits for them, and re-layouts: 5.4 us -> 3.47 us
    all_to_all x2, waiting for transfers between devices: 30.1 us -> 5.23 us  [the longest x1 4.96 us: on_device(): lax.all_to_all(filled.reshape(N_GRP, SENT, 1, lanes), 'grp', 0, 0, tiled=...]
    all_gather x0 -> x1, blocking collectives: none -> 24 us  [on_device(): gathered = lax.all_gather(payload, 'mem', axis=0)]
    pallas_call x4, Pallas kernels: 8.59 us -> 6.57 us  [the longest x1 3.74 us: on_device(): call(arrive_kernel, (cells, lanes), [VMEM] * 3, [(cells, lanes)] * 2 + [(...]
    unnamed x24 -> x20, local copies, waits for them, and re-layouts: 5.4 us -> 3.47 us
    all_gather x1, blocking collectives: 19.2 us -> 17.3 us  [on_device(): tendencies = lax.all_gather(tendency, 'mem', axis=0, tiled=True)]
  transfers between devices with their start and end apart: 4 -> 4, of which waited for: 3 -> 2; matrix products, arithmetic and copies ran while one was open for 0% -> 0% of each run, Pallas kernels for 4% -> 6%
where the time goes in v5:
time: 101 us
  blocking collectives  41.3 us (41%)
  starting transfers between devices  38 us (38%)
  Pallas kernels  12.1 us (12%)
  waiting for transfers between devices  5.24 us (5%)
  local copies, waits for them, and re-layouts  3.47 us (3%)
    all_gather x1, blocking collectives, on_device(): gathered = lax.all_gather(payload, 'mem', axis=0)  24 us
    all_gather x1, blocking collectives, on_device(): tendencies = lax.all_gather(tendency, 'mem', axis=0, tiled=True)  17.3 us
    all_to_all x1, starting transfers between devices, on_device(): lax.all_to_all(filled.reshape(N_GRP, SENT, 1, lanes), 'grp', 0, 0, tiled=...  13.9 us
    ppermute x1, starting transfers between devices, on_device(): after = lax.ppermute(top, 'grp', down)  9.84 us
    all_to_all x1, starting transfers between devices, on_device(): lax.all_to_all(early.reshape(N_GRP, EARLY, 1, lanes), 'grp', 0, 0, tiled=...  9.77 us
    all_to_all x1, waiting for transfers between devices, on_device(): lax.all_to_all(filled.reshape(N_GRP, SENT, 1, lanes), 'grp', 0, 0, tiled=...  4.96 us
    ppermute x1, starting transfers between devices, on_device(): before = lax.ppermute(end, 'grp', up)  4.51 us
    pallas_call x1, Pallas kernels, on_device(): call(arrive_kernel, (cells, lanes), [VMEM] * 3, [(cells, lanes)] * 2 + [(...  3.74 us
  transfers between devices with their start and end apart: 4, of which 2 were waited for; matrix products, arithmetic and copies ran while one was open for 0% of the time, Pallas kernels for 6%

profile of v5, /device:TPU:1, one launch (start us, length us, event | category | flops | bytes accessed | tf_op | source)
XLA Modules:
  0.0 100.9 jit_solution(11348236143595994613)
XLA Ops:
  0.6 1.9 %shard_map.121 = (f32[4,32,128]{2,1,0:T(8,128)}, f32[1,32,128]{2,1,0:T(8,128)}, f32[1,32,128]{2,1,0:T(8,128)}) custom-call(f32[2,4,32,58]{3,2,1,0:T(8,128)} %bitcast.25, f32[4,32,58]{2,1,0:T(8,128)} %bitcast.33, f32[4,32]{1,0:T(4,128)} %mass_at.1, f32[128,128]{1,0:T(8,128)} %constant.6.clone.table_at, s32[1,32]{1,0:T(1,128)} %bitcast.28), custom_call_target="tpu_custom_call" | custom-call | tf_op jit(solution)/shard_map/pallas_call | solution.py:303
  2.5 4.5 %collective-permute-start = (f32[1,32,128]{2,1,0:T(8,128)}, f32[1,32,128]{2,1,0:T(8,128)S(1)}, u32[]{:S(2)}, u32[]{:S(2)}) collective-permute-start(f32[1,32,128]{2,1,0:T(8,128)} %get-tuple-element.24), channel_id=1, source_target_pairs={{0,12},{12,24},{24,36},{36,48},{48,60},{60,72},{72,84},{84,96},{96... | collective-permute-start | bytes 49160 | tf_op jit(solution)/shard_map/ppermute | solution.py:316
  7.1 9.8 %collective-permute-start.1 = (f32[1,32,128]{2,1,0:T(8,128)}, f32[1,32,128]{2,1,0:T(8,128)S(1)}, u32[]{:S(2)}, u32[]{:S(2)}) collective-permute-start(f32[1,32,128]{2,1,0:T(8,128)} %get-tuple-element.25), channel_id=1, source_target_pairs={{12,0},{24,12},{36,24},{48,36},{60,48},{72,60},{84,72},{96,84},{10... | collective-permute-start | bytes 49160 | tf_op jit(solution)/shard_map/ppermute | solution.py:317
  16.9 0.0 copy-start.7
  16.9 0.6 copy-done.7
  17.6 0.0 copy-start
  17.6 1.2 %copy-done = f32[32,58,128]{2,0,1:T(8,128)S(1)} copy-done((f32[32,58,128]{2,0,1:T(8,128)S(1)}, f32[32,58,128]{2,0,1:T(8,128)}, u32[]{:S(2)}) %copy-start) | copy-done | bytes 950296
  18.8 2.1 %shard_map.122 = (f32[1920,128]{1,0:T(8,128)}, f32[1856,128]{1,0:T(8,128)S(1)}) custom-call(s32[32]{0:T(128)S(1)} %copy-done.7, f32[1856,128]{1,0:T(8,128)S(1)} %bitcast.20), custom_call_target="tpu_custom_call" | custom-call | tf_op jit(solution)/shard_map/pallas_call | solution.py:311
  20.8 0.0 collective-permute-done.before
  20.8 0.0 collective-permute-done.1.after
  20.8 0.0 copy-start.6
  20.8 9.8 %all-to-all-start = ((f32[64,30,1,128]{3,2,1,0:T(1,128)}), f32[64,30,1,128]{3,2,1,0:T(1,128)S(1)}, u32[]{:S(2)}, u32[]{:S(2)}) async-start(f32[64,30,1,128]{3,2,1,0:T(1,128)} %bitcast.11), calls=%async_computation | async-start | bytes 1966080 | tf_op jit(solution)/shard_map/all_to_all | solution.py:319
  30.6 0.0 copy-done.6
  30.6 0.2 shard_map.123
  30.9 24.0 %all-gather = f32[480,128]{1,0:T(8,128)S(1)} all-gather(f32[40,128]{1,0:T(8,128)S(1)} %get-tuple-element.29), channel_id=2, replica_groups=mesh['grp'=64,'mem'=12] {'mem'}, dimensions={0}, use_global_device_ids=true | all-gather | bytes 266240 | tf_op jit(solution)/shard_map/all_gather | solution.py:323
  54.8 0.0 copy-start.8
  54.8 0.7 copy-done.8
  55.5 0.0 copy-done.9
  55.5 0.5 shard_map.124
  56.0 0.9 copy-done.2
  57.0 0.3 all-to-all-done
  57.3 13.9 %all-to-all-start.1 = ((f32[64,29,1,128]{3,2,1,0:T(1,128)}), f32[64,29,1,128]{3,2,1,0:T(1,128)S(1)}, u32[]{:S(2)}, u32[]{:S(2)}) async-start(f32[64,29,1,128]{3,2,1,0:T(1,128)} %bitcast.24), calls=%async_computation.1 | async-start | bytes 1900544 | tf_op jit(solution)/shard_map/all_to_all | solution.py:330
  71.2 0.0 copy-done.1
  71.2 0.0 copy-done.3
  71.2 0.0 copy-done.5
  71.2 1.9 %shard_map.126 = f32[32,128]{1,0:T(8,128)S(1)} custom-call(f32[1856,128]{1,0:T(8,128)S(1)} %bitcast.21, f32[32,128]{1,0:T(8,128)S(1)} %get-tuple-element.32.force, bf16[256,256]{1,0:T(8,128)(2,1)S(1)} %copy-done.3, bf16[256,128]{1,0:T(8,128)(2,1)S(1)} %copy-done.5), custom_call_target="tpu_custom_call" | custom-call | tf_op jit(solution)/shard_map/pallas_call | solution.py:332
  73.1 17.3 %all_gather.11.tendency = f32[384,128]{1,0:T(8,128)S(1)} all-gather(f32[32,128]{1,0:T(8,128)S(1)} %shard_map.126), channel_id=1, replica_groups=mesh['grp'=64,'mem'=12] {'mem'}, dimensions={0}, use_global_device_ids=true | all-gather | bytes 212992 | tf_op jit(solution)/shard_map/all_gather | solution.py:333
  90.4 1.0 %shard_map.127 = f32[2,32,58]{2,1,0:T(8,128)} custom-call(f32[384,128]{1,0:T(8,128)S(1)} %all_gather.11.tendency, f32[12,40,128]{2,1,0:T(8,128)S(1)} %bitcast.23), custom_call_target="tpu_custom_call" | custom-call | tf_op jit(solution)/shard_map/pallas_call | solution.py:335
  91.4 0.0 copy-done.4
  91.4 0.8 shard_map.125
  92.2 5.0 %all-to-all-done.1 = f32[64,29,1,128]{3,2,1,0:T(1,128)S(1)} async-done(((f32[64,29,1,128]{3,2,1,0:T(1,128)}), f32[64,29,1,128]{3,2,1,0:T(1,128)S(1)}, u32[]{:S(2)}, u32[]{:S(2)}) %all-to-all-start.1) | async-done | bytes 950304 | tf_op jit(solution)/shard_map/all_to_all | solution.py:330
  97.2 3.7 %shard_map.128 = f32[1856,128]{1,0:T(8,128)} custom-call(f32[1920,128]{1,0:T(8,128)S(1)} %bitcast.18, f32[1856,128]{1,0:T(8,128)S(1)} %bitcast.19, bf16[256,256]{1,0:T(8,128)(2,1)S(1)} %copy-done.3), custom_call_target="tpu_custom_call" | custom-call | tf_op jit(solution)/shard_map/pallas_call | solution.py:336
  (6 shorter events, 0.0 us)
Async XLA Ops:
  2.5 18.3 %collective-permute-start = (f32[1,32,128]{2,1,0:T(8,128)}, f32[1,32,128]{2,1,0:T(8,128)S(1)}, u32[]{:S(2)}, u32[]{:S(2)}) collective-permute-start(f32[1,32,128]{2,1,0:T(8,128)} %get-tuple-element.24), channel_id=1, source_target_pairs={{0,12},{12,24},{24,36},{36,48},{48,60},{60,72},{72,84},{84,96},{96... | collective-permute-start | bytes 49160 | tf_op jit(solution)/shard_map/ppermute | solution.py:316
  7.1 13.8 %collective-permute-start.1 = (f32[1,32,128]{2,1,0:T(8,128)}, f32[1,32,128]{2,1,0:T(8,128)S(1)}, u32[]{:S(2)}, u32[]{:S(2)}) collective-permute-start(f32[1,32,128]{2,1,0:T(8,128)} %get-tuple-element.25), channel_id=1, source_target_pairs={{12,0},{24,12},{36,24},{48,36},{60,48},{72,60},{84,72},{96,84},{10... | collective-permute-start | bytes 49160 | tf_op jit(solution)/shard_map/ppermute | solution.py:317
  16.9 0.7 copy-start.7
  17.6 1.2 %copy-start = (f32[32,58,128]{2,0,1:T(8,128)S(1)}, f32[32,58,128]{2,0,1:T(8,128)}, u32[]{:S(2)}) copy-start(f32[32,58,128]{2,0,1:T(8,128)} %param.13) | copy-start | bytes 2850820
  20.8 9.8 %copy-start.6 = (f32[4,32,128]{2,1,0:T(8,128)S(1)}, f32[4,32,128]{2,1,0:T(8,128)}, u32[]{:S(2)}) copy-start(f32[4,32,128]{2,1,0:T(8,128)} %get-tuple-element.21.own) | copy-start | bytes 196612
  20.8 36.4 %all-to-all-start = ((f32[64,30,1,128]{3,2,1,0:T(1,128)}), f32[64,30,1,128]{3,2,1,0:T(1,128)S(1)}, u32[]{:S(2)}, u32[]{:S(2)}) async-start(f32[64,30,1,128]{3,2,1,0:T(1,128)} %bitcast.11), calls=%async_computation | async-start | bytes 1966080 | tf_op jit(solution)/shard_map/all_to_all | solution.py:319
  54.8 0.7 copy-start.8
  54.8 0.7 copy-start.9
  56.0 0.9 copy-start.2
  57.3 13.9 %copy-start.1 = (f32[32,58,128]{2,0,1:T(8,128)S(1)}, f32[32,58,128]{2,0,1:T(8,128)}, u32[]{:S(2)}) copy-start(f32[32,58,128]{2,0,1:T(8,128)} %param.13) | copy-start | bytes 2850820
  57.3 13.9 %copy-start.3 = (bf16[256,256]{1,0:T(8,128)(2,1)S(1)}, bf16[256,256]{1,0:T(8,128)(2,1)}, u32[]{:S(2)}) copy-start(bf16[256,256]{1,0:T(8,128)(2,1)} %constant.7.clone.table) | copy-start | bytes 393220
  57.3 13.9 %copy-start.5 = (bf16[256,128]{1,0:T(8,128)(2,1)S(1)}, bf16[256,128]{1,0:T(8,128)(2,1)}, u32[]{:S(2)}) copy-start(bf16[256,128]{1,0:T(8,128)(2,1)} %constant.8.clone.means) | copy-start | bytes 196612
  57.3 39.9 %all-to-all-start.1 = ((f32[64,29,1,128]{3,2,1,0:T(1,128)}), f32[64,29,1,128]{3,2,1,0:T(1,128)S(1)}, u32[]{:S(2)}, u32[]{:S(2)}) async-start(f32[64,29,1,128]{3,2,1,0:T(1,128)} %bitcast.24), calls=%async_computation.1 | async-start | bytes 1900544 | tf_op jit(solution)/shard_map/all_to_all | solution.py:330
  90.4 1.0 %copy-start.4 = (f32[2,58,4,32]{1,3,2,0:T(8,128)S(1)}, f32[2,58,4,32]{1,3,2,0:T(8,128)}, u32[]{:S(2)}) copy-start(f32[2,58,4,32]{1,3,2,0:T(8,128)} %param.10) | copy-start | bytes 178180

commit v6 on v5

--- a/solution.py
+++ b/solution.py
@@ -58,10 +58,18 @@
     return jnp.concatenate([heat, gap, moist, gap], axis=1)
 
 
-def bucket_kernel(migrate, state, early, late):
+def bucket_kernel(migrate, state, batch, moves, steps, early, late, index):
+    new = moves[...]
+    group = jnp.floor((new.astype(F32) + 0.5) * (1.0 / COLS))
+    place = (new & (SLOTS - 1)).astype(F32) + 1.0
+    lane = iota((SLOTS, 2 * HALF), 1)
+    columns = jnp.zeros((SLOTS, 2 * HALF), F32)
+    for i, row in enumerate((batch[...].astype(F32), place, steps[...].astype(F32), group)):
+        columns = jnp.where(lane == i, to_column(row), columns)
+    index[...] = columns
     for s in range(SLOTS):
         group = lax.div(migrate[s], COLS)
-        early[pl.ds(group * EARLY, EARLY), :] = state[pl.ds(s, EARLY, stride=SLOTS), :]
+        early[pl.ds(pl.multiple_of(group * EARLY, 8), EARLY), :] = state[pl.ds(s, EARLY, stride=SLOTS), :]
         late[pl.ds(group * SENT, LATE), :] = state[pl.ds(EARLY * SLOTS + s, LATE, stride=SLOTS), :]
 
 
@@ -114,7 +122,7 @@
     payload[...] = jnp.concatenate([forcing] + left + right, axis=0)
 
 
-def forcing_kernel(gathered, batch, migrate, steps, late, force, edge, filled):
+def forcing_kernel(gathered, index, late, force, edge, filled):
     rows = []
     for d in range(N_MEM):
         right = gathered[d, SLOTS + ROWS : SLOTS + 2 * ROWS, :]
@@ -124,25 +132,21 @@
     joined = jnp.concatenate(rows, axis=0)
     edge[...] = joined
     columns = gathered[:, :SLOTS, :].reshape(COLS, 2 * HALF)
-    slot = batch[...]
-    pick = jnp.where(iota((COLS, SLOTS), 0) == slot, 1.0, 0.0).astype(F32)
-    e = iota((N_MEM * ROWS, SLOTS), 0)
+    slot = index[:, 0:1].astype(jnp.int32)
+    pick = jnp.where(iota((SLOTS, COLS), 1) == slot, 1.0, 0.0).astype(F32)
+    e = iota((SLOTS, N_MEM * ROWS), 1)
     dev, half = e // ROWS, (e % ROWS) // 2
     ahead = jnp.where(dev == N_MEM - 1, 0, dev + 1)
     last = slot == dev * SLOTS + half * 16 + 15
     first = slot == ahead * SLOTS + half * 16
     pick_edge = jnp.where(last, 0.25, 0.0) + jnp.where(first, 0.25, 0.0)
-    forced = dot_t(pick, columns) + dot_t(pick_edge, joined)
-    new = migrate[...]
-    place = to_column((new & (SLOTS - 1)).astype(F32)) + 1.0
-    count = to_column(steps[...].astype(F32))
+    forced = dot(pick, columns) + dot(pick_edge, joined)
     lane = iota((SLOTS, 2 * HALF), 1)
-    forced = jnp.where(lane == LEV, place, jnp.where(lane == LEV + 1, count, forced))
+    forced = jnp.where(lane == LEV, index[:, 1:2], jnp.where(lane == LEV + 1, index[:, 2:3], forced))
     force[...] = forced
-    group = jnp.floor((new.astype(F32) + 0.5) * (1.0 / COLS)).astype(jnp.int32)
-    goes = jnp.where(iota((N_GRP, SLOTS), 0) == group, 1.0, 0.0).astype(F32)
+    goes = jnp.where(iota((SLOTS, N_GRP), 1) == index[:, 3:4].astype(jnp.int32), 1.0, 0.0).astype(F32)
     filled[...] = late[...]
-    filled[pl.ds(LATE, N_GRP, stride=SENT), :] = dot(goes, forced)
+    filled[pl.ds(LATE, N_GRP, stride=SENT), :] = dot_t(goes, forced)
 
 
 def neighbours_table():
@@ -168,7 +172,7 @@
     return jnp.concatenate([lead, trail], axis=1)
 
 
-EARLY = 30
+EARLY = 32
 LATE = LEV - EARLY
 SENT = LATE + 1
 CHUNKS = [(0, 8), (8, 8), (16, 8), (24, 8), (32, 8), (40, 8), (48, 8), (56, 2)]
@@ -233,7 +237,7 @@
     run_cloud(state, force, table, middle, keep)
 
 
-def arrive_kernel(early, late, table, out, held, middle, force, row, origin, done):
+def arrive_kernel(early, late, table, out, held, middle, stepped_at, force, row, origin, done, written):
     last = late[pl.ds(LATE, N_GRP, stride=SENT), :]
     slot = (iota((N_GRP, SLOTS), 1) + 1).astype(F32)
     pick = jnp.where(last[:, LEV : LEV + 1] == slot, 1.0, 0.0).astype(F32)
@@ -245,13 +249,20 @@
     copy.wait()
     for j in range(SLOTS):
         g = origin[0, j]
-        held[pl.ds(j, EARLY, stride=SLOTS), :] = early[pl.ds(g * EARLY, EARLY), :]
+        held[pl.ds(j, EARLY, stride=SLOTS), :] = early[pl.ds(pl.multiple_of(g * EARLY, 8), EARLY), :]
         held[pl.ds(EARLY * SLOTS + j, LATE, stride=SLOTS), :] = late[pl.ds(g * SENT, LATE), :]
 
+    copies = []
+
     def keep(first, count, stepped):
-        out[first * SLOTS : (first + count) * SLOTS, :] = stepped
+        rows = pl.ds(first * SLOTS, count * SLOTS)
+        stepped_at[rows, :] = stepped
+        copies.append(pltpu.make_async_copy(stepped_at.at[rows], out.at[rows], written.at[len(copies)]))
+        copies[-1].start()
 
     run_cloud(held, force, table, middle, keep)
+    for copy in copies:
+        copy.wait()
 
 
 def next_kernel(dyn, inner, edge, out):
@@ -307,10 +318,10 @@
         [(2, ROWS, POINTS, LEV), (ROWS, POINTS, LEV), (ROWS, POINTS), table.shape, ints, dma((5,))],
         limit=60,
     )(dyn, wind, mass_weight, table, batch)
-    weighed, state_later = lax.optimization_barrier((weighed, state))
-    early, late = call(bucket_kernel, [(N_GRP * EARLY, lanes), (N_GRP * SENT, lanes)], [SMEM, VMEM])(
-        migrate_to, state_later
-    )
+    weighed, batch_later = lax.optimization_barrier((weighed, batch))
+    early, late, index = call(
+        bucket_kernel, [(N_GRP * EARLY, lanes), (N_GRP * SENT, lanes), (SLOTS, lanes)], [SMEM] + [VMEM] * 4
+    )(migrate_to, state, batch_later, moves, steps)
     up = [(i, (i + 1) % N_GRP) for i in range(N_GRP)]
     down = [(j, i) for i, j in up]
     before = lax.ppermute(end, "grp", up)
@@ -324,8 +335,8 @@
     force, edge, filled = call(
         forcing_kernel,
         [(SLOTS, lanes), (N_MEM * ROWS, lanes), (N_GRP * SENT, lanes)],
-        [VMEM] * 5,
-    )(gathered, batch, moves, steps, late)
+        [VMEM] * 3,
+    )(gathered, index, late)
     filled, first = lax.optimization_barrier((filled, first))
     second = lax.all_to_all(filled.reshape(N_GRP, SENT, 1, lanes), "grp", 0, 0, tiled=True)
     mix, means = jnp.asarray(neighbours_table()), jnp.asarray(means_table())
@@ -337,8 +348,9 @@
         arrive_kernel,
         (cells, lanes),
         [VMEM] * 3,
-        [(cells, lanes)] * 2
-        + [(SLOTS, lanes), ints, pltpu.SMEM((1, SLOTS), jnp.int32), dma],
+        [(cells, lanes)] * 3
+        + [(SLOTS, lanes), ints, pltpu.SMEM((1, SLOTS), jnp.int32), dma, dma((len(CHUNKS),))],
+        HBM,
     )(first.reshape(N_GRP * EARLY, lanes), second.reshape(N_GRP * SENT, lanes), mix)
     crm_next = new.reshape(LEV, SLOTS, lanes).transpose(1, 0, 2)
     return (dyn_next.transpose(0, 3, 1, 2), phys.transpose(0, 2, 1), crm_next)

time: 101 us -> 99.5 us (0.985)
  starting transfers between devices: 38 us -> 36 us
  blocking collectives: 41.3 us -> 42.6 us
    all_to_all x1, waiting for transfers between devices: 4.96 us -> 2.36 us  [on_device(): lax.all_to_all(filled.reshape(N_GRP, SENT, 1, lanes), 'grp', 0, 0, tiled=...]
    all_to_all x1, waiting for transfers between devices: 0.27 us -> 2.29 us  [on_device(): lax.all_to_all(early.reshape(N_GRP, EARLY, 1, lanes), 'grp', 0, 0, tiled=...]
    all_to_all x1, starting transfers between devices: 13.9 us -> 11.9 us  [on_device(): lax.all_to_all(filled.reshape(N_GRP, SENT, 1, lanes), 'grp', 0, 0, tiled=...]
    all_gather x1, blocking collectives: 17.3 us -> 18.6 us  [on_device(): tendencies = lax.all_gather(tendency, 'mem', axis=0, tiled=True)]
  transfers between devices with their start and end apart: 4 -> 4, of which waited for: 2 -> 2; matrix products, arithmetic and copies ran while one was open for 0% -> 0% of each run, Pallas kernels for 6% -> 7%
where the time goes in v6:
time: 99.5 us; the launch traced here: 98.8 us
  blocking collectives  42.6 us (43%)
  starting transfers between devices  36 us (36%)
  Pallas kernels  12.1 us (12%)
  waiting for transfers between devices  4.65 us (5%)
  local copies, waits for them, and re-layouts  2.79 us (3%)
    all_gather x1, blocking collectives, on_device(): gathered = lax.all_gather(payload, 'mem', axis=0)  24 us
    all_gather x1, blocking collectives, on_device(): tendencies = lax.all_gather(tendency, 'mem', axis=0, tiled=True)  18.6 us
    all_to_all x1, starting transfers between devices, on_device(): lax.all_to_all(filled.reshape(N_GRP, SENT, 1, lanes), 'grp', 0, 0, tiled=...  11.9 us
    ppermute x1, starting transfers between devices, on_device(): after = lax.ppermute(top, 'grp', down)  9.84 us
    all_to_all x1, starting transfers between devices, on_device(): lax.all_to_all(early.reshape(N_GRP, EARLY, 1, lanes), 'grp', 0, 0, tiled=...  9.72 us
    ppermute x1, starting transfers between devices, on_device(): before = lax.ppermute(end, 'grp', up)  4.51 us
    pallas_call x1, Pallas kernels, on_device(): call(arrive_kernel, (cells, lanes), [VMEM] * 3, [(cells, lanes)] * 3 + [(...  3.64 us
    unnamed x20, local copies, waits for them, and re-layouts  2.79 us
  transfers between devices with their start and end apart: 4, of which 2 were waited for; matrix products, arithmetic and copies ran while one was open for 0% of the time, Pallas kernels for 7%

profile of v6, /device:TPU:1, one launch (start us, length us, event | category | flops | bytes accessed | tf_op | source)
XLA Modules:
  0.0 98.8 jit_solution(317835959737959339)
XLA Ops:
  0.6 1.9 %shard_map.121 = (f32[4,32,128]{2,1,0:T(8,128)}, f32[1,32,128]{2,1,0:T(8,128)}, f32[1,32,128]{2,1,0:T(8,128)}) custom-call(f32[2,4,32,58]{3,2,1,0:T(8,128)} %bitcast.27, f32[4,32,58]{2,1,0:T(8,128)} %bitcast.35, f32[4,32]{1,0:T(4,128)} %mass_at.1, f32[128,128]{1,0:T(8,128)} %constant.6.clone.table_at, s32[1,32]{1,0:T(1,128)} %bitcast.29), custom_call_target="tpu_custom_call" | custom-call | tf_op jit(solution)/shard_map/pallas_call | solution.py:314
  2.5 4.5 %collective-permute-start = (f32[1,32,128]{2,1,0:T(8,128)}, f32[1,32,128]{2,1,0:T(8,128)S(1)}, u32[]{:S(2)}, u32[]{:S(2)}) collective-permute-start(f32[1,32,128]{2,1,0:T(8,128)} %get-tuple-element.25), channel_id=1, source_target_pairs={{0,12},{12,24},{24,36},{36,48},{48,60},{60,72},{72,84},{84,96},{96... | collective-permute-start | bytes 49160 | tf_op jit(solution)/shard_map/ppermute | solution.py:327
  7.1 9.8 %collective-permute-start.1 = (f32[1,32,128]{2,1,0:T(8,128)}, f32[1,32,128]{2,1,0:T(8,128)S(1)}, u32[]{:S(2)}, u32[]{:S(2)}) collective-permute-start(f32[1,32,128]{2,1,0:T(8,128)} %get-tuple-element.26), channel_id=1, source_target_pairs={{12,0},{24,12},{36,24},{48,36},{60,48},{72,60},{84,72},{96,84},{10... | collective-permute-start | bytes 49160 | tf_op jit(solution)/shard_map/ppermute | solution.py:328
  16.9 0.0 copy-start.7
  16.9 0.0 copy-start.8
  16.9 0.0 copy-start.9
  16.9 0.6 copy-done.7
  17.6 0.0 copy-done.8
  17.6 0.0 copy-done.9
  17.6 0.0 copy-start
  17.6 1.2 %copy-done = f32[32,58,128]{2,0,1:T(8,128)S(1)} copy-done((f32[32,58,128]{2,0,1:T(8,128)S(1)}, f32[32,58,128]{2,0,1:T(8,128)}, u32[]{:S(2)}) %copy-start) | copy-done | bytes 950296
  18.8 2.1 %shard_map.122 = (f32[2048,128]{1,0:T(8,128)}, f32[1728,128]{1,0:T(8,128)S(1)}, f32[32,128]{1,0:T(8,128)S(1)}) custom-call(s32[32]{0:T(128)S(1)} %copy-done.8, f32[1856,128]{1,0:T(8,128)S(1)} %bitcast.21, s32[1,32]{1,0:T(1,128)S(1)} %bitcast.30, s32[1,32]{1,0:T(1,128)S(1)} %bitcast.31, s32[1,32]{1,0:T(1,128)S(1)} %bitcast.32), custom_call_target="tpu_custom_call" | custom-call | tf_op jit(solution)/shard_map/pallas_call | solution.py:322
  20.9 0.0 collective-permute-done.before
  20.9 0.0 collective-permute-done.1.after
  20.9 9.7 %all-to-all-start = ((f32[64,32,1,128]{3,1,2,0:T(8,128)}), f32[64,32,1,128]{3,1,2,0:T(8,128)S(1)}, u32[]{:S(2)}, u32[]{:S(2)}) async-start(f32[64,32,1,128]{3,1,2,0:T(8,128)} %bitcast.12), calls=%async_computation | async-start | bytes 2097152 | tf_op jit(solution)/shard_map/all_to_all | solution.py:330
  30.6 0.0 copy-done.6
  30.6 0.2 shard_map.123
  30.9 24.0 %all-gather = f32[480,128]{1,0:T(8,128)S(1)} all-gather(f32[40,128]{1,0:T(8,128)S(1)} %get-tuple-element.30), channel_id=2, replica_groups=mesh['grp'=64,'mem'=12] {'mem'}, dimensions={0}, use_global_device_ids=true | all-gather | bytes 266240 | tf_op jit(solution)/shard_map/all_gather | solution.py:334
  54.8 0.5 shard_map.124
  55.4 0.9 copy-done.2
  56.3 2.3 %all-to-all-done = f32[64,32,1,128]{3,1,2,0:T(8,128)S(1)} async-done(((f32[64,32,1,128]{3,1,2,0:T(8,128)}), f32[64,32,1,128]{3,1,2,0:T(8,128)S(1)}, u32[]{:S(2)}, u32[]{:S(2)}) %all-to-all-start) | async-done | bytes 1048608 | tf_op jit(solution)/shard_map/all_to_all | solution.py:330
  58.6 11.9 %all-to-all-start.1 = ((f32[64,27,1,128]{3,2,1,0:T(1,128)}), f32[64,27,1,128]{3,2,1,0:T(1,128)S(1)}, u32[]{:S(2)}, u32[]{:S(2)}) async-start(f32[64,27,1,128]{3,2,1,0:T(1,128)} %bitcast.26), calls=%async_computation.1 | async-start | bytes 1769472 | tf_op jit(solution)/shard_map/all_to_all | solution.py:341
  70.5 0.0 copy-done.1
  70.5 0.0 copy-done.3
  70.5 0.0 copy-done.5
  70.5 1.9 %shard_map.126 = f32[32,128]{1,0:T(8,128)S(1)} custom-call(f32[1856,128]{1,0:T(8,128)S(1)} %bitcast.22, f32[32,128]{1,0:T(8,128)S(1)} %get-tuple-element.34.force, bf16[256,256]{1,0:T(8,128)(2,1)S(1)} %copy-done.3, bf16[256,128]{1,0:T(8,128)(2,1)S(1)} %copy-done.5), custom_call_target="tpu_custom_call" | custom-call | tf_op jit(solution)/shard_map/pallas_call | solution.py:343
  72.4 18.6 %all_gather.11.tendency = f32[384,128]{1,0:T(8,128)S(1)} all-gather(f32[32,128]{1,0:T(8,128)S(1)} %shard_map.126), channel_id=1, replica_groups=mesh['grp'=64,'mem'=12] {'mem'}, dimensions={0}, use_global_device_ids=true | all-gather | bytes 212992 | tf_op jit(solution)/shard_map/all_gather | solution.py:344
  91.0 1.0 %shard_map.127 = f32[2,32,58]{2,1,0:T(8,128)} custom-call(f32[384,128]{1,0:T(8,128)S(1)} %all_gather.11.tendency, f32[12,40,128]{2,1,0:T(8,128)S(1)} %bitcast.25), custom_call_target="tpu_custom_call" | custom-call | tf_op jit(solution)/shard_map/pallas_call | solution.py:346
  92.0 0.0 copy-done.4
  92.0 0.8 shard_map.125
  92.8 2.4 %all-to-all-done.1 = f32[64,27,1,128]{3,2,1,0:T(1,128)S(1)} async-done(((f32[64,27,1,128]{3,2,1,0:T(1,128)}), f32[64,27,1,128]{3,2,1,0:T(1,128)S(1)}, u32[]{:S(2)}, u32[]{:S(2)}) %all-to-all-start.1) | async-done | bytes 884768 | tf_op jit(solution)/shard_map/all_to_all | solution.py:341
  95.1 3.6 %shard_map.128 = f32[1856,128]{1,0:T(8,128)} custom-call(f32[2048,128]{1,0:T(8,128)S(1)} %bitcast.20, f32[1728,128]{1,0:T(8,128)S(1)} %bitcast.23, bf16[256,256]{1,0:T(8,128)(2,1)S(1)} %copy-done.3), custom_call_target="tpu_custom_call" | custom-call | tf_op jit(solution)/shard_map/pallas_call | solution.py:347
  (6 shorter events, 0.0 us)
Async XLA Ops:
  2.5 18.3 %collective-permute-start = (f32[1,32,128]{2,1,0:T(8,128)}, f32[1,32,128]{2,1,0:T(8,128)S(1)}, u32[]{:S(2)}, u32[]{:S(2)}) collective-permute-start(f32[1,32,128]{2,1,0:T(8,128)} %get-tuple-element.25), channel_id=1, source_target_pairs={{0,12},{12,24},{24,36},{36,48},{48,60},{60,72},{72,84},{84,96},{96... | collective-permute-start | bytes 49160 | tf_op jit(solution)/shard_map/ppermute | solution.py:327
  7.1 13.8 %collective-permute-start.1 = (f32[1,32,128]{2,1,0:T(8,128)}, f32[1,32,128]{2,1,0:T(8,128)S(1)}, u32[]{:S(2)}, u32[]{:S(2)}) collective-permute-start(f32[1,32,128]{2,1,0:T(8,128)} %get-tuple-element.26), channel_id=1, source_target_pairs={{12,0},{24,12},{36,24},{48,36},{60,48},{72,60},{84,72},{96,84},{10... | collective-permute-start | bytes 49160 | tf_op jit(solution)/shard_map/ppermute | solution.py:328
  16.9 0.7 copy-start.7
  16.9 0.7 copy-start.8
  16.9 0.7 copy-start.9
  17.6 1.2 %copy-start = (f32[32,58,128]{2,0,1:T(8,128)S(1)}, f32[32,58,128]{2,0,1:T(8,128)}, u32[]{:S(2)}) copy-start(f32[32,58,128]{2,0,1:T(8,128)} %param.13) | copy-start | bytes 2850820
  20.9 9.7 %copy-start.6 = (f32[4,32,128]{2,1,0:T(8,128)S(1)}, f32[4,32,128]{2,1,0:T(8,128)}, u32[]{:S(2)}) copy-start(f32[4,32,128]{2,1,0:T(8,128)} %get-tuple-element.22.own) | copy-start | bytes 196612
  20.9 37.7 %all-to-all-start = ((f32[64,32,1,128]{3,1,2,0:T(8,128)}), f32[64,32,1,128]{3,1,2,0:T(8,128)S(1)}, u32[]{:S(2)}, u32[]{:S(2)}) async-start(f32[64,32,1,128]{3,1,2,0:T(8,128)} %bitcast.12), calls=%async_computation | async-start | bytes 2097152 | tf_op jit(solution)/shard_map/all_to_all | solution.py:330
  55.4 0.9 copy-start.2
  56.3 14.2 %copy-start.1 = (f32[32,58,128]{2,0,1:T(8,128)S(1)}, f32[32,58,128]{2,0,1:T(8,128)}, u32[]{:S(2)}) copy-start(f32[32,58,128]{2,0,1:T(8,128)} %param.13) | copy-start | bytes 2850820
  58.6 11.9 %copy-start.3 = (bf16[256,256]{1,0:T(8,128)(2,1)S(1)}, bf16[256,256]{1,0:T(8,128)(2,1)}, u32[]{:S(2)}) copy-start(bf16[256,256]{1,0:T(8,128)(2,1)} %constant.7.clone.table) | copy-start | bytes 393220
  58.6 11.9 %copy-start.5 = (bf16[256,128]{1,0:T(8,128)(2,1)S(1)}, bf16[256,128]{1,0:T(8,128)(2,1)}, u32[]{:S(2)}) copy-start(bf16[256,128]{1,0:T(8,128)(2,1)} %constant.8.clone.means) | copy-start | bytes 196612
  58.6 36.5 %all-to-all-start.1 = ((f32[64,27,1,128]{3,2,1,0:T(1,128)}), f32[64,27,1,128]{3,2,1,0:T(1,128)S(1)}, u32[]{:S(2)}, u32[]{:S(2)}) async-start(f32[64,27,1,128]{3,2,1,0:T(1,128)} %bitcast.26), calls=%async_computation.1 | async-start | bytes 1769472 | tf_op jit(solution)/shard_map/all_to_all | solution.py:341
  91.0 1.0 %copy-start.4 = (f32[2,58,4,32]{1,3,2,0:T(8,128)S(1)}, f32[2,58,4,32]{1,3,2,0:T(8,128)}, u32[]{:S(2)}) copy-start(f32[2,58,4,32]{1,3,2,0:T(8,128)} %param.10) | copy-start | bytes 178180

commit v7 on v6

--- a/solution.py
+++ b/solution.py
@@ -58,7 +58,7 @@
     return jnp.concatenate([heat, gap, moist, gap], axis=1)
 
 
-def bucket_kernel(migrate, state, batch, moves, steps, early, late, index):
+def index_columns(batch, moves, steps):
     new = moves[...]
     group = jnp.floor((new.astype(F32) + 0.5) * (1.0 / COLS))
     place = (new & (SLOTS - 1)).astype(F32) + 1.0
@@ -66,20 +66,29 @@
     columns = jnp.zeros((SLOTS, 2 * HALF), F32)
     for i, row in enumerate((batch[...].astype(F32), place, steps[...].astype(F32), group)):
         columns = jnp.where(lane == i, to_column(row), columns)
-    index[...] = columns
-    for s in range(SLOTS):
-        group = lax.div(migrate[s], COLS)
-        early[pl.ds(pl.multiple_of(group * EARLY, 8), EARLY), :] = state[pl.ds(s, EARLY, stride=SLOTS), :]
-        late[pl.ds(group * SENT, LATE), :] = state[pl.ds(EARLY * SLOTS + s, LATE, stride=SLOTS), :]
-
-
-def weigh_kernel(dyn_at, wind_at, mass_at, table_at, batch_at, out, top, end, dyn, wind, mass, table, batch, done):
-    pairs = [(dyn_at, dyn), (wind_at, wind), (mass_at, mass), (table_at, table), (batch_at, batch)]
-    copies = [pltpu.make_async_copy(a, b, done.at[i]) for i, (a, b) in enumerate(pairs)]
+    return columns
+
+
+def first_kernel(*refs):
+    given, (out, top, end, index, early_at, late_at) = refs[:9], refs[9:15]
+    state, migrate, dyn, wind, mass, table, batch, moves, steps, early, late, done, sent = refs[15:]
+    held = (state, migrate, dyn, wind, mass, table, batch, moves, steps)
+    copies = [pltpu.make_async_copy(a, b, done.at[i]) for i, (a, b) in enumerate(zip(given, held))]
     for copy in copies:
         copy.start()
     for copy in copies:
         copy.wait()
+    for s in range(SLOTS):
+        group = lax.div(migrate[0, s], COLS)
+        early[pl.ds(pl.multiple_of(group * EARLY, 8), EARLY), :] = state[pl.ds(s, EARLY, stride=SLOTS), :]
+        late[pl.ds(group * SENT, LATE), :] = state[pl.ds(EARLY * SLOTS + s, LATE, stride=SLOTS), :]
+    leaving = [
+        pltpu.make_async_copy(early, early_at, sent.at[0]),
+        pltpu.make_async_copy(late, late_at, sent.at[1]),
+    ]
+    for copy in leaving:
+        copy.start()
+    index[...] = index_columns(batch, moves, steps)
     field = both_kinds(dyn[0].reshape(ROWS * POINTS, LEV), dyn[1].reshape(ROWS * POINTS, LEV))
     blow = wind[...].reshape(ROWS * POINTS, LEV)
     slope = dot(table[...], field)
@@ -93,6 +102,8 @@
     out[...] = weighed
     top[0] = weighed[0]
     end[0] = weighed[ROWS - 1]
+    for copy in leaving:
+        copy.wait()
 
 
 def assemble_kernel(own, before, after, inner, payload):
@@ -311,17 +322,17 @@
     cells = LEV * SLOTS
     dma = pltpu.SemaphoreType.DMA
     ints = pltpu.VMEM((1, SLOTS), jnp.int32)
-    weighed, top, end = call(
-        weigh_kernel,
-        [(ROWS, POINTS, lanes), (1, POINTS, lanes), (1, POINTS, lanes)],
-        [HBM] * 5,
-        [(2, ROWS, POINTS, LEV), (ROWS, POINTS, LEV), (ROWS, POINTS), table.shape, ints, dma((5,))],
+    weighed, top, end, index, early, late = call(
+        first_kernel,
+        [(ROWS, POINTS, lanes), (1, POINTS, lanes), (1, POINTS, lanes), (SLOTS, lanes)]
+        + [(N_GRP * EARLY, lanes), (N_GRP * SENT, lanes)],
+        [HBM] * 9,
+        [(cells, lanes), pltpu.SMEM((1, SLOTS), jnp.int32)]
+        + [(2, ROWS, POINTS, LEV), (ROWS, POINTS, LEV), (ROWS, POINTS), table.shape, ints, ints, ints]
+        + [(N_GRP * EARLY, lanes), (N_GRP * SENT, lanes), dma((9,)), dma((2,))],
+        [VMEM] * 4 + [HBM] * 2,
         limit=60,
-    )(dyn, wind, mass_weight, table, batch)
-    weighed, batch_later = lax.optimization_barrier((weighed, batch))
-    early, late, index = call(
-        bucket_kernel, [(N_GRP * EARLY, lanes), (N_GRP * SENT, lanes), (SLOTS, lanes)], [SMEM] + [VMEM] * 4
-    )(migrate_to, state, batch_later, moves, steps)
+    )(state, moves, dyn, wind, mass_weight, table, batch, moves, steps)
     up = [(i, (i + 1) % N_GRP) for i in range(N_GRP)]
     down = [(j, i) for i, j in up]
     before = lax.ppermute(end, "grp", up)

time: 99.5 us -> 101 us (1.015)
  starting transfers between devices: 36 us -> 39 us
  local copies, waits for them, and re-layouts: 2.79 us -> 0.94 us
    all_to_all x1, starting transfers between devices: 9.72 us -> 12.7 us  [on_device(): lax.all_to_all(early.reshape(N_GRP, EARLY, 1, lanes), 'grp', 0, 0, tiled=...]
    unnamed x20 -> x16, local copies, waits for them, and re-layouts: 2.79 us -> 0.94 us
    ppermute x1, waiting for transfers between devices: 0.01 us -> 1.02 us  [on_device(): after = lax.ppermute(top, 'grp', down)]
    pallas_call x2 -> x1, Pallas kernels: 3.98 us -> 3.75 us  [on_device(): call(first_kernel, [(ROWS, POINTS, lanes), (1, POINTS, lanes), (1, POINTS...]
  transfers between devices with their start and end apart: 4 -> 4, of which waited for: 2 -> 3; matrix products, arithmetic and copies ran while one was open for 0% -> 0% of each run, Pallas kernels for 7% -> 5%
where the time goes in v7:
time: 101 us
  blocking collectives  42.5 us (42%)
  starting transfers between devices  39 us (39%)
  Pallas kernels  12 us (12%)
  waiting for transfers between devices  5.63 us (6%)
    all_gather x1, blocking collectives, on_device(): gathered = lax.all_gather(payload, 'mem', axis=0)  24.1 us
    all_gather x1, blocking collectives, on_device(): tendencies = lax.all_gather(tendency, 'mem', axis=0, tiled=True)  18.3 us
    all_to_all x1, starting transfers between devices, on_device(): lax.all_to_all(early.reshape(N_GRP, EARLY, 1, lanes), 'grp', 0, 0, tiled=...  12.7 us
    all_to_all x1, starting transfers between devices, on_device(): lax.all_to_all(filled.reshape(N_GRP, SENT, 1, lanes), 'grp', 0, 0, tiled=...  12 us
    ppermute x1, starting transfers between devices, on_device(): after = lax.ppermute(top, 'grp', down)  9.84 us
    ppermute x1, starting transfers between devices, on_device(): before = lax.ppermute(end, 'grp', up)  4.51 us
    pallas_call x1, Pallas kernels, on_device(): call(first_kernel, [(ROWS, POINTS, lanes), (1, POINTS, lanes), (1, POINTS...  3.75 us
    pallas_call x1, Pallas kernels, on_device(): call(arrive_kernel, (cells, lanes), [VMEM] * 3, [(cells, lanes)] * 3 + [(...  3.67 us
  transfers between devices with their start and end apart: 4, of which 3 were waited for; matrix products, arithmetic and copies ran while one was open for 0% of the time, Pallas kernels for 5%

profile of v7, /device:TPU:1, one launch (start us, length us, event | category | flops | bytes accessed | tf_op | source)
XLA Modules:
  0.0 100.8 jit_solution(7696010923374840984)
XLA Ops:
  0.6 3.7 %shard_map.121 = (f32[4,32,128]{2,1,0:T(8,128)}, f32[1,32,128]{2,1,0:T(8,128)}, f32[1,32,128]{2,1,0:T(8,128)}, f32[32,128]{1,0:T(8,128)}, f32[2048,128]{1,0:T(8,128)}, /*index=5*/f32[1728,128]{1,0:T(8,128)}) custom-call(f32[1856,128]{1,0:T(8,128)} %bitcast.21, s32[1,32]{1,0:T(1,128)} %bitcast.34, f32[2,4,32,58]{3,2,1,0:T(8,128)} %bitcast.27, ...), custom_call_target="tpu_custom_call" | custom-call | tf_op jit(solution)/shard_map/pallas_call | solution.py:325
  4.4 4.5 %collective-permute-start = (f32[1,32,128]{2,1,0:T(8,128)}, f32[1,32,128]{2,1,0:T(8,128)S(1)}, u32[]{:S(2)}, u32[]{:S(2)}) collective-permute-start(f32[1,32,128]{2,1,0:T(8,128)} %get-tuple-element.21), channel_id=1, source_target_pairs={{0,12},{12,24},{24,36},{36,48},{48,60},{60,72},{72,84},{84,96},{96... | collective-permute-start | bytes 49160 | tf_op jit(solution)/shard_map/ppermute | solution.py:338
  8.9 9.8 %collective-permute-start.1 = (f32[1,32,128]{2,1,0:T(8,128)}, f32[1,32,128]{2,1,0:T(8,128)S(1)}, u32[]{:S(2)}, u32[]{:S(2)}) collective-permute-start(f32[1,32,128]{2,1,0:T(8,128)} %get-tuple-element.22), channel_id=1, source_target_pairs={{12,0},{24,12},{36,24},{48,36},{60,48},{72,60},{84,72},{96,84},{10... | collective-permute-start | bytes 49160 | tf_op jit(solution)/shard_map/ppermute | solution.py:339
  18.7 0.0 collective-permute-done.before
  18.8 1.0 %collective-permute-done.1.after = f32[1,32,128]{2,1,0:T(8,128)S(1)} collective-permute-done((f32[1,32,128]{2,1,0:T(8,128)}, f32[1,32,128]{2,1,0:T(8,128)S(1)}, u32[]{:S(2)}, u32[]{:S(2)}) %collective-permute-start.1) | collective-permute-done | bytes 16416 | tf_op jit(solution)/shard_map/ppermute | solution.py:339
  19.8 0.0 copy-start.6
  19.8 0.0 copy-start.2
  19.8 12.7 %all-to-all-start = ((f32[64,32,1,128]{3,1,2,0:T(8,128)}), f32[64,32,1,128]{3,1,2,0:T(8,128)S(1)}, u32[]{:S(2)}, u32[]{:S(2)}) async-start(f32[64,32,1,128]{3,1,2,0:T(8,128)} %bitcast.29), calls=%async_computation | async-start | bytes 2097152 | tf_op jit(solution)/shard_map/all_to_all | solution.py:341
  32.4 0.0 copy-done.6
  32.5 0.2 shard_map.122
  32.7 0.0 copy-start.7
  32.7 24.1 %all-gather = f32[480,128]{1,0:T(8,128)S(1)} all-gather(f32[40,128]{1,0:T(8,128)S(1)} %get-tuple-element.26), channel_id=2, replica_groups=mesh['grp'=64,'mem'=12] {'mem'}, dimensions={0}, use_global_device_ids=true | all-gather | bytes 266240 | tf_op jit(solution)/shard_map/all_gather | solution.py:345
  56.8 0.0 copy-done.2
  56.8 0.0 copy-done.7
  56.8 0.5 shard_map.123
  57.4 0.0 copy-start.1
  57.4 0.9 copy-done.1
  58.3 0.0 copy-start
  58.3 2.1 %all-to-all-done = f32[64,32,1,128]{3,1,2,0:T(8,128)S(1)} async-done(((f32[64,32,1,128]{3,1,2,0:T(8,128)}), f32[64,32,1,128]{3,1,2,0:T(8,128)S(1)}, u32[]{:S(2)}, u32[]{:S(2)}) %all-to-all-start) | async-done | bytes 1048608 | tf_op jit(solution)/shard_map/all_to_all | solution.py:341
  60.4 0.0 copy-start.3
  60.4 0.0 copy-start.5
  60.4 12.0 %all-to-all-start.1 = ((f32[64,27,1,128]{3,2,1,0:T(1,128)}), f32[64,27,1,128]{3,2,1,0:T(1,128)S(1)}, u32[]{:S(2)}, u32[]{:S(2)}) async-start(f32[64,27,1,128]{3,2,1,0:T(1,128)} %bitcast.26), calls=%async_computation.1 | async-start | bytes 1769472 | tf_op jit(solution)/shard_map/all_to_all | solution.py:352
  72.5 0.0 copy-done
  72.5 0.0 copy-done.3
  72.5 0.0 copy-done.5
  72.5 2.0 %shard_map.125 = f32[32,128]{1,0:T(8,128)S(1)} custom-call(f32[1856,128]{1,0:T(8,128)S(1)} %bitcast.22, f32[32,128]{1,0:T(8,128)S(1)} %get-tuple-element.30.force, bf16[256,256]{1,0:T(8,128)(2,1)S(1)} %copy-done.3, bf16[256,128]{1,0:T(8,128)(2,1)S(1)} %copy-done.5), custom_call_target="tpu_custom_call" | custom-call | tf_op jit(solution)/shard_map/pallas_call | solution.py:354
  74.5 18.3 %all_gather.11.tendency = f32[384,128]{1,0:T(8,128)S(1)} all-gather(f32[32,128]{1,0:T(8,128)S(1)} %shard_map.125), channel_id=1, replica_groups=mesh['grp'=64,'mem'=12] {'mem'}, dimensions={0}, use_global_device_ids=true | all-gather | bytes 212992 | tf_op jit(solution)/shard_map/all_gather | solution.py:355
  92.9 1.0 %shard_map.126 = f32[2,32,58]{2,1,0:T(8,128)} custom-call(f32[384,128]{1,0:T(8,128)S(1)} %all_gather.11.tendency, f32[12,40,128]{2,1,0:T(8,128)S(1)} %bitcast.25), custom_call_target="tpu_custom_call" | custom-call | tf_op jit(solution)/shard_map/pallas_call | solution.py:357
  93.9 0.0 copy-done.4
  93.9 0.8 shard_map.124
  94.7 2.5 %all-to-all-done.1 = f32[64,27,1,128]{3,2,1,0:T(1,128)S(1)} async-done(((f32[64,27,1,128]{3,2,1,0:T(1,128)}), f32[64,27,1,128]{3,2,1,0:T(1,128)S(1)}, u32[]{:S(2)}, u32[]{:S(2)}) %all-to-all-start.1) | async-done | bytes 884768 | tf_op jit(solution)/shard_map/all_to_all | solution.py:352
  97.1 3.7 %shard_map.127 = f32[1856,128]{1,0:T(8,128)} custom-call(f32[2048,128]{1,0:T(8,128)S(1)} %bitcast.20, f32[1728,128]{1,0:T(8,128)S(1)} %bitcast.23, bf16[256,256]{1,0:T(8,128)(2,1)S(1)} %copy-done.3), custom_call_target="tpu_custom_call" | custom-call | tf_op jit(solution)/shard_map/pallas_call | solution.py:358
  (1 shorter events, 0.0 us)
Async XLA Ops:
  4.4 14.4 %collective-permute-start = (f32[1,32,128]{2,1,0:T(8,128)}, f32[1,32,128]{2,1,0:T(8,128)S(1)}, u32[]{:S(2)}, u32[]{:S(2)}) collective-permute-start(f32[1,32,128]{2,1,0:T(8,128)} %get-tuple-element.21), channel_id=1, source_target_pairs={{0,12},{12,24},{24,36},{36,48},{48,60},{60,72},{72,84},{84,96},{96... | collective-permute-start | bytes 49160 | tf_op jit(solution)/shard_map/ppermute | solution.py:338
  8.9 10.9 %collective-permute-start.1 = (f32[1,32,128]{2,1,0:T(8,128)}, f32[1,32,128]{2,1,0:T(8,128)S(1)}, u32[]{:S(2)}, u32[]{:S(2)}) collective-permute-start(f32[1,32,128]{2,1,0:T(8,128)} %get-tuple-element.22), channel_id=1, source_target_pairs={{12,0},{24,12},{36,24},{48,36},{60,48},{72,60},{84,72},{96,84},{10... | collective-permute-start | bytes 49160 | tf_op jit(solution)/shard_map/ppermute | solution.py:339
  19.8 12.7 %copy-start.6 = (f32[4,32,128]{2,1,0:T(8,128)S(1)}, f32[4,32,128]{2,1,0:T(8,128)}, u32[]{:S(2)}) copy-start(f32[4,32,128]{2,1,0:T(8,128)} %get-tuple-element.19.own) | copy-start | bytes 196612
  19.8 37.0 %copy-start.2 = (f32[1728,128]{1,0:T(8,128)S(1)}, f32[1728,128]{1,0:T(8,128)}, u32[]{:S(2)}) copy-start(f32[1728,128]{1,0:T(8,128)} %get-tuple-element.28.late) | copy-start | bytes 2654212
  19.8 40.7 %all-to-all-start = ((f32[64,32,1,128]{3,1,2,0:T(8,128)}), f32[64,32,1,128]{3,1,2,0:T(8,128)S(1)}, u32[]{:S(2)}, u32[]{:S(2)}) async-start(f32[64,32,1,128]{3,1,2,0:T(8,128)} %bitcast.29), calls=%async_computation | async-start | bytes 2097152 | tf_op jit(solution)/shard_map/all_to_all | solution.py:341
  32.7 24.1 %copy-start.7 = (f32[32,128]{1,0:T(8,128)S(1)}, f32[32,128]{1,0:T(8,128)}, u32[]{:S(2)}) copy-start(f32[32,128]{1,0:T(8,128)} %get-tuple-element.27.index) | copy-start | bytes 49156
  57.4 0.9 copy-start.1
  58.3 14.2 %copy-start = (f32[32,58,128]{2,0,1:T(8,128)S(1)}, f32[32,58,128]{2,0,1:T(8,128)}, u32[]{:S(2)}) copy-start(f32[32,58,128]{2,0,1:T(8,128)} %param.13) | copy-start | bytes 2850820
  60.4 12.0 %copy-start.3 = (bf16[256,256]{1,0:T(8,128)(2,1)S(1)}, bf16[256,256]{1,0:T(8,128)(2,1)}, u32[]{:S(2)}) copy-start(bf16[256,256]{1,0:T(8,128)(2,1)} %constant.7.clone.table) | copy-start | bytes 393220
  60.4 12.1 %copy-start.5 = (bf16[256,128]{1,0:T(8,128)(2,1)S(1)}, bf16[256,128]{1,0:T(8,128)(2,1)}, u32[]{:S(2)}) copy-start(bf16[256,128]{1,0:T(8,128)(2,1)} %constant.8.clone.means) | copy-start | bytes 196612
  60.4 36.7 %all-to-all-start.1 = ((f32[64,27,1,128]{3,2,1,0:T(1,128)}), f32[64,27,1,128]{3,2,1,0:T(1,128)S(1)}, u32[]{:S(2)}, u32[]{:S(2)}) async-start(f32[64,27,1,128]{3,2,1,0:T(1,128)} %bitcast.26), calls=%async_computation.1 | async-start | bytes 1769472 | tf_op jit(solution)/shard_map/all_to_all | solution.py:352
  92.9 1.1 %copy-start.4 = (f32[2,58,4,32]{1,3,2,0:T(8,128)S(1)}, f32[2,58,4,32]{1,3,2,0:T(8,128)}, u32[]{:S(2)}) copy-start(f32[2,58,4,32]{1,3,2,0:T(8,128)} %param.10) | copy-start | bytes 178180

commit v8 on v6

--- a/solution.py
+++ b/solution.py
@@ -69,7 +69,7 @@
     index[...] = columns
     for s in range(SLOTS):
         group = lax.div(migrate[s], COLS)
-        early[pl.ds(pl.multiple_of(group * EARLY, 8), EARLY), :] = state[pl.ds(s, EARLY, stride=SLOTS), :]
+        early[pl.ds(group * EARLY, EARLY), :] = state[pl.ds(s, EARLY, stride=SLOTS), :]
         late[pl.ds(group * SENT, LATE), :] = state[pl.ds(EARLY * SLOTS + s, LATE, stride=SLOTS), :]
 
 
@@ -172,7 +172,7 @@
     return jnp.concatenate([lead, trail], axis=1)
 
 
-EARLY = 32
+EARLY = 34
 LATE = LEV - EARLY
 SENT = LATE + 1
 CHUNKS = [(0, 8), (8, 8), (16, 8), (24, 8), (32, 8), (40, 8), (48, 8), (56, 2)]
@@ -249,7 +249,7 @@
     copy.wait()
     for j in range(SLOTS):
         g = origin[0, j]
-        held[pl.ds(j, EARLY, stride=SLOTS), :] = early[pl.ds(pl.multiple_of(g * EARLY, 8), EARLY), :]
+        held[pl.ds(j, EARLY, stride=SLOTS), :] = early[pl.ds(g * EARLY, EARLY), :]
         held[pl.ds(EARLY * SLOTS + j, LATE, stride=SLOTS), :] = late[pl.ds(g * SENT, LATE), :]
 
     copies = []
@@ -265,8 +265,17 @@
         copy.wait()
 
 
-def next_kernel(dyn, inner, edge, out):
+def finish_kernel(tendency, gathered, dyn, inner, edge, phys, out):
     me = lax.axis_index("mem")
+    serves = gathered[:, :SLOTS, :].reshape(COLS, 2 * HALF)[:, LEV : LEV + 1]
+    column = (iota((COLS, SLOTS), 1) + me * SLOTS).astype(F32)
+    pick = jnp.where(serves == column, 1.0, 0.0).astype(jnp.bfloat16)
+    parts = lax.dot_general(
+        pick, two_parts(tendency[...]), (((0,), (0,)), ((), ())), preferred_element_type=F32
+    )
+    mine = parts[:, : 2 * HALF] + parts[:, 2 * HALF :]
+    phys[0] = mine[:, :LEV]
+    phys[1] = mine[:, HALF : HALF + LEV]
     behind = lax.rem(me + N_MEM - 1, N_MEM)
     for y in range(ROWS):
         point = iota((POINTS, 2 * HALF), 0)
@@ -275,15 +284,6 @@
         ratio = jnp.where(point == 0, left, jnp.where(point == POINTS - 1, right, inner[y]))
         out[0, y] = dyn[0, y] + 0.2 * ratio[:, :LEV]
         out[1, y] = dyn[1, y] + 0.2 * ratio[:, HALF : HALF + LEV]
-
-
-def column_kernel(tendency, gathered, out):
-    serves = gathered[:, :SLOTS, :].reshape(COLS, 2 * HALF)[:, LEV : LEV + 1]
-    column = (iota((COLS, SLOTS), 1) + lax.axis_index("mem") * SLOTS).astype(F32)
-    pick = jnp.where(serves == column, 1.0, 0.0).astype(F32)
-    mine = dot_t(pick, tendency[...])
-    out[0] = mine[:, :LEV]
-    out[1] = mine[:, HALF : HALF + LEV]
 
 
 def call(kernel, shapes, specs, scratch=(), out_specs=None, aliases=None, limit=24):
@@ -342,8 +342,9 @@
     mix, means = jnp.asarray(neighbours_table()), jnp.asarray(means_table())
     tendency = call(tendency_kernel, (SLOTS, lanes), [VMEM] * 4, [(cells, lanes)])(state, force, mix, means)
     tendencies = lax.all_gather(tendency, "mem", axis=0, tiled=True)
-    dyn_next = call(next_kernel, (2, ROWS, POINTS, LEV), [VMEM] * 3)(dyn, inner, edge)
-    phys = call(column_kernel, (2, SLOTS, LEV), [VMEM] * 2)(tendencies, gathered)
+    phys, dyn_next = call(
+        finish_kernel, [(2, SLOTS, LEV), (2, ROWS, POINTS, LEV)], [VMEM] * 5
+    )(tendencies, gathered, dyn, inner, edge)
     new = call(
         arrive_kernel,
         (cells, lanes),

time: 99.5 us -> 102 us (1.025)
  the two profiles are of different devices: /device:TPU:1 before, /device:TPU:2 now
where the time goes in v8:
time: 102 us
  blocking collectives  51.1 us (50%)
  starting transfers between devices  33.1 us (32%)
  Pallas kernels  11.3 us (11%)
  local copies, waits for them, and re-layouts  5.38 us (5%)
    all_gather x1, blocking collectives, on_device(): gathered = lax.all_gather(payload, 'mem', axis=0)  28.1 us
    all_gather x1, blocking collectives, on_device(): tendencies = lax.all_gather(tendency, 'mem', axis=0, tiled=True)  23 us
    all_to_all x1, starting transfers between devices, on_device(): lax.all_to_all(early.reshape(N_GRP, EARLY, 1, lanes), 'grp', 0, 0, tiled=...  17.1 us
    all_to_all x1, starting transfers between devices, on_device(): lax.all_to_all(filled.reshape(N_GRP, SENT, 1, lanes), 'grp', 0, 0, tiled=...  10.4 us
    unnamed x24, local copies, waits for them, and re-layouts  5.38 us
    pallas_call x1, Pallas kernels, on_device(): call(arrive_kernel, (cells, lanes), [VMEM] * 3, [(cells, lanes)] * 3 + [(...  3.64 us
    ppermute x1, starting transfers between devices, on_device(): after = lax.ppermute(top, 'grp', down)  3.64 us
    pallas_call x1, Pallas kernels, on_device(): call(bucket_kernel, [(N_GRP * EARLY, lanes), (N_GRP * SENT, lanes), (SLOT...  2.14 us
  transfers between devices with their start and end apart: 4, of which 0 were waited for; matrix products, arithmetic and copies ran while one was open for 0% of the time, Pallas kernels for 6%

profile of v8, /device:TPU:2, one launch (start us, length us, event | category | flops | bytes accessed | tf_op | source)
XLA Modules:
  0.0 101.7 jit_solution(4829426635716568592)
XLA Ops:
  0.6 1.9 %shard_map.121 = (f32[4,32,128]{2,1,0:T(8,128)}, f32[1,32,128]{2,1,0:T(8,128)}, f32[1,32,128]{2,1,0:T(8,128)}) custom-call(f32[2,4,32,58]{3,2,1,0:T(8,128)} %bitcast.25, f32[4,32,58]{2,1,0:T(8,128)} %bitcast.32, f32[4,32]{1,0:T(4,128)} %mass_at.1, f32[128,128]{1,0:T(8,128)} %constant.6.clone.table_at, s32[1,32]{1,0:T(1,128)} %bitcast.27), custom_call_target="tpu_custom_call" | custom-call | tf_op jit(solution)/shard_map/pallas_call | solution.py:314
  2.5 1.9 %collective-permute-start = (f32[1,32,128]{2,1,0:T(8,128)}, f32[1,32,128]{2,1,0:T(8,128)S(1)}, u32[]{:S(2)}, u32[]{:S(2)}) collective-permute-start(f32[1,32,128]{2,1,0:T(8,128)} %get-tuple-element.27), channel_id=1, source_target_pairs={{0,12},{12,24},{24,36},{36,48},{48,60},{60,72},{72,84},{84,96},{96... | collective-permute-start | bytes 49160 | tf_op jit(solution)/shard_map/ppermute | solution.py:327
  4.5 3.6 %collective-permute-start.1 = (f32[1,32,128]{2,1,0:T(8,128)}, f32[1,32,128]{2,1,0:T(8,128)S(1)}, u32[]{:S(2)}, u32[]{:S(2)}) collective-permute-start(f32[1,32,128]{2,1,0:T(8,128)} %get-tuple-element.28), channel_id=1, source_target_pairs={{12,0},{24,12},{36,24},{48,36},{60,48},{72,60},{84,72},{96,84},{10... | collective-permute-start | bytes 49160 | tf_op jit(solution)/shard_map/ppermute | solution.py:328
  8.1 0.0 copy-start
  8.1 1.2 %copy-done = f32[32,58,128]{2,0,1:T(8,128)S(1)} copy-done((f32[32,58,128]{2,0,1:T(8,128)S(1)}, f32[32,58,128]{2,0,1:T(8,128)}, u32[]{:S(2)}) %copy-start) | copy-done | bytes 950296
  9.3 0.0 copy-start.9
  9.3 0.7 copy-done.9
  10.0 0.7 copy-done.10
  10.6 0.7 copy-done.11
  11.3 2.1 %shard_map.122 = (f32[2176,128]{1,0:T(8,128)}, f32[1600,128]{1,0:T(8,128)S(1)}, f32[32,128]{1,0:T(8,128)S(1)}) custom-call(s32[32]{0:T(128)S(1)} %copy-done.10, f32[1856,128]{1,0:T(8,128)S(1)} %bitcast.19, s32[1,32]{1,0:T(1,128)S(1)} %bitcast.28, s32[1,32]{1,0:T(1,128)S(1)} %bitcast.29, s32[1,32]{1,0:T(1,128)S(1)} %bitcast.30), custom_call_target="tpu_custom_call" | custom-call | tf_op jit(solution)/shard_map/pallas_call | solution.py:322
  13.4 0.0 collective-permute-done.before
  13.4 0.0 collective-permute-done.1.after
  13.4 17.1 %all-to-all-start = ((f32[64,34,1,128]{3,2,1,0:T(1,128)}), f32[64,34,1,128]{3,2,1,0:T(1,128)S(1)}, u32[]{:S(2)}, u32[]{:S(2)}) async-start(f32[64,34,1,128]{3,2,1,0:T(1,128)} %bitcast.11), calls=%async_computation | async-start | bytes 2228224 | tf_op jit(solution)/shard_map/all_to_all | solution.py:330
  30.5 0.0 copy-done.6
  30.6 0.2 shard_map.123
  30.8 28.1 %all-gather = f32[480,128]{1,0:T(8,128)S(1)} all-gather(f32[40,128]{1,0:T(8,128)S(1)} %get-tuple-element.31), channel_id=2, replica_groups=mesh['grp'=64,'mem'=12] {'mem'}, dimensions={0}, use_global_device_ids=true | all-gather | bytes 266240 | tf_op jit(solution)/shard_map/all_gather | solution.py:334
  58.9 0.5 shard_map.124
  59.5 0.9 copy-done.2
  60.4 0.6 copy-done.7
  61.0 0.0 all-to-all-done
  61.0 10.4 %all-to-all-start.1 = ((f32[64,25,1,128]{3,2,1,0:T(1,128)}), f32[64,25,1,128]{3,2,1,0:T(1,128)S(1)}, u32[]{:S(2)}, u32[]{:S(2)}) async-start(f32[64,25,1,128]{3,2,1,0:T(1,128)} %bitcast.24), calls=%async_computation.1 | async-start | bytes 1638400 | tf_op jit(solution)/shard_map/all_to_all | solution.py:341
  71.4 0.0 copy-done.1
  71.4 0.0 copy-done.3
  71.4 0.0 copy-done.5
  71.4 0.0 copy-start.8
  71.4 0.7 copy-done.8
  72.2 1.9 %shard_map.125 = f32[32,128]{1,0:T(8,128)S(1)} custom-call(f32[1856,128]{1,0:T(8,128)S(1)} %bitcast.20, f32[32,128]{1,0:T(8,128)S(1)} %copy-done.8, bf16[256,256]{1,0:T(8,128)(2,1)S(1)} %copy-done.3, bf16[256,128]{1,0:T(8,128)(2,1)S(1)} %copy-done.5), custom_call_target="tpu_custom_call" | custom-call | tf_op jit(solution)/shard_map/pallas_call | solution.py:343
  74.0 23.0 %all_gather.11.tendency = f32[384,128]{1,0:T(8,128)S(1)} all-gather(f32[32,128]{1,0:T(8,128)S(1)} %shard_map.125), channel_id=1, replica_groups=mesh['grp'=64,'mem'=12] {'mem'}, dimensions={0}, use_global_device_ids=true | all-gather | bytes 212992 | tf_op jit(solution)/shard_map/all_gather | solution.py:344
  97.0 0.0 copy-done.4
  97.0 1.0 shard_map.126
  98.0 0.0 all-to-all-done.1
  98.0 3.6 %shard_map.127 = f32[1856,128]{1,0:T(8,128)} custom-call(f32[2176,128]{1,0:T(8,128)S(1)} %bitcast.18, f32[1600,128]{1,0:T(8,128)S(1)} %bitcast.21, bf16[256,256]{1,0:T(8,128)(2,1)S(1)} %copy-done.3), custom_call_target="tpu_custom_call" | custom-call | tf_op jit(solution)/shard_map/pallas_call | solution.py:348
  (9 shorter events, 0.0 us)
Async XLA Ops:
  2.5 10.9 %collective-permute-start = (f32[1,32,128]{2,1,0:T(8,128)}, f32[1,32,128]{2,1,0:T(8,128)S(1)}, u32[]{:S(2)}, u32[]{:S(2)}) collective-permute-start(f32[1,32,128]{2,1,0:T(8,128)} %get-tuple-element.27), channel_id=1, source_target_pairs={{0,12},{12,24},{24,36},{36,48},{48,60},{60,72},{72,84},{84,96},{96... | collective-permute-start | bytes 49160 | tf_op jit(solution)/shard_map/ppermute | solution.py:327
  4.5 9.0 %collective-permute-start.1 = (f32[1,32,128]{2,1,0:T(8,128)}, f32[1,32,128]{2,1,0:T(8,128)S(1)}, u32[]{:S(2)}, u32[]{:S(2)}) collective-permute-start(f32[1,32,128]{2,1,0:T(8,128)} %get-tuple-element.28), channel_id=1, source_target_pairs={{12,0},{24,12},{36,24},{48,36},{60,48},{72,60},{84,72},{96,84},{10... | collective-permute-start | bytes 49160 | tf_op jit(solution)/shard_map/ppermute | solution.py:328
  8.1 1.2 %copy-start = (f32[32,58,128]{2,0,1:T(8,128)S(1)}, f32[32,58,128]{2,0,1:T(8,128)}, u32[]{:S(2)}) copy-start(f32[32,58,128]{2,0,1:T(8,128)} %param.13) | copy-start | bytes 2850820
  9.3 0.7 copy-start.9
  10.0 0.7 copy-start.10
  10.6 0.7 copy-start.11
  13.4 17.1 %copy-start.6 = (f32[4,32,128]{2,1,0:T(8,128)S(1)}, f32[4,32,128]{2,1,0:T(8,128)}, u32[]{:S(2)}) copy-start(f32[4,32,128]{2,1,0:T(8,128)} %get-tuple-element.24.own) | copy-start | bytes 196612
  13.4 47.5 %all-to-all-start = ((f32[64,34,1,128]{3,2,1,0:T(1,128)}), f32[64,34,1,128]{3,2,1,0:T(1,128)S(1)}, u32[]{:S(2)}, u32[]{:S(2)}) async-start(f32[64,34,1,128]{3,2,1,0:T(1,128)} %bitcast.11), calls=%async_computation | async-start | bytes 2228224 | tf_op jit(solution)/shard_map/all_to_all | solution.py:330
  58.9 12.5 %copy-start.1 = (f32[32,58,128]{2,0,1:T(8,128)S(1)}, f32[32,58,128]{2,0,1:T(8,128)}, u32[]{:S(2)}) copy-start(f32[32,58,128]{2,0,1:T(8,128)} %param.13) | copy-start | bytes 2850820
  58.9 12.5 %copy-start.3 = (bf16[256,256]{1,0:T(8,128)(2,1)S(1)}, bf16[256,256]{1,0:T(8,128)(2,1)}, u32[]{:S(2)}) copy-start(bf16[256,256]{1,0:T(8,128)(2,1)} %constant.7.clone.table) | copy-start | bytes 393220
  58.9 12.5 %copy-start.5 = (bf16[256,128]{1,0:T(8,128)(2,1)S(1)}, bf16[256,128]{1,0:T(8,128)(2,1)}, u32[]{:S(2)}) copy-start(bf16[256,128]{1,0:T(8,128)(2,1)} %constant.8.clone.means) | copy-start | bytes 196612
  59.5 0.9 copy-start.2
  60.4 0.6 copy-start.7
  61.0 36.1 %copy-start.4 = (f32[2,58,4,32]{1,3,2,0:T(8,128)S(1)}, f32[2,58,4,32]{1,3,2,0:T(8,128)}, u32[]{:S(2)}) copy-start(f32[2,58,4,32]{1,3,2,0:T(8,128)} %param.10) | copy-start | bytes 178180
  61.0 37.1 %all-to-all-start.1 = ((f32[64,25,1,128]{3,2,1,0:T(1,128)}), f32[64,25,1,128]{3,2,1,0:T(1,128)S(1)}, u32[]{:S(2)}, u32[]{:S(2)}) async-start(f32[64,25,1,128]{3,2,1,0:T(1,128)} %bitcast.24), calls=%async_computation.1 | async-start | bytes 1638400 | tf_op jit(solution)/shard_map/all_to_all | solution.py:341
  71.4 0.7 copy-start.8

commit v9 on v8

--- a/solution.py
+++ b/solution.py
@@ -69,7 +69,7 @@
     index[...] = columns
     for s in range(SLOTS):
         group = lax.div(migrate[s], COLS)
-        early[pl.ds(group * EARLY, EARLY), :] = state[pl.ds(s, EARLY, stride=SLOTS), :]
+        early[pl.ds(pl.multiple_of(group * EARLY, 8), EARLY), :] = state[pl.ds(s, EARLY, stride=SLOTS), :]
         late[pl.ds(group * SENT, LATE), :] = state[pl.ds(EARLY * SLOTS + s, LATE, stride=SLOTS), :]
 
 
@@ -172,7 +172,7 @@
     return jnp.concatenate([lead, trail], axis=1)
 
 
-EARLY = 34
+EARLY = 32
 LATE = LEV - EARLY
 SENT = LATE + 1
 CHUNKS = [(0, 8), (8, 8), (16, 8), (24, 8), (32, 8), (40, 8), (48, 8), (56, 2)]
@@ -249,7 +249,7 @@
     copy.wait()
     for j in range(SLOTS):
         g = origin[0, j]
-        held[pl.ds(j, EARLY, stride=SLOTS), :] = early[pl.ds(g * EARLY, EARLY), :]
+        held[pl.ds(j, EARLY, stride=SLOTS), :] = early[pl.ds(pl.multiple_of(g * EARLY, 8), EARLY), :]
         held[pl.ds(EARLY * SLOTS + j, LATE, stride=SLOTS), :] = late[pl.ds(g * SENT, LATE), :]
 
     copies = []

time: 102 us -> 99.3 us (0.974)
  the two profiles are of different devices: /device:TPU:2 before, /device:TPU:1 now
where the time goes in v9:
time: 99.3 us; the launch traced here: 98.8 us
  blocking collectives  42.7 us (43%)
  starting transfers between devices  35.9 us (36%)
  Pallas kernels  11.3 us (11%)
  waiting for transfers between devices  5.34 us (5%)
  local copies, waits for them, and re-layouts  2.8 us (3%)
    all_gather x1, blocking collectives, on_device(): gathered = lax.all_gather(payload, 'mem', axis=0)  24 us
    all_gather x1, blocking collectives, on_device(): tendencies = lax.all_gather(tendency, 'mem', axis=0, tiled=True)  18.7 us
    all_to_all x1, starting transfers between devices, on_device(): lax.all_to_all(filled.reshape(N_GRP, SENT, 1, lanes), 'grp', 0, 0, tiled=...  11.9 us
    ppermute x1, starting transfers between devices, on_device(): after = lax.ppermute(top, 'grp', down)  9.84 us
    all_to_all x1, starting transfers between devices, on_device(): lax.all_to_all(early.reshape(N_GRP, EARLY, 1, lanes), 'grp', 0, 0, tiled=...  9.71 us
    ppermute x1, starting transfers between devices, on_device(): before = lax.ppermute(end, 'grp', up)  4.51 us
    pallas_call x1, Pallas kernels, on_device(): call(arrive_kernel, (cells, lanes), [VMEM] * 3, [(cells, lanes)] * 3 + [(...  3.65 us
    all_to_all x1, waiting for transfers between devices, on_device(): lax.all_to_all(filled.reshape(N_GRP, SENT, 1, lanes), 'grp', 0, 0, tiled=...  3.04 us
  transfers between devices with their start and end apart: 4, of which 2 were waited for; matrix products, arithmetic and copies ran while one was open for 0% of the time, Pallas kernels for 6%

profile of v9, /device:TPU:1, one launch (start us, length us, event | category | flops | bytes accessed | tf_op | source)
XLA Modules:
  0.0 98.8 jit_solution(503929352534004057)
XLA Ops:
  0.6 1.9 %shard_map.121 = (f32[4,32,128]{2,1,0:T(8,128)}, f32[1,32,128]{2,1,0:T(8,128)}, f32[1,32,128]{2,1,0:T(8,128)}) custom-call(f32[2,4,32,58]{3,2,1,0:T(8,128)} %bitcast.27, f32[4,32,58]{2,1,0:T(8,128)} %bitcast.34, f32[4,32]{1,0:T(4,128)} %mass_at.1, f32[128,128]{1,0:T(8,128)} %constant.6.clone.table_at, s32[1,32]{1,0:T(1,128)} %bitcast.29), custom_call_target="tpu_custom_call" | custom-call | tf_op jit(solution)/shard_map/pallas_call | solution.py:314
  2.5 4.5 %collective-permute-start = (f32[1,32,128]{2,1,0:T(8,128)}, f32[1,32,128]{2,1,0:T(8,128)S(1)}, u32[]{:S(2)}, u32[]{:S(2)}) collective-permute-start(f32[1,32,128]{2,1,0:T(8,128)} %get-tuple-element.27), channel_id=1, source_target_pairs={{0,12},{12,24},{24,36},{36,48},{48,60},{60,72},{72,84},{84,96},{96... | collective-permute-start | bytes 49160 | tf_op jit(solution)/shard_map/ppermute | solution.py:327
  7.1 9.8 %collective-permute-start.1 = (f32[1,32,128]{2,1,0:T(8,128)}, f32[1,32,128]{2,1,0:T(8,128)S(1)}, u32[]{:S(2)}, u32[]{:S(2)}) collective-permute-start(f32[1,32,128]{2,1,0:T(8,128)} %get-tuple-element.28), channel_id=1, source_target_pairs={{12,0},{24,12},{36,24},{48,36},{60,48},{72,60},{84,72},{96,84},{10... | collective-permute-start | bytes 49160 | tf_op jit(solution)/shard_map/ppermute | solution.py:328
  16.9 0.0 copy-start.7
  16.9 0.0 copy-start.8
  16.9 0.0 copy-start.9
  16.9 0.6 copy-done.7
  17.6 0.0 copy-done.8
  17.6 0.0 copy-done.9
  17.6 0.0 copy-start
  17.6 1.2 %copy-done = f32[32,58,128]{2,0,1:T(8,128)S(1)} copy-done((f32[32,58,128]{2,0,1:T(8,128)S(1)}, f32[32,58,128]{2,0,1:T(8,128)}, u32[]{:S(2)}) %copy-start) | copy-done | bytes 950296
  18.8 2.1 %shard_map.122 = (f32[2048,128]{1,0:T(8,128)}, f32[1728,128]{1,0:T(8,128)S(1)}, f32[32,128]{1,0:T(8,128)S(1)}) custom-call(s32[32]{0:T(128)S(1)} %copy-done.8, f32[1856,128]{1,0:T(8,128)S(1)} %bitcast.21, s32[1,32]{1,0:T(1,128)S(1)} %bitcast.30, s32[1,32]{1,0:T(1,128)S(1)} %bitcast.31, s32[1,32]{1,0:T(1,128)S(1)} %bitcast.32), custom_call_target="tpu_custom_call" | custom-call | tf_op jit(solution)/shard_map/pallas_call | solution.py:322
  20.9 0.0 collective-permute-done.before
  20.9 0.0 collective-permute-done.1.after
  20.9 9.7 %all-to-all-start = ((f32[64,32,1,128]{3,1,2,0:T(8,128)}), f32[64,32,1,128]{3,1,2,0:T(8,128)S(1)}, u32[]{:S(2)}, u32[]{:S(2)}) async-start(f32[64,32,1,128]{3,1,2,0:T(8,128)} %bitcast.12), calls=%async_computation | async-start | bytes 2097152 | tf_op jit(solution)/shard_map/all_to_all | solution.py:330
  30.6 0.0 copy-done.6
  30.6 0.2 shard_map.123
  30.9 24.0 %all-gather = f32[480,128]{1,0:T(8,128)S(1)} all-gather(f32[40,128]{1,0:T(8,128)S(1)} %get-tuple-element.31), channel_id=2, replica_groups=mesh['grp'=64,'mem'=12] {'mem'}, dimensions={0}, use_global_device_ids=true | all-gather | bytes 266240 | tf_op jit(solution)/shard_map/all_gather | solution.py:334
  54.8 0.5 shard_map.124
  55.4 0.9 copy-done.2
  56.3 2.3 %all-to-all-done = f32[64,32,1,128]{3,1,2,0:T(8,128)S(1)} async-done(((f32[64,32,1,128]{3,1,2,0:T(8,128)}), f32[64,32,1,128]{3,1,2,0:T(8,128)S(1)}, u32[]{:S(2)}, u32[]{:S(2)}) %all-to-all-start) | async-done | bytes 1048608 | tf_op jit(solution)/shard_map/all_to_all | solution.py:330
  58.6 11.9 %all-to-all-start.1 = ((f32[64,27,1,128]{3,2,1,0:T(1,128)}), f32[64,27,1,128]{3,2,1,0:T(1,128)S(1)}, u32[]{:S(2)}, u32[]{:S(2)}) async-start(f32[64,27,1,128]{3,2,1,0:T(1,128)} %bitcast.26), calls=%async_computation.1 | async-start | bytes 1769472 | tf_op jit(solution)/shard_map/all_to_all | solution.py:341
  70.5 0.0 copy-done.1
  70.5 0.0 copy-done.3
  70.5 0.0 copy-done.5
  70.5 1.9 %shard_map.125 = f32[32,128]{1,0:T(8,128)S(1)} custom-call(f32[1856,128]{1,0:T(8,128)S(1)} %bitcast.22, f32[32,128]{1,0:T(8,128)S(1)} %get-tuple-element.34.force, bf16[256,256]{1,0:T(8,128)(2,1)S(1)} %copy-done.3, bf16[256,128]{1,0:T(8,128)(2,1)S(1)} %copy-done.5), custom_call_target="tpu_custom_call" | custom-call | tf_op jit(solution)/shard_map/pallas_call | solution.py:343
  72.4 0.0 copy-start.4
  72.4 18.7 %all_gather.11.tendency = f32[384,128]{1,0:T(8,128)S(1)} all-gather(f32[32,128]{1,0:T(8,128)S(1)} %shard_map.125), channel_id=1, replica_groups=mesh['grp'=64,'mem'=12] {'mem'}, dimensions={0}, use_global_device_ids=true | all-gather | bytes 212992 | tf_op jit(solution)/shard_map/all_gather | solution.py:344
  91.1 0.0 copy-done.4
  91.1 1.0 shard_map.126
  92.1 3.0 %all-to-all-done.1 = f32[64,27,1,128]{3,2,1,0:T(1,128)S(1)} async-done(((f32[64,27,1,128]{3,2,1,0:T(1,128)}), f32[64,27,1,128]{3,2,1,0:T(1,128)S(1)}, u32[]{:S(2)}, u32[]{:S(2)}) %all-to-all-start.1) | async-done | bytes 884768 | tf_op jit(solution)/shard_map/all_to_all | solution.py:341
  95.1 3.7 %shard_map.127 = f32[1856,128]{1,0:T(8,128)} custom-call(f32[2048,128]{1,0:T(8,128)S(1)} %bitcast.20, f32[1728,128]{1,0:T(8,128)S(1)} %bitcast.23, bf16[256,256]{1,0:T(8,128)(2,1)S(1)} %copy-done.3), custom_call_target="tpu_custom_call" | custom-call | tf_op jit(solution)/shard_map/pallas_call | solution.py:348
  (5 shorter events, 0.0 us)
Async XLA Ops:
  2.5 18.3 %collective-permute-start = (f32[1,32,128]{2,1,0:T(8,128)}, f32[1,32,128]{2,1,0:T(8,128)S(1)}, u32[]{:S(2)}, u32[]{:S(2)}) collective-permute-start(f32[1,32,128]{2,1,0:T(8,128)} %get-tuple-element.27), channel_id=1, source_target_pairs={{0,12},{12,24},{24,36},{36,48},{48,60},{60,72},{72,84},{84,96},{96... | collective-permute-start | bytes 49160 | tf_op jit(solution)/shard_map/ppermute | solution.py:327
  7.1 13.8 %collective-permute-start.1 = (f32[1,32,128]{2,1,0:T(8,128)}, f32[1,32,128]{2,1,0:T(8,128)S(1)}, u32[]{:S(2)}, u32[]{:S(2)}) collective-permute-start(f32[1,32,128]{2,1,0:T(8,128)} %get-tuple-element.28), channel_id=1, source_target_pairs={{12,0},{24,12},{36,24},{48,36},{60,48},{72,60},{84,72},{96,84},{10... | collective-permute-start | bytes 49160 | tf_op jit(solution)/shard_map/ppermute | solution.py:328
  16.9 0.7 copy-start.7
  16.9 0.7 copy-start.8
  16.9 0.7 copy-start.9
  17.6 1.2 %copy-start = (f32[32,58,128]{2,0,1:T(8,128)S(1)}, f32[32,58,128]{2,0,1:T(8,128)}, u32[]{:S(2)}) copy-start(f32[32,58,128]{2,0,1:T(8,128)} %param.13) | copy-start | bytes 2850820
  20.9 9.7 %copy-start.6 = (f32[4,32,128]{2,1,0:T(8,128)S(1)}, f32[4,32,128]{2,1,0:T(8,128)}, u32[]{:S(2)}) copy-start(f32[4,32,128]{2,1,0:T(8,128)} %get-tuple-element.24.own) | copy-start | bytes 196612
  20.9 37.7 %all-to-all-start = ((f32[64,32,1,128]{3,1,2,0:T(8,128)}), f32[64,32,1,128]{3,1,2,0:T(8,128)S(1)}, u32[]{:S(2)}, u32[]{:S(2)}) async-start(f32[64,32,1,128]{3,1,2,0:T(8,128)} %bitcast.12), calls=%async_computation | async-start | bytes 2097152 | tf_op jit(solution)/shard_map/all_to_all | solution.py:330
  55.4 0.9 copy-start.2
  56.3 14.2 %copy-start.1 = (f32[32,58,128]{2,0,1:T(8,128)S(1)}, f32[32,58,128]{2,0,1:T(8,128)}, u32[]{:S(2)}) copy-start(f32[32,58,128]{2,0,1:T(8,128)} %param.13) | copy-start | bytes 2850820
  58.6 11.9 %copy-start.3 = (bf16[256,256]{1,0:T(8,128)(2,1)S(1)}, bf16[256,256]{1,0:T(8,128)(2,1)}, u32[]{:S(2)}) copy-start(bf16[256,256]{1,0:T(8,128)(2,1)} %constant.7.clone.table) | copy-start | bytes 393220
  58.6 11.9 %copy-start.5 = (bf16[256,128]{1,0:T(8,128)(2,1)S(1)}, bf16[256,128]{1,0:T(8,128)(2,1)}, u32[]{:S(2)}) copy-start(bf16[256,128]{1,0:T(8,128)(2,1)} %constant.8.clone.means) | copy-start | bytes 196612
  58.6 36.5 %all-to-all-start.1 = ((f32[64,27,1,128]{3,2,1,0:T(1,128)}), f32[64,27,1,128]{3,2,1,0:T(1,128)S(1)}, u32[]{:S(2)}, u32[]{:S(2)}) async-start(f32[64,27,1,128]{3,2,1,0:T(1,128)} %bitcast.26), calls=%async_computation.1 | async-start | bytes 1769472 | tf_op jit(solution)/shard_map/all_to_all | solution.py:341
  72.4 18.7 %copy-start.4 = (f32[2,58,4,32]{1,3,2,0:T(8,128)S(1)}, f32[2,58,4,32]{1,3,2,0:T(8,128)}, u32[]{:S(2)}) copy-start(f32[2,58,4,32]{1,3,2,0:T(8,128)} %param.10) | copy-start | bytes 178180
